TPU v7x, 128 devices: a whole 4x4x4 slice. The times are simulated.
128 devices in a mesh: dp: 16 (over y, x), dim: 8 (over z, core).
Axes of the slice: x: 4, y: 4, z: 4, core: 2. Of those that a mesh axis runs over, the one named last changes fastest.
Arguments:
- noise: bfloat16 [256, 324480], P(('dp', 'dim')), may hold values from -5 to 5
- data: bfloat16 [256, 324480], P(('dp', 'dim')), may hold values from -10 to 10
Outputs:
- targets: bfloat16 [256, 324480], P(('dp', 'dim'))
- row_potential: float32 [256], P(('dp', 'dim'))
- col_potential: float32 [256], P(('dp', 'dim'))
All inputs are finite; a program needn't handle non-finite values.
Results may differ from a plain program's by a relative error of at most 0.014.
Values may be sent and summed in bfloat16 or wider, within the bound.
No kernel may reach another device: no remote copies, remote signals or barrier semaphores. Data moves between devices by JAX's collectives and lax.ppermute only.
A program may use at most 128 MiB of HBM per device.

v0:
```python
import math

import jax
import jax.numpy as jnp
from jax import lax
from jax.sharding import PartitionSpec as P

SWEEPS = 20
LATENT = 324480


def lse_rows(values):
    top = jnp.max(values, axis=1, keepdims=True)
    return top[:, 0] + jnp.log(jnp.sum(jnp.exp(values - top), axis=1))


def products(noise_cols, piece):
    return lax.dot_general(
        noise_cols, piece, (((1,), (1,)), ((), ())), preferred_element_type=jnp.float32
    )


def squares(piece):
    return jnp.einsum("rf,rf->r", piece, piece, preferred_element_type=jnp.float32)


def whole_sweeps(full_cost, temper):

    def sweep_all(step, carry):
        row_pot, col_pot = carry
        row_pot = -temper * lse_rows((col_pot[None, :] - full_cost) / temper)
        scaled = (row_pot[:, None] - full_cost) / temper
        top = jnp.max(scaled, axis=0)
        col_pot = -temper * (top + jnp.log(jnp.sum(jnp.exp(scaled - top[None, :]), axis=0)))
        return (row_pot, col_pot)

    rows = full_cost.shape[0]
    begin = (jnp.zeros((rows,), jnp.float32), jnp.zeros((rows,), jnp.float32))
    return lax.fori_loop(0, SWEEPS, sweep_all, begin)


def on_device(noise, data):
    temper = 0.25 / math.sqrt(LATENT)
    my_dp = lax.axis_index("dp")
    my_dim = lax.axis_index("dim")
    pairs = noise.shape[0]
    noise_ent, data_ent = (
        lax.all_to_all(noise, ("dp", "dim"), split_axis=1, concat_axis=0, tiled=True),
        lax.all_to_all(data, ("dp", "dim"), split_axis=1, concat_axis=0, tiled=True),
    )
    gram = products(noise_ent, data_ent)
    noise_sq = squares(noise_ent)
    data_sq = squares(data_ent)
    gram, noise_sq, data_sq = lax.psum((gram, noise_sq, data_sq), ("dp", "dim"))
    full_cost = (noise_sq[:, None] + data_sq[None, :] - 2.0 * gram) / LATENT
    row_pot, col_pot = whole_sweeps(full_cost, temper)
    weights = jax.nn.softmax((col_pot[None, :] - full_cost) / temper, axis=1).astype(jnp.bfloat16)
    moved = jnp.dot(weights, data_ent, preferred_element_type=jnp.float32)
    targets = lax.all_to_all(
        moved.astype(jnp.bfloat16), ("dp", "dim"), split_axis=0, concat_axis=1, tiled=True
    )
    offset = (my_dp * lax.axis_size("dim") + my_dim) * pairs
    row_out = lax.dynamic_slice_in_dim(row_pot, offset, pairs, 0)
    col_out = lax.dynamic_slice_in_dim(col_pot, offset, pairs, 0)
    return (targets, row_out, col_out)


def solution(mesh):
    return jax.shard_map(
        on_device,
        mesh=mesh,
        in_specs=(P(("dp", "dim"), None), P(("dp", "dim"), None)),
        out_specs=(P(("dp", "dim"), None), P(("dp", "dim")), P(("dp", "dim"))),
        check_vma=False,
    )
```

profile of v0, /device:TPU:1, one launch (start us, length us, event | category | flops | bytes accessed | tf_op | source)
XLA Modules:
  0.0 280.0 jit_solution(16719100778355314292)
XLA Ops:
  7.2 3.5 %reshape.34 = bf16[648960]{0:T(1024)(128)(2,1)S(1)} reshape(bf16[2,324480]{1,0:T(2,128)(2,1)} %param.5) | data formatting | bytes 2595840
  10.7 1.7 all_to_all.46
  12.4 2.4 copy.11
  14.8 11.5 %all-to-all-start.1 = ((bf16[2,128,2535]{2,0,1:T(2,128)(2,1)}), bf16[2,128,2535]{2,0,1:T(2,128)(2,1)S(1)}, u32[]{:S(2)}, u32[]{:S(2)}) async-start(bf16[2,128,2535]{2,0,1:T(2,128)(2,1)} %copy.11), calls=%async_computation.1 | async-start | bytes 2621440 | tf_op jit(solution)/shard_map/all_to_all | solution.py:49
  26.4 3.3 %reshape.36 = bf16[648960]{0:T(1024)(128)(2,1)} reshape(bf16[2,324480]{1,0:T(2,128)(2,1)S(1)} %copy-done.1) | data formatting | bytes 2595840
  29.6 3.1 %all_to_all.42 = bf16[2,128,2535]{2,1,0:T(8,128)(2,1)S(1)} reshape(bf16[648960]{0:T(1024)(128)(2,1)} %reshape.36) | data formatting | bytes 2595840 | tf_op jit(solution)/shard_map/all_to_all | solution.py:48
  32.7 2.4 copy.10
  35.2 13.1 %all-to-all-done.1 = bf16[2,128,2535]{2,0,1:T(2,128)(2,1)S(1)} async-done(((bf16[2,128,2535]{2,0,1:T(2,128)(2,1)}), bf16[2,128,2535]{2,0,1:T(2,128)(2,1)S(1)}, u32[]{:S(2)}, u32[]{:S(2)}) %all-to-all-start.1) | async-done | bytes 1297952 | tf_op jit(solution)/shard_map/all_to_all | solution.py:49
  48.3 5.8 %all-to-all-start = ((bf16[2,128,2535]{2,0,1:T(2,128)(2,1)}), bf16[2,128,2535]{2,0,1:T(2,128)(2,1)}, u32[]{:S(2)}, u32[]{:S(2)}) async-start(bf16[2,128,2535]{2,0,1:T(2,128)(2,1)} %copy.10), calls=%async_computation | async-start | bytes 2621440 | tf_op jit(solution)/shard_map/all_to_all | solution.py:48
  54.2 1.0 all_to_all.49
  55.2 20.7 %all-to-all-done = bf16[2,128,2535]{2,0,1:T(2,128)(2,1)} async-done(((bf16[2,128,2535]{2,0,1:T(2,128)(2,1)}), bf16[2,128,2535]{2,0,1:T(2,128)(2,1)}, u32[]{:S(2)}, u32[]{:S(2)}) %all-to-all-start) | async-done | bytes 1297952 | tf_op jit(solution)/shard_map/all_to_all | solution.py:48
  75.9 3.2 %all_to_all.45 = bf16[256,2535]{1,0:T(8,128)(2,1)S(1)} reshape(bf16[128,2,2535]{2,1,0:T(2,128)(2,1)} %bitcast) | data formatting | bytes 2595840 | tf_op jit(solution)/shard_map/all_to_all | solution.py:48
  79.1 1.3 fusion.11
  80.3 0.6 fusion.2
  80.9 63.5 %all-reduce = (f32[256]{0:T(256)S(1)}, f32[256]{0:T(256)S(1)}) all-reduce(f32[256]{0:T(256)S(1)} %get-tuple-element.51, f32[256]{0:T(256)S(1)} %get-tuple-element.52), channel_id=1, replica_groups=mesh['dp'=16,'dim'=8] {'dp','dim'}, use_global_device_ids=true, to_apply=%region_1.0 | all-reduce | flops 512 | bytes 4096 | tf_op jit(solution)/shard_map/psum | solution.py:54
  144.4 73.7 %all-reduce.3.cloned.1.call-done = f32[256,256]{1,0:T(8,128)} async-done(((f32[256,256]{1,0:T(8,128)}), f32[256,256]{1,0:T(8,128)}) %all-reduce.3.cloned.1.call-update) | async-done | bytes 262160 | tf_op jit(solution)/shard_map/psum | solution.py:54
  218.2 1.0 subtract_multiply_fusion.3
  219.2 18.3 %while.13 = (s32[]{:T(128)}, f32[256]{0:T(256)}, f32[256]{0:T(256)S(1)}, f32[256,256]{1,0:T(8,128)S(1)}, s32[]{:T(128)}, /*index=5*/s32[]{:T(128)}) while((s32[]{:T(128)}, f32[256]{0:T(256)}, f32[256]{0:T(256)S(1)}, f32[256,256]{1,0:T(8,128)S(1)}, s32[]{:T(128)}, /*index=5*/s32[]{:T(128)}) %tuple.27), condition=%wide.region_8.0_spmd.clone, body=%wide.region_3.0_spmd.clone.sunk | while | flops 917763 | bytes 1071211 | solution.py:39
  219.4 0.2 exponential_reduce_fusion.4
  219.9 0.3 copy-done.2
  220.3 0.2 exponential_reduce_fusion.4
  220.8 0.3 copy-done.2
  221.2 0.2 exponential_reduce_fusion.4
  221.7 0.3 copy-done.2
  222.1 0.2 exponential_reduce_fusion.4
  222.6 0.3 copy-done.2
  223.0 0.2 exponential_reduce_fusion.4
  223.5 0.3 copy-done.2
  223.9 0.2 exponential_reduce_fusion.4
  224.4 0.3 copy-done.2
  225.4 0.3 copy-done.2
  225.8 0.2 exponential_reduce_fusion.4
  226.3 0.3 copy-done.2
  226.7 0.2 exponential_reduce_fusion.4
  227.2 0.3 copy-done.2
  227.6 0.2 exponential_reduce_fusion.4
  228.1 0.3 copy-done.2
  228.5 0.2 exponential_reduce_fusion.4
  229.0 0.3 copy-done.2
  229.4 0.2 exponential_reduce_fusion.4
  229.9 0.3 copy-done.2
  230.3 0.2 exponential_reduce_fusion.4
  230.8 0.3 copy-done.2
  231.2 0.2 exponential_reduce_fusion.4
  231.8 0.3 copy-done.2
  232.2 0.2 exponential_reduce_fusion.4
  232.7 0.3 copy-done.2
  233.1 0.2 exponential_reduce_fusion.4
  233.6 0.3 copy-done.2
  234.5 0.3 copy-done.2
  235.4 0.3 copy-done.2
  236.3 0.3 copy-done.2
  237.2 0.3 copy-done.2
  237.5 0.2 fusion.4
  237.7 0.2 fusion.5
  238.0 0.7 convolution_convert_fusion
  238.7 0.8 copy.12
  239.5 1.4 all_to_all.50
  240.9 5.7 %all-to-all-start.2 = ((bf16[128,2,2535]{2,1,0:T(2,128)(2,1)}), bf16[128,2,2535]{2,1,0:T(2,128)(2,1)S(1)}, u32[]{:S(2)}, u32[]{:S(2)}) async-start(bf16[128,2,2535]{2,1,0:T(2,128)(2,1)} %all_to_all.50), calls=%async_computation.2 | async-start | bytes 2621440 | tf_op jit(solution)/shard_map/all_to_all | solution.py:59
  246.6 0.6 dynamic_slice.7
  247.2 0.6 dynamic_slice.6
  247.8 20.7 %all-to-all-done.2 = bf16[128,2,2535]{2,1,0:T(2,128)(2,1)S(1)} async-done(((bf16[128,2,2535]{2,1,0:T(2,128)(2,1)}), bf16[128,2,2535]{2,1,0:T(2,128)(2,1)S(1)}, u32[]{:S(2)}, u32[]{:S(2)}) %all-to-all-start.2) | async-done | bytes 1297952 | tf_op jit(solution)/shard_map/all_to_all | solution.py:59
  268.7 1.6 reshape.38
  270.3 2.8 %all_to_all.53 = bf16[2,324480]{1,0:T(2,128)(2,1)} reshape(bf16[648960]{0:T(1024)(128)(2,1)S(1)} %reshape.38) | data formatting | bytes 2595840 | tf_op jit(solution)/shard_map/all_to_all | solution.py:59
  (156 shorter events, 9.1 us)
Async XLA Ops:
  14.8 11.5 %copy-start.1 = (bf16[2,324480]{1,0:T(2,128)(2,1)S(1)}, bf16[2,324480]{1,0:T(2,128)(2,1)}, u32[]{:S(2)}) copy-start(bf16[2,324480]{1,0:T(2,128)(2,1)} %param.4) | copy-start | bytes 3893764
  14.8 33.4 %all-to-all-start.1 = ((bf16[2,128,2535]{2,0,1:T(2,128)(2,1)}), bf16[2,128,2535]{2,0,1:T(2,128)(2,1)S(1)}, u32[]{:S(2)}, u32[]{:S(2)}) async-start(bf16[2,128,2535]{2,0,1:T(2,128)(2,1)} %copy.11), calls=%async_computation.1 | async-start | bytes 2621440 | tf_op jit(solution)/shard_map/all_to_all | solution.py:49
  48.3 27.6 %all-to-all-start = ((bf16[2,128,2535]{2,0,1:T(2,128)(2,1)}), bf16[2,128,2535]{2,0,1:T(2,128)(2,1)}, u32[]{:S(2)}, u32[]{:S(2)}) async-start(bf16[2,128,2535]{2,0,1:T(2,128)(2,1)} %copy.10), calls=%async_computation | async-start | bytes 2621440 | tf_op jit(solution)/shard_map/all_to_all | solution.py:48
  54.1 164.1 %all-reduce.3.cloned.1.call-start = ((), (), s32[]{:S(2)}) async-start(), calls=%async_computation.3 | async-start | bytes 524288 | tf_op jit(solution)/shard_map/psum | solution.py:54
  219.2 18.3 %copy-start = (f32[256,256]{1,0:T(8,128)S(1)}, f32[256,256]{1,0:T(8,128)}, u32[]{:S(2)}) copy-start(f32[256,256]{1,0:T(8,128)} %all-reduce.3.cloned.1.call-done) | copy-start | bytes 786436
  219.6 0.6 copy-start.2
  220.5 0.6 copy-start.2
  221.4 0.6 copy-start.2
  222.3 0.6 copy-start.2
  223.2 0.6 copy-start.2
  224.2 0.6 copy-start.2
  225.1 0.6 copy-start.2
  226.0 0.6 copy-start.2
  226.9 0.6 copy-start.2
  227.8 0.6 copy-start.2
  228.7 0.6 copy-start.2
  229.6 0.6 copy-start.2
  230.5 0.6 copy-start.2
  231.5 0.6 copy-start.2
  232.4 0.6 copy-start.2
  233.3 0.6 copy-start.2
  234.2 0.6 copy-start.2
  235.1 0.6 copy-start.2
  236.0 0.6 copy-start.2
  236.9 0.6 copy-start.2
  240.9 6.3 %copy-start.3 = (f32[256]{0:T(256)S(1)}, f32[256]{0:T(256)}, u32[]{:S(2)}) copy-start(f32[256]{0:T(256)} %get-tuple-element.26) | copy-start | bytes 3076
  240.9 27.6 %all-to-all-start.2 = ((bf16[128,2,2535]{2,1,0:T(2,128)(2,1)}), bf16[128,2,2535]{2,1,0:T(2,128)(2,1)S(1)}, u32[]{:S(2)}, u32[]{:S(2)}) async-start(bf16[128,2,2535]{2,1,0:T(2,128)(2,1)} %all_to_all.50), calls=%async_computation.2 | async-start | bytes 2621440 | tf_op jit(solution)/shard_map/all_to_all | solution.py:59
Sparse Core Ops, SparseCore 0:
  80.4 137.6 all-reduce.2
where the time goes:
time: 281 us; the launch traced here: 280 us
  waiting for transfers between devices  128 us (46%)
  blocking collectives  63.5 us (23%)
  local copies, waits for them, and re-layouts  34.4 us (12%)
  starting transfers between devices  23.1 us (8%)
  between operations  14.2 us (5%)
  other arithmetic  13.8 us (5%)
    psum x1, waiting for transfers between devices, on_device(): gram, noise_sq, data_sq = lax.psum((gram, noise_sq, data_sq), ('dp', 'dim'))  73.7 us
    psum x1, blocking collectives, on_device(): gram, noise_sq, data_sq = lax.psum((gram, noise_sq, data_sq), ('dp', 'dim'))  63.5 us
    all_to_all x1, waiting for transfers between devices, on_device(): lax.all_to_all(moved.astype(jnp.bfloat16), ('dp', 'dim'), split_axis=0, c...  20.7 us
    all_to_all x1, waiting for transfers between devices, on_device(): lax.all_to_all(noise, ('dp', 'dim'), split_axis=1, concat_axis=0, tiled=T...  20.7 us
    all_to_all x1, waiting for transfers between devices, on_device(): lax.all_to_all(data, ('dp', 'dim'), split_axis=1, concat_axis=0, tiled=True)  13.1 us
    all_to_all x1, starting transfers between devices, on_device(): lax.all_to_all(data, ('dp', 'dim'), split_axis=1, concat_axis=0, tiled=True)  11.5 us
    all_to_all x3, local copies, waits for them, and re-layouts, on_device(): lax.all_to_all(noise, ('dp', 'dim'), split_axis=1, concat_axis=0, tiled=T...  8.69 us
    unnamed x9, local copies, waits for them, and re-layouts  8.45 us
  transfers between devices with their start and end apart: 4, of which 4 were waited for; matrix products, arithmetic and copies ran while one was open for 3% of the time, Pallas kernels for 0%

commit v1 on v0

v1 whole, which is shorter than its diff:
```python
import math

import jax
import jax.numpy as jnp
from jax import lax
from jax.experimental import pallas as pl
from jax.experimental.pallas import tpu as pltpu
from jax.sharding import PartitionSpec as P

SWEEPS = 20
LATENT = 324480
BATCH = 256
AXES = ("dp", "dim")
LANES = 128
TEMPER = 0.25 / math.sqrt(LATENT)
UNIT = TEMPER * math.log(2.0)
DRIFT = 2.0**40
VMEM = 48 * 1024 * 1024


def pieces_of(value, pieces_ref):
    for piece in range(BATCH * 2 // 4):
        row, half = 4 * (piece // 2), LANES * (piece % 2)
        pieces_ref[piece] = value[row : row + 4, half : half + LANES]


def whole_of(pieces_ref):
    rows = []
    for row in range(BATCH // 4):
        rows.append(jnp.concatenate([pieces_ref[2 * row], pieces_ref[2 * row + 1]], axis=1))
    return jnp.concatenate(rows, axis=0)


def gram_kernel(noise_ref, data_ref, out_ref):
    data = data_ref[...]
    gram = lax.dot_general(
        data, noise_ref[...], (((1,), (1,)), ((), ())), preferred_element_type=jnp.float32
    )
    wide = data.astype(jnp.float32)
    data_sq = jnp.sum(wide * wide, axis=1, keepdims=True)
    pieces_of(data_sq - 2.0 * gram, out_ref)


def sum_kernel(parts_ref, out_ref):
    total = jnp.sum(parts_ref[...], axis=0)
    out_ref[...] = jnp.broadcast_to(total[None], out_ref.shape)


def sweep_kernel(cost_ref, data_ref, out_ref, pots_ref, bias, kern, row_base, col_base, row_fac, col_fac):
    bias[...] = whole_of(cost_ref) * (-1.0 / (LATENT * UNIT))

    def log_sweep():
        col = col_base[...] + jnp.log2(col_fac[...])
        scaled = bias[...] + col
        top = jnp.max(scaled, axis=0, keepdims=True)
        row = -(top + jnp.log2(jnp.sum(jnp.exp2(scaled - top), axis=0, keepdims=True)))
        scaled = bias[...] + row
        top = jnp.max(scaled, axis=1, keepdims=True)
        col = -(top + jnp.log2(jnp.sum(jnp.exp2(scaled - top), axis=1, keepdims=True)))
        row_base[...] = row
        col_base[...] = col
        row_fac[...] = jnp.ones_like(row)
        col_fac[...] = jnp.ones_like(col)
        kern[...] = jnp.exp2(scaled + col)

    col_base[...] = jnp.zeros_like(col_base)
    col_fac[...] = jnp.ones_like(col_fac)
    log_sweep()

    def sweep(step, carry):
        row = 1.0 / jnp.sum(kern[...] * col_fac[...], axis=0, keepdims=True)
        col = 1.0 / jnp.sum(kern[...] * row, axis=1, keepdims=True)
        near = (
            (jnp.max(row) <= DRIFT)
            & (jnp.min(row) >= 1.0 / DRIFT)
            & (jnp.max(col) <= DRIFT)
            & (jnp.min(col) >= 1.0 / DRIFT)
        )

        @pl.when(near)
        def _():
            row_fac[...] = row
            col_fac[...] = col

        @pl.when(jnp.logical_not(near))
        def _():
            log_sweep()

        return carry

    lax.fori_loop(1, SWEEPS, sweep, 0)
    near = jnp.min(jnp.sum(kern[...] * col_fac[...], axis=0)) >= 1.0 / DRIFT

    @pl.when(near)
    def _():
        kern[...] = kern[...] * col_fac[...]

    @pl.when(jnp.logical_not(near))
    def _():
        scaled = bias[...] + (col_base[...] + jnp.log2(col_fac[...]))
        kern[...] = jnp.exp2(scaled - jnp.max(scaled, axis=0, keepdims=True))

    scaled = kern[...]
    weights = (scaled / jnp.sum(scaled, axis=0, keepdims=True)).astype(jnp.bfloat16)
    out_ref[...] = lax.dot_general(
        weights, data_ref[...], (((0,), (0,)), ((), ())), preferred_element_type=jnp.float32
    ).astype(jnp.bfloat16)
    pots_ref[0:1, :] = (row_base[...] + jnp.log2(row_fac[...])) * UNIT
    pots_ref[1:2, :] = jnp.transpose((col_base[...] + jnp.log2(col_fac[...])) * UNIT)


def on_device(noise, data):
    devices = lax.axis_size(AXES)
    own = noise.shape[0]
    ent = -(-LATENT // (LANES * devices)) * LANES
    params = pltpu.CompilerParams(vmem_limit_bytes=VMEM)

    both = jnp.concatenate([noise, data], axis=0)
    both = jnp.pad(both, ((0, 0), (0, ent * devices - LATENT))).reshape(2 * own, devices, ent)
    both = lax.all_to_all(both, AXES, split_axis=1, concat_axis=1)
    noise_ent = both[:own].transpose(1, 0, 2).reshape(BATCH, ent)
    data_ent = both[own:].transpose(1, 0, 2).reshape(BATCH, ent)

    pieces = jax.ShapeDtypeStruct((devices, 4, LANES), jnp.float32)
    parts = pl.pallas_call(gram_kernel, out_shape=pieces, compiler_params=params)(noise_ent, data_ent)
    parts = lax.all_to_all(parts, AXES, split_axis=0, concat_axis=0)
    total = pl.pallas_call(sum_kernel, out_shape=pieces, compiler_params=params)(parts)
    total = lax.all_to_all(total, AXES, split_axis=0, concat_axis=0)

    moved, pots = pl.pallas_call(
        sweep_kernel,
        out_shape=(
            jax.ShapeDtypeStruct((BATCH, ent), jnp.bfloat16),
            jax.ShapeDtypeStruct((2, BATCH), jnp.float32),
        ),
        scratch_shapes=[
            pltpu.VMEM((BATCH, BATCH), jnp.float32),
            pltpu.VMEM((BATCH, BATCH), jnp.float32),
            pltpu.VMEM((1, BATCH), jnp.float32),
            pltpu.VMEM((BATCH, 1), jnp.float32),
            pltpu.VMEM((1, BATCH), jnp.float32),
            pltpu.VMEM((BATCH, 1), jnp.float32),
        ],
        compiler_params=params,
    )(total, data_ent)
    targets = lax.all_to_all(moved.reshape(devices, own, ent), AXES, split_axis=0, concat_axis=0)
    targets = targets.transpose(1, 0, 2).reshape(own, devices * ent)[:, :LATENT]

    offset = lax.axis_index(AXES) * own
    mine = lax.dynamic_slice_in_dim(pots, offset, own, 1)
    wide = noise.astype(jnp.float32)
    noise_sq = jnp.sum(wide * wide, axis=1)
    return (targets, mine[0] + noise_sq / LATENT, mine[1])


def solution(mesh):
    return jax.shard_map(
        on_device,
        mesh=mesh,
        in_specs=(P(AXES, None), P(AXES, None)),
        out_specs=(P(AXES, None), P(AXES), P(AXES)),
        check_vma=False,
    )
```

time: 281 us -> 128 us (0.46)
  waiting for transfers between devices: 128 us -> 18.1 us
  local copies, waits for them, and re-layouts: 34.4 us -> 10.7 us
  starting transfers between devices: 23.1 us -> 4.63 us
  blocking collectives: 63.5 us -> 77.4 us
  between operations: 14.2 us -> 0.7 us
  Pallas kernels: 0 us -> 7.66 us
  other arithmetic: 13.8 us -> 8.64 us
    all_to_all x0 -> x3, blocking collectives: none -> 77.4 us  [the longest x1 47 us: on_device(): both = lax.all_to_all(both, AXES, split_axis=1, concat_axis=1)]
    psum x1 -> x0, waiting for transfers between devices: 73.7 us -> none  [on_device(): gram, noise_sq, data_sq = lax.psum((gram, noise_sq, data_sq), ('dp', 'dim'))]
    psum x1 -> x0, blocking collectives: 63.5 us -> none  [on_device(): gram, noise_sq, data_sq = lax.psum((gram, noise_sq, data_sq), ('dp', 'dim'))]
    all_to_all x3 -> x1, waiting for transfers between devices: 54.5 us -> 18.1 us  [on_device(): lax.all_to_all(moved.reshape(devices, own, ent), AXES, split_axis=0, conc...]
    all_to_all x3 -> x1, starting transfers between devices: 23 us -> 4.63 us  [on_device(): lax.all_to_all(moved.reshape(devices, own, ent), AXES, split_axis=0, conc...]
    all_to_all x9 -> x0, local copies, waits for them, and re-layouts: 18.2 us -> none  [the longest x3 8.69 us: on_device(): lax.all_to_all(noise, ('dp', 'dim'), split_axis=1, concat_axis=0, tiled=T...]
    unnamed x9 -> x2, local copies, waits for them, and re-layouts: 8.45 us -> 0.01 us
    pallas_call x0 -> x3, Pallas kernels: none -> 7.66 us  [the longest x1 6.94 us: on_device(): pl.pallas_call(sweep_kernel, out_shape=(jax.ShapeDtypeStruct((BATCH, ent)...]
  transfers between devices with their start and end apart: 4 -> 1, of which waited for: 4 -> 1; matrix products, arithmetic and copies ran while one was open for 3% -> 3% of each run, Pallas kernels for 0% -> 0%
where the time goes in v1:
time: 128 us
  blocking collectives  77.4 us (60%)
  waiting for transfers between devices  18.1 us (14%)
  local copies, waits for them, and re-layouts  10.7 us (8%)
  other arithmetic  8.64 us (7%)
  Pallas kernels  7.66 us (6%)
  starting transfers between devices  4.63 us (4%)
    all_to_all x1, blocking collectives, on_device(): both = lax.all_to_all(both, AXES, split_axis=1, concat_axis=1)  47 us
    all_to_all x1, waiting for transfers between devices, on_device(): lax.all_to_all(moved.reshape(devices, own, ent), AXES, split_axis=0, conc...  18.1 us
    all_to_all x1, blocking collectives, on_device(): total = lax.all_to_all(total, AXES, split_axis=0, concat_axis=0)  15.2 us
    all_to_all x1, blocking collectives, on_device(): parts = lax.all_to_all(parts, AXES, split_axis=0, concat_axis=0)  15.2 us
    pallas_call x1, Pallas kernels, on_device(): pl.pallas_call(sweep_kernel, out_shape=(jax.ShapeDtypeStruct((BATCH, ent)...  6.94 us
    concatenate x1, other arithmetic, on_device(): both = jnp.concatenate([noise, data], axis=0)  5.31 us
    all_to_all x1, starting transfers between devices, on_device(): lax.all_to_all(moved.reshape(devices, own, ent), AXES, split_axis=0, conc...  4.63 us
    reshape x1, local copies, waits for them, and re-layouts, on_device(): data_ent = both[own:].transpose(1, 0, 2).reshape(BATCH, ent)  3.19 us
  transfers between devices with their start and end apart: 1, of which 1 were waited for; matrix products, arithmetic and copies ran while one was open for 3% of the time, Pallas kernels for 0%

profile of v1, /device:TPU:1, one launch (start us, length us, event | category | flops | bytes accessed | tf_op | source)
XLA Modules:
  0.0 127.8 jit_solution(7309695553668405071)
XLA Ops:
  0.6 5.3 %fusion.2 = bf16[4,327680]{1,0:T(4,128)(2,1)S(1)} fusion(bf16[2,324480]{1,0:T(2,128)(2,1)} %param.3, bf16[2,324480]{1,0:T(2,128)(2,1)} %param.2), kind=kLoop, calls=%fused_computation.3 | loop fusion | flops 9175040 | bytes 5217280 | tf_op jit(solution)/shard_map/concatenate | solution.py:118
  5.9 47.0 %all_to_all.20 = bf16[4,128,2560]{2,0,1:T(4,128)(2,1)S(1)} all-to-all(bf16[4,128,2560]{2,0,1:T(4,128)(2,1)S(1)} %bitcast.12), channel_id=1, replica_groups=mesh['dp'=16,'dim'=8] {'dp','dim'}, dimensions={1} | all-to-all | bytes 5242880 | tf_op jit(solution)/shard_map/all_to_all | solution.py:120
  53.0 2.9 %slice_bitcast_fusion = (bf16[128,2,2560]{2,1,0:T(2,128)(2,1)}, bf16[128,2,2560]{2,1,0:T(2,128)(2,1)S(1)}) fusion(bf16[4,128,2560]{2,0,1:T(4,128)(2,1)S(1)} %all_to_all.20), kind=kLoop, calls=%fused_computation.5 | loop fusion | bytes 5242880 | tf_op jit(solution)/shard_map/transpose | solution.py:122
  55.9 0.5 reshape.22.noise_ref
  56.4 3.2 %reshape.23.data_ref = bf16[256,2560]{1,0:T(8,128)(2,1)S(1)} reshape(bf16[128,2,2560]{2,1,0:T(2,128)(2,1)} %get-tuple-element.7) | data formatting | bytes 2621440 | tf_op jit(solution)/shard_map/reshape | solution.py:122
  59.6 0.6 shard_map.49
  60.1 15.2 %all_to_all.21.parts_ref = f32[128,4,128]{2,1,0:T(4,128)S(1)} all-to-all(f32[128,4,128]{2,1,0:T(4,128)S(1)} %shard_map.49), channel_id=1, replica_groups=mesh['dp'=16,'dim'=8] {'dp','dim'}, dimensions={0} | all-to-all | bytes 524288 | tf_op jit(solution)/shard_map/all_to_all | solution.py:126
  75.3 0.2 shard_map.50
  75.5 15.2 %all_to_all.22.cost_ref = f32[128,4,128]{2,1,0:T(4,128)S(1)} all-to-all(f32[128,4,128]{2,1,0:T(4,128)S(1)} %shard_map.50), channel_id=1, replica_groups=mesh['dp'=16,'dim'=8] {'dp','dim'}, dimensions={0} | all-to-all | bytes 524288 | tf_op jit(solution)/shard_map/all_to_all | solution.py:128
  90.7 6.9 %shard_map.51 = (bf16[256,2560]{1,0:T(8,128)(2,1)S(1)}, f32[2,256]{1,0:T(2,128)S(1)}) custom-call(f32[128,4,128]{2,1,0:T(4,128)S(1)} %all_to_all.22.cost_ref, bf16[256,2560]{1,0:T(8,128)(2,1)S(1)} %reshape.23.data_ref), custom_call_target="tpu_custom_call" | custom-call | tf_op jit(solution)/shard_map/pallas_call | solution.py:130
  97.7 1.4 %reshape.24 = bf16[128,2,2560]{2,1,0:T(2,128)(2,1)} reshape(bf16[256,2560]{1,0:T(8,128)(2,1)S(1)} %get-tuple-element.5) | data formatting | bytes 2621440 | tf_op jit(solution)/shard_map/reshape | solution.py:146
  99.0 0.0 copy-start
  99.0 4.6 %all-to-all-start.3 = ((bf16[128,2,2560]{2,1,0:T(2,128)(2,1)}), bf16[128,2,2560]{2,1,0:T(2,128)(2,1)S(1)}, u32[]{:S(2)}, u32[]{:S(2)}) async-start(bf16[128,2,2560]{2,1,0:T(2,128)(2,1)} %reshape.24), calls=%async_computation.3 | async-start | bytes 2621440 | tf_op jit(solution)/shard_map/all_to_all | solution.py:146
  103.7 0.0 copy-done
  103.7 2.8 %multiply_reduce_fusion = f32[2]{0:T(128)S(1)} fusion(bf16[2,324480]{1,0:T(2,128)(2,1)S(1)} %copy-done), kind=kLoop, calls=%fused_computation.4 | loop fusion | flops 1946878 | bytes 1297928 | tf_op jit(solution)/shard_map/reduce_sum | solution.py:152
  106.5 0.1 constant_dynamic-slice_fusion
  106.6 0.5 slice_bitcast_fusion.2
  107.1 0.5 bitcast_add_fusion
  107.6 18.1 %all-to-all-done.3 = bf16[128,2,2560]{2,1,0:T(2,128)(2,1)S(1)} async-done(((bf16[128,2,2560]{2,1,0:T(2,128)(2,1)}), bf16[128,2,2560]{2,1,0:T(2,128)(2,1)S(1)}, u32[]{:S(2)}, u32[]{:S(2)}) %all-to-all-start.3) | async-done | bytes 1310752 | tf_op jit(solution)/shard_map/all_to_all | solution.py:146
  125.7 2.1 %slice.22 = bf16[2,324480]{1,0:T(2,128)(2,1)} slice(bf16[2,327680]{1,0:T(2,128)(2,1)S(1)} %bitcast.13), slice={[0:2], [0:324480]} | slice | bytes 2595840 | tf_op jit(solution)/shard_map/slice | solution.py:147
Async XLA Ops:
  99.0 4.6 %copy-start = (bf16[2,324480]{1,0:T(2,128)(2,1)S(1)}, bf16[2,324480]{1,0:T(2,128)(2,1)}, u32[]{:S(2)}) copy-start(bf16[2,324480]{1,0:T(2,128)(2,1)} %param.2) | copy-start | bytes 3893764
  99.0 26.7 %all-to-all-start.3 = ((bf16[128,2,2560]{2,1,0:T(2,128)(2,1)}), bf16[128,2,2560]{2,1,0:T(2,128)(2,1)S(1)}, u32[]{:S(2)}, u32[]{:S(2)}) async-start(bf16[128,2,2560]{2,1,0:T(2,128)(2,1)} %reshape.24), calls=%async_computation.3 | async-start | bytes 2621440 | tf_op jit(solution)/shard_map/all_to_all | solution.py:146

commit v2 on v1

--- a/solution.py
+++ b/solution.py
@@ -15,7 +15,45 @@
 TEMPER = 0.25 / math.sqrt(LATENT)
 UNIT = TEMPER * math.log(2.0)
 DRIFT = 2.0**40
-VMEM = 48 * 1024 * 1024
+VMEM = 16 * 1024 * 1024
+UNITS = 4
+UNIT_TILES = 5
+
+
+def pack_kernel(noise_ref, data_ref, out_ref, zeros, sems):
+    devices, units = out_ref.shape[0], noise_ref.shape[0]
+    zeros[...] = jnp.zeros_like(zeros)
+    copies = []
+    for kind, ref in enumerate((noise_ref, data_ref)):
+        for q in range(UNITS):
+            slot = kind * UNITS + q
+            start = q * devices
+            count = min(devices, units - start)
+            copies.append((ref.at[pl.ds(start, count)], out_ref.at[pl.ds(0, count), slot]))
+            if count < devices:
+                copies.append((zeros, out_ref.at[pl.ds(count, devices - count), slot]))
+    copies = [pltpu.make_async_copy(src, dst, sems.at[n]) for n, (src, dst) in enumerate(copies)]
+    for copy in copies:
+        copy.start()
+    for copy in copies:
+        copy.wait()
+
+
+def unpack_kernel(moved_ref, out_ref, sems):
+    devices, units = moved_ref.shape[0], out_ref.shape[0]
+    copies = []
+    for q in range(UNITS):
+        start = q * devices
+        count = min(devices, units - start)
+        copies.append(
+            pltpu.make_async_copy(
+                moved_ref.at[pl.ds(0, count), q], out_ref.at[pl.ds(start, count)], sems.at[q]
+            )
+        )
+    for copy in copies:
+        copy.start()
+    for copy in copies:
+        copy.wait()
 
 
 def pieces_of(value, pieces_ref):
@@ -31,10 +69,11 @@
     return jnp.concatenate(rows, axis=0)
 
 
-def gram_kernel(noise_ref, data_ref, out_ref):
-    data = data_ref[...]
+def gram_kernel(both_ref, out_ref):
+    ent = both_ref.shape[1] // 2
+    data = both_ref[:, ent:]
     gram = lax.dot_general(
-        data, noise_ref[...], (((1,), (1,)), ((), ())), preferred_element_type=jnp.float32
+        data, both_ref[:, :ent], (((1,), (1,)), ((), ())), preferred_element_type=jnp.float32
     )
     wide = data.astype(jnp.float32)
     data_sq = jnp.sum(wide * wide, axis=1, keepdims=True)
@@ -46,7 +85,7 @@
     out_ref[...] = jnp.broadcast_to(total[None], out_ref.shape)
 
 
-def sweep_kernel(cost_ref, data_ref, out_ref, pots_ref, bias, kern, row_base, col_base, row_fac, col_fac):
+def sweep_kernel(cost_ref, both_ref, out_ref, pots_ref, bias, kern, row_base, col_base, row_fac, col_fac):
     bias[...] = whole_of(cost_ref) * (-1.0 / (LATENT * UNIT))
 
     def log_sweep():
@@ -103,7 +142,7 @@
     scaled = kern[...]
     weights = (scaled / jnp.sum(scaled, axis=0, keepdims=True)).astype(jnp.bfloat16)
     out_ref[...] = lax.dot_general(
-        weights, data_ref[...], (((0,), (0,)), ((), ())), preferred_element_type=jnp.float32
+        weights, both_ref[:, both_ref.shape[1] // 2 :], (((0,), (0,)), ((), ())), preferred_element_type=jnp.float32
     ).astype(jnp.bfloat16)
     pots_ref[0:1, :] = (row_base[...] + jnp.log2(row_fac[...])) * UNIT
     pots_ref[1:2, :] = jnp.transpose((col_base[...] + jnp.log2(col_fac[...])) * UNIT)
@@ -112,17 +151,29 @@
 def on_device(noise, data):
     devices = lax.axis_size(AXES)
     own = noise.shape[0]
-    ent = -(-LATENT // (LANES * devices)) * LANES
+    ent = UNITS * UNIT_TILES * LANES
     params = pltpu.CompilerParams(vmem_limit_bytes=VMEM)
-
-    both = jnp.concatenate([noise, data], axis=0)
-    both = jnp.pad(both, ((0, 0), (0, ent * devices - LATENT))).reshape(2 * own, devices, ent)
-    both = lax.all_to_all(both, AXES, split_axis=1, concat_axis=1)
-    noise_ent = both[:own].transpose(1, 0, 2).reshape(BATCH, ent)
-    data_ent = both[own:].transpose(1, 0, 2).reshape(BATCH, ent)
+    anywhere = pl.BlockSpec(memory_space=pl.ANY)
+
+    def units_of(rows):
+        units = rows.shape[1] // (UNIT_TILES * LANES)
+        return rows.reshape(own, units, UNIT_TILES, LANES).transpose(1, 2, 0, 3)
+
+    both = pl.pallas_call(
+        pack_kernel,
+        out_shape=jax.ShapeDtypeStruct((devices, 2 * UNITS, UNIT_TILES, own, LANES), noise.dtype),
+        in_specs=[anywhere, anywhere],
+        out_specs=anywhere,
+        scratch_shapes=[
+            pltpu.VMEM((UNITS * devices - LATENT // (UNIT_TILES * LANES), UNIT_TILES, own, LANES), noise.dtype),
+            pltpu.SemaphoreType.DMA((4 * UNITS,)),
+        ],
+    )(units_of(noise), units_of(data))
+    both = both.reshape(devices, -1, own, LANES).transpose(0, 2, 1, 3).reshape(devices, own, 2 * ent)
+    both = lax.all_to_all(both, AXES, split_axis=0, concat_axis=0).reshape(BATCH, 2 * ent)
 
     pieces = jax.ShapeDtypeStruct((devices, 4, LANES), jnp.float32)
-    parts = pl.pallas_call(gram_kernel, out_shape=pieces, compiler_params=params)(noise_ent, data_ent)
+    parts = pl.pallas_call(gram_kernel, out_shape=pieces, compiler_params=params)(both)
     parts = lax.all_to_all(parts, AXES, split_axis=0, concat_axis=0)
     total = pl.pallas_call(sum_kernel, out_shape=pieces, compiler_params=params)(parts)
     total = lax.all_to_all(total, AXES, split_axis=0, concat_axis=0)
@@ -142,9 +193,17 @@
             pltpu.VMEM((BATCH, 1), jnp.float32),
         ],
         compiler_params=params,
-    )(total, data_ent)
-    targets = lax.all_to_all(moved.reshape(devices, own, ent), AXES, split_axis=0, concat_axis=0)
-    targets = targets.transpose(1, 0, 2).reshape(own, devices * ent)[:, :LATENT]
+    )(total, both)
+    moved = lax.all_to_all(moved.reshape(devices, own, ent), AXES, split_axis=0, concat_axis=0)
+    moved = moved.reshape(devices, own, UNITS, UNIT_TILES, LANES).transpose(0, 2, 3, 1, 4)
+    targets = pl.pallas_call(
+        unpack_kernel,
+        out_shape=jax.ShapeDtypeStruct((LATENT // (UNIT_TILES * LANES), UNIT_TILES, own, LANES), moved.dtype),
+        in_specs=[anywhere],
+        out_specs=anywhere,
+        scratch_shapes=[pltpu.SemaphoreType.DMA((UNITS,))],
+    )(moved)
+    targets = targets.transpose(2, 0, 1, 3).reshape(own, LATENT)
 
     offset = lax.axis_index(AXES) * own
     mine = lax.dynamic_slice_in_dim(pots, offset, own, 1)

time: 128 us -> 245 us (1.91)
  Pallas kernels: 7.66 us -> 128 us
  other arithmetic: 8.64 us -> 3.33 us
    pallas_call x1 -> x3, Pallas kernels: 0.56 us -> 121 us  [the longest x1 79.9 us: on_device(): pl.pallas_call(pack_kernel, out_shape=jax.ShapeDtypeStruct((devices, 2 *...]
    concatenate x1 -> x0, other arithmetic: 5.31 us -> none  [on_device(): both = jnp.concatenate([noise, data], axis=0)]
    transpose x1 -> x0, local copies, waits for them, and re-layouts: 2.88 us -> none  [on_device(): data_ent = both[own:].transpose(1, 0, 2).reshape(BATCH, ent)]
    reshape x1, local copies, waits for them, and re-layouts: 1.38 us -> 3.94 us  [on_device(): moved.reshape(devices, own, ent)]
    reshape x2 -> x1, local copies, waits for them, and re-layouts: 3.71 us -> 5.34 us  [on_device(): lax.all_to_all(both, AXES, split_axis=0, concat_axis=0)]
  transfers between devices with their start and end apart: 1 -> 1, of which waited for: 1 -> 1; matrix products, arithmetic and copies ran while one was open for 3% -> 2% of each run, Pallas kernels for 0% -> 0%
where the time goes in v2:
time: 245 us
  Pallas kernels  128 us (52%)
  blocking collectives  77.7 us (32%)
  waiting for transfers between devices  18.1 us (7%)
  local copies, waits for them, and re-layouts  12 us (5%)
  starting transfers between devices  4.63 us (2%)
  other arithmetic  3.33 us (1%)
    pallas_call x1, Pallas kernels, on_device(): pl.pallas_call(pack_kernel, out_shape=jax.ShapeDtypeStruct((devices, 2 *...  79.9 us
    all_to_all x1, blocking collectives, on_device(): lax.all_to_all(both, AXES, split_axis=0, concat_axis=0)  47.4 us
    pallas_call x1, Pallas kernels, on_device(): pl.pallas_call(unpack_kernel, out_shape=jax.ShapeDtypeStruct((LATENT // (...  40.5 us
    all_to_all x1, waiting for transfers between devices, on_device(): lax.all_to_all(moved.reshape(devices, own, ent), AXES, split_axis=0, conc...  18.1 us
    all_to_all x1, blocking collectives, on_device(): total = lax.all_to_all(total, AXES, split_axis=0, concat_axis=0)  15.2 us
    all_to_all x1, blocking collectives, on_device(): parts = lax.all_to_all(parts, AXES, split_axis=0, concat_axis=0)  15.2 us
    pallas_call x1, Pallas kernels, on_device(): pl.pallas_call(sweep_kernel, out_shape=(jax.ShapeDtypeStruct((BATCH, ent)...  6.95 us
    reshape x1, local copies, waits for them, and re-layouts, on_device(): lax.all_to_all(both, AXES, split_axis=0, concat_axis=0)  5.34 us
  transfers between devices with their start and end apart: 1, of which 1 were waited for; matrix products, arithmetic and copies ran while one was open for 2% of the time, Pallas kernels for 0%

profile of v2, /device:TPU:1, one launch (start us, length us, event | category | flops | bytes accessed | tf_op | source)
XLA Modules:
  0.0 244.6 jit_solution(1975385443323694451)
XLA Ops:
  0.6 79.9 %shard_map.49 = bf16[128,8,5,2,128]{4,3,2,1,0:T(2,128)(2,1)} custom-call(bf16[507,5,2,128]{3,2,1,0:T(2,128)(2,1)} %bitcast.23, bf16[507,5,2,128]{3,2,1,0:T(2,128)(2,1)} %bitcast.24), custom_call_target="tpu_custom_call" | custom-call | tf_op jit(solution)/shard_map/pallas_call | solution.py:162
  80.5 47.4 %all_to_all.20 = bf16[128,2,5120]{2,1,0:T(2,128)(2,1)} all-to-all(bf16[128,2,5120]{2,1,0:T(2,128)(2,1)} %bitcast.21), channel_id=1, replica_groups=mesh['dp'=16,'dim'=8] {'dp','dim'}, dimensions={0} | all-to-all | bytes 5242880 | tf_op jit(solution)/shard_map/all_to_all | solution.py:173
  127.9 5.3 %reshape.34.both_ref = bf16[256,5120]{1,0:T(8,128)(2,1)S(1)} reshape(bf16[128,2,5120]{2,1,0:T(2,128)(2,1)} %all_to_all.20) | data formatting | bytes 5242880 | tf_op jit(solution)/shard_map/reshape | solution.py:173
  133.2 0.6 shard_map.50
  133.8 15.2 %all_to_all.21.parts_ref = f32[128,4,128]{2,1,0:T(4,128)S(1)} all-to-all(f32[128,4,128]{2,1,0:T(4,128)S(1)} %shard_map.50), channel_id=1, replica_groups=mesh['dp'=16,'dim'=8] {'dp','dim'}, dimensions={0} | all-to-all | bytes 524288 | tf_op jit(solution)/shard_map/all_to_all | solution.py:177
  149.0 0.2 shard_map.51
  149.2 15.2 %all_to_all.22.cost_ref = f32[128,4,128]{2,1,0:T(4,128)S(1)} all-to-all(f32[128,4,128]{2,1,0:T(4,128)S(1)} %shard_map.51), channel_id=1, replica_groups=mesh['dp'=16,'dim'=8] {'dp','dim'}, dimensions={0} | all-to-all | bytes 524288 | tf_op jit(solution)/shard_map/all_to_all | solution.py:179
  164.4 6.9 %shard_map.52 = (bf16[256,2560]{1,0:T(8,128)(2,1)S(1)}, f32[2,256]{1,0:T(2,128)S(1)}) custom-call(f32[128,4,128]{2,1,0:T(4,128)S(1)} %all_to_all.22.cost_ref, bf16[256,5120]{1,0:T(8,128)(2,1)S(1)} %reshape.34.both_ref), custom_call_target="tpu_custom_call" | custom-call | tf_op jit(solution)/shard_map/pallas_call | solution.py:181
  171.4 0.0 copy-start
  171.4 1.0 copy-done
  172.4 3.9 %reshape.35 = bf16[128,2,2560]{2,1,0:T(2,128)(2,1)} reshape(bf16[256,2560]{1,0:T(8,128)(2,1)} %copy-done) | data formatting | bytes 2621440 | tf_op jit(solution)/shard_map/reshape | solution.py:197
  176.4 0.0 copy-start.2
  176.4 4.6 %all-to-all-start.3 = ((bf16[128,2,2560]{2,1,0:T(2,128)(2,1)}), bf16[128,2,2560]{2,1,0:T(2,128)(2,1)S(1)}, u32[]{:S(2)}, u32[]{:S(2)}) async-start(bf16[128,2,2560]{2,1,0:T(2,128)(2,1)} %reshape.35), calls=%async_computation.3 | async-start | bytes 2621440 | tf_op jit(solution)/shard_map/all_to_all | solution.py:197
  181.0 0.0 copy-done.2
  181.0 2.8 %multiply_reduce_fusion = f32[2]{0:T(128)S(1)} fusion(bf16[2,324480]{1,0:T(2,128)(2,1)S(1)} %copy-done.2), kind=kLoop, calls=%fused_computation | loop fusion | flops 1946878 | bytes 1297928 | tf_op jit(solution)/shard_map/reduce_sum | solution.py:211
  183.8 0.1 constant_dynamic-slice_fusion
  183.9 0.5 slice_bitcast_fusion
  184.4 0.5 bitcast_add_fusion
  184.9 18.1 %all-to-all-done.3 = bf16[128,2,2560]{2,1,0:T(2,128)(2,1)S(1)} async-done(((bf16[128,2,2560]{2,1,0:T(2,128)(2,1)}), bf16[128,2,2560]{2,1,0:T(2,128)(2,1)S(1)}, u32[]{:S(2)}, u32[]{:S(2)}) %all-to-all-start.3) | async-done | bytes 1310752 | tf_op jit(solution)/shard_map/all_to_all | solution.py:197
  203.1 0.0 copy-start.1
  203.1 1.1 copy-done.1
  204.1 40.5 %shard_map.53 = bf16[507,5,2,128]{3,2,1,0:T(2,128)(2,1)} custom-call(bf16[128,4,5,2,128]{4,3,2,1,0:T(2,128)(2,1)} %bitcast.22), custom_call_target="tpu_custom_call" | custom-call | tf_op jit(solution)/shard_map/pallas_call | solution.py:199
Async XLA Ops:
  171.4 1.1 copy-start
  176.4 4.6 %copy-start.2 = (bf16[2,324480]{1,0:T(2,128)(2,1)S(1)}, bf16[2,324480]{1,0:T(2,128)(2,1)}, u32[]{:S(2)}) copy-start(bf16[2,324480]{1,0:T(2,128)(2,1)} %param.2) | copy-start | bytes 3893764
  176.4 26.7 %all-to-all-start.3 = ((bf16[128,2,2560]{2,1,0:T(2,128)(2,1)}), bf16[128,2,2560]{2,1,0:T(2,128)(2,1)S(1)}, u32[]{:S(2)}, u32[]{:S(2)}) async-start(bf16[128,2,2560]{2,1,0:T(2,128)(2,1)} %reshape.35), calls=%async_computation.3 | async-start | bytes 2621440 | tf_op jit(solution)/shard_map/all_to_all | solution.py:197
  203.1 1.1 copy-start.1

commit v3 on v2

--- a/solution.py
+++ b/solution.py
@@ -13,11 +13,11 @@
 AXES = ("dp", "dim")
 LANES = 128
 TEMPER = 0.25 / math.sqrt(LATENT)
-UNIT = TEMPER * math.log(2.0)
+BIT = TEMPER * math.log(2.0)
 DRIFT = 2.0**40
-VMEM = 16 * 1024 * 1024
+VMEM = 12 * 1024 * 1024
 UNITS = 4
-UNIT_TILES = 5
+UNIT = 640
 
 
 def pack_kernel(noise_ref, data_ref, out_ref, zeros, sems):
@@ -86,7 +86,7 @@
 
 
 def sweep_kernel(cost_ref, both_ref, out_ref, pots_ref, bias, kern, row_base, col_base, row_fac, col_fac):
-    bias[...] = whole_of(cost_ref) * (-1.0 / (LATENT * UNIT))
+    bias[...] = whole_of(cost_ref) * (-1.0 / (LATENT * BIT))
 
     def log_sweep():
         col = col_base[...] + jnp.log2(col_fac[...])
@@ -144,32 +144,33 @@
     out_ref[...] = lax.dot_general(
         weights, both_ref[:, both_ref.shape[1] // 2 :], (((0,), (0,)), ((), ())), preferred_element_type=jnp.float32
     ).astype(jnp.bfloat16)
-    pots_ref[0:1, :] = (row_base[...] + jnp.log2(row_fac[...])) * UNIT
-    pots_ref[1:2, :] = jnp.transpose((col_base[...] + jnp.log2(col_fac[...])) * UNIT)
+    pots_ref[0:1, :] = (row_base[...] + jnp.log2(row_fac[...])) * BIT
+    pots_ref[1:2, :] = jnp.transpose((col_base[...] + jnp.log2(col_fac[...])) * BIT)
 
 
 def on_device(noise, data):
     devices = lax.axis_size(AXES)
     own = noise.shape[0]
-    ent = UNITS * UNIT_TILES * LANES
+    ent = UNITS * UNIT
+    units = LATENT // UNIT
     params = pltpu.CompilerParams(vmem_limit_bytes=VMEM)
     anywhere = pl.BlockSpec(memory_space=pl.ANY)
 
     def units_of(rows):
-        units = rows.shape[1] // (UNIT_TILES * LANES)
-        return rows.reshape(own, units, UNIT_TILES, LANES).transpose(1, 2, 0, 3)
+        return rows.reshape(own, units, UNIT).transpose(1, 0, 2)
 
     both = pl.pallas_call(
         pack_kernel,
-        out_shape=jax.ShapeDtypeStruct((devices, 2 * UNITS, UNIT_TILES, own, LANES), noise.dtype),
+        out_shape=jax.ShapeDtypeStruct((devices, 2 * UNITS, own, UNIT), noise.dtype),
         in_specs=[anywhere, anywhere],
         out_specs=anywhere,
         scratch_shapes=[
-            pltpu.VMEM((UNITS * devices - LATENT // (UNIT_TILES * LANES), UNIT_TILES, own, LANES), noise.dtype),
+            pltpu.VMEM((UNITS * devices - units, own, UNIT), noise.dtype),
             pltpu.SemaphoreType.DMA((4 * UNITS,)),
         ],
+        compiler_params=params,
     )(units_of(noise), units_of(data))
-    both = both.reshape(devices, -1, own, LANES).transpose(0, 2, 1, 3).reshape(devices, own, 2 * ent)
+    both = both.transpose(0, 2, 1, 3).reshape(devices, own, 2 * ent)
     both = lax.all_to_all(both, AXES, split_axis=0, concat_axis=0).reshape(BATCH, 2 * ent)
 
     pieces = jax.ShapeDtypeStruct((devices, 4, LANES), jnp.float32)
@@ -195,15 +196,16 @@
         compiler_params=params,
     )(total, both)
     moved = lax.all_to_all(moved.reshape(devices, own, ent), AXES, split_axis=0, concat_axis=0)
-    moved = moved.reshape(devices, own, UNITS, UNIT_TILES, LANES).transpose(0, 2, 3, 1, 4)
+    moved = moved.reshape(devices, own, UNITS, UNIT).transpose(0, 2, 1, 3)
     targets = pl.pallas_call(
         unpack_kernel,
-        out_shape=jax.ShapeDtypeStruct((LATENT // (UNIT_TILES * LANES), UNIT_TILES, own, LANES), moved.dtype),
+        out_shape=jax.ShapeDtypeStruct((units, own, UNIT), moved.dtype),
         in_specs=[anywhere],
         out_specs=anywhere,
         scratch_shapes=[pltpu.SemaphoreType.DMA((UNITS,))],
+        compiler_params=params,
     )(moved)
-    targets = targets.transpose(2, 0, 1, 3).reshape(own, LATENT)
+    targets = targets.transpose(1, 0, 2).reshape(own, LATENT)
 
     offset = lax.axis_index(AXES) * own
     mine = lax.dynamic_slice_in_dim(pots, offset, own, 1)

time: 245 us -> 128 us (0.52)
  Pallas kernels: 128 us -> 9.28 us
    pallas_call x1, Pallas kernels: 79.9 us -> 0.52 us  [on_device(): pl.pallas_call(pack_kernel, out_shape=jax.ShapeDtypeStruct((devices, 2 *...]
    pallas_call x1, Pallas kernels: 40.5 us -> 1.08 us  [on_device(): pl.pallas_call(unpack_kernel, out_shape=jax.ShapeDtypeStruct((units, own,...]
  transfers between devices with their start and end apart: 1 -> 1, of which waited for: 1 -> 1; matrix products, arithmetic and copies ran while one was open for 2% -> 3% of each run, Pallas kernels for 0% -> 0%
where the time goes in v3:
time: 128 us; the launch traced here: 127 us
  blocking collectives  77.5 us (61%)
  waiting for transfers between devices  18.1 us (14%)
  local copies, waits for them, and re-layouts  13.6 us (11%)
  Pallas kernels  9.28 us (7%)
  starting transfers between devices  4.63 us (4%)
  other arithmetic  3.33 us (3%)
    all_to_all x1, blocking collectives, on_device(): lax.all_to_all(both, AXES, split_axis=0, concat_axis=0)  47.1 us
    all_to_all x1, waiting for transfers between devices, on_device(): lax.all_to_all(moved.reshape(devices, own, ent), AXES, split_axis=0, conc...  18.1 us
    all_to_all x1, blocking collectives, on_device(): total = lax.all_to_all(total, AXES, split_axis=0, concat_axis=0)  15.2 us
    all_to_all x1, blocking collectives, on_device(): parts = lax.all_to_all(parts, AXES, split_axis=0, concat_axis=0)  15.2 us
    pallas_call x1, Pallas kernels, on_device(): pl.pallas_call(sweep_kernel, out_shape=(jax.ShapeDtypeStruct((BATCH, ent)...  6.94 us
    reshape x1, local copies, waits for them, and re-layouts, on_device(): lax.all_to_all(both, AXES, split_axis=0, concat_axis=0)  5.34 us
    all_to_all x1, starting transfers between devices, on_device(): lax.all_to_all(moved.reshape(devices, own, ent), AXES, split_axis=0, conc...  4.63 us
    reshape x1, local copies, waits for them, and re-layouts, on_device(): moved.reshape(devices, own, ent)  3.95 us
  transfers between devices with their start and end apart: 1, of which 1 were waited for; matrix products, arithmetic and copies ran while one was open for 3% of the time, Pallas kernels for 0%

profile of v3, /device:TPU:1, one launch (start us, length us, event | category | flops | bytes accessed | tf_op | source)
XLA Modules:
  0.0 127.2 jit_solution(10042174395964713436)
XLA Ops:
  0.6 0.0 copy-start
  0.6 1.3 %copy-done = bf16[2,324480]{1,0:T(2,128)(2,1)S(1)} copy-done((bf16[2,324480]{1,0:T(2,128)(2,1)S(1)}, bf16[2,324480]{1,0:T(2,128)(2,1)}, u32[]{:S(2)}) %copy-start) | copy-done | bytes 1297944
  1.9 0.0 copy-start.3
  1.9 1.3 %copy-done.3 = bf16[2,324480]{1,0:T(2,128)(2,1)S(1)} copy-done((bf16[2,324480]{1,0:T(2,128)(2,1)S(1)}, bf16[2,324480]{1,0:T(2,128)(2,1)}, u32[]{:S(2)}) %copy-start.3) | copy-done | bytes 1297944
  3.3 0.5 shard_map.49
  3.8 47.1 %all_to_all.20 = bf16[128,2,5120]{2,1,0:T(2,128)(2,1)} all-to-all(bf16[128,2,5120]{2,1,0:T(2,128)(2,1)S(1)} %bitcast.19), channel_id=1, replica_groups=mesh['dp'=16,'dim'=8] {'dp','dim'}, dimensions={0} | all-to-all | bytes 5242880 | tf_op jit(solution)/shard_map/all_to_all | solution.py:174
  50.9 5.3 %reshape.30.both_ref = bf16[256,5120]{1,0:T(8,128)(2,1)S(1)} reshape(bf16[128,2,5120]{2,1,0:T(2,128)(2,1)} %all_to_all.20) | data formatting | bytes 5242880 | tf_op jit(solution)/shard_map/reshape | solution.py:174
  56.3 0.6 shard_map.50
  56.9 15.2 %all_to_all.21.parts_ref = f32[128,4,128]{2,1,0:T(4,128)S(1)} all-to-all(f32[128,4,128]{2,1,0:T(4,128)S(1)} %shard_map.50), channel_id=1, replica_groups=mesh['dp'=16,'dim'=8] {'dp','dim'}, dimensions={0} | all-to-all | bytes 524288 | tf_op jit(solution)/shard_map/all_to_all | solution.py:178
  72.0 0.2 shard_map.51
  72.2 15.2 %all_to_all.22.cost_ref = f32[128,4,128]{2,1,0:T(4,128)S(1)} all-to-all(f32[128,4,128]{2,1,0:T(4,128)S(1)} %shard_map.51), channel_id=1, replica_groups=mesh['dp'=16,'dim'=8] {'dp','dim'}, dimensions={0} | all-to-all | bytes 524288 | tf_op jit(solution)/shard_map/all_to_all | solution.py:180
  87.4 6.9 %shard_map.52 = (bf16[256,2560]{1,0:T(8,128)(2,1)S(1)}, f32[2,256]{1,0:T(2,128)S(1)}) custom-call(f32[128,4,128]{2,1,0:T(4,128)S(1)} %all_to_all.22.cost_ref, bf16[256,5120]{1,0:T(8,128)(2,1)S(1)} %reshape.30.both_ref), custom_call_target="tpu_custom_call" | custom-call | tf_op jit(solution)/shard_map/pallas_call | solution.py:182
  94.4 0.0 copy-start.2
  94.4 1.1 copy-done.2
  95.4 4.0 %reshape.31 = bf16[128,2,2560]{2,1,0:T(2,128)(2,1)} reshape(bf16[256,2560]{1,0:T(8,128)(2,1)} %copy-done.2) | data formatting | bytes 2621440 | tf_op jit(solution)/shard_map/reshape | solution.py:198
  99.4 0.0 copy-start.1
  99.4 4.6 %all-to-all-start.3 = ((bf16[128,2,2560]{2,1,0:T(2,128)(2,1)}), bf16[128,2,2560]{2,1,0:T(2,128)(2,1)S(1)}, u32[]{:S(2)}, u32[]{:S(2)}) async-start(bf16[128,2,2560]{2,1,0:T(2,128)(2,1)} %reshape.31), calls=%async_computation.3 | async-start | bytes 2621440 | tf_op jit(solution)/shard_map/all_to_all | solution.py:198
  104.0 0.0 copy-done.1
  104.1 2.8 %multiply_reduce_fusion = f32[2]{0:T(128)S(1)} fusion(bf16[2,324480]{1,0:T(2,128)(2,1)S(1)} %copy-done.1), kind=kLoop, calls=%fused_computation | loop fusion | flops 1946878 | bytes 1297928 | tf_op jit(solution)/shard_map/reduce_sum | solution.py:213
  106.9 0.1 constant_dynamic-slice_fusion
  106.9 0.5 slice_bitcast_fusion
  107.5 0.5 bitcast_add_fusion
  108.0 18.1 %all-to-all-done.3 = bf16[128,2,2560]{2,1,0:T(2,128)(2,1)S(1)} async-done(((bf16[128,2,2560]{2,1,0:T(2,128)(2,1)}), bf16[128,2,2560]{2,1,0:T(2,128)(2,1)S(1)}, u32[]{:S(2)}, u32[]{:S(2)}) %all-to-all-start.3) | async-done | bytes 1310752 | tf_op jit(solution)/shard_map/all_to_all | solution.py:198
  126.1 1.1 shard_map.53
Async XLA Ops:
  0.6 1.3 %copy-start = (bf16[2,324480]{1,0:T(2,128)(2,1)S(1)}, bf16[2,324480]{1,0:T(2,128)(2,1)}, u32[]{:S(2)}) copy-start(bf16[2,324480]{1,0:T(2,128)(2,1)} %param.2) | copy-start | bytes 3893764
  1.9 1.3 %copy-start.3 = (bf16[2,324480]{1,0:T(2,128)(2,1)S(1)}, bf16[2,324480]{1,0:T(2,128)(2,1)}, u32[]{:S(2)}) copy-start(bf16[2,324480]{1,0:T(2,128)(2,1)} %param.3) | copy-start | bytes 3893764
  94.4 1.1 copy-start.2
  99.4 4.6 %copy-start.1 = (bf16[2,324480]{1,0:T(2,128)(2,1)S(1)}, bf16[2,324480]{1,0:T(2,128)(2,1)}, u32[]{:S(2)}) copy-start(bf16[2,324480]{1,0:T(2,128)(2,1)} %param.2) | copy-start | bytes 3893764
  99.4 26.7 %all-to-all-start.3 = ((bf16[128,2,2560]{2,1,0:T(2,128)(2,1)}), bf16[128,2,2560]{2,1,0:T(2,128)(2,1)S(1)}, u32[]{:S(2)}, u32[]{:S(2)}) async-start(bf16[128,2,2560]{2,1,0:T(2,128)(2,1)} %reshape.31), calls=%async_computation.3 | async-start | bytes 2621440 | tf_op jit(solution)/shard_map/all_to_all | solution.py:198

commit v4 on v3

--- a/solution.py
+++ b/solution.py
@@ -15,7 +15,7 @@
 TEMPER = 0.25 / math.sqrt(LATENT)
 BIT = TEMPER * math.log(2.0)
 DRIFT = 2.0**40
-VMEM = 12 * 1024 * 1024
+VMEM = 24 * 1024 * 1024
 UNITS = 4
 UNIT = 640
 
@@ -69,11 +69,13 @@
     return jnp.concatenate(rows, axis=0)
 
 
-def gram_kernel(both_ref, out_ref):
-    ent = both_ref.shape[1] // 2
-    data = both_ref[:, ent:]
+def gram_kernel(both_ref, out_ref, data_ref):
+    ent = data_ref.shape[1]
+    noise = both_ref[:, :, :ent].reshape(data_ref.shape)
+    data = both_ref[:, :, ent:].reshape(data_ref.shape)
+    data_ref[...] = data
     gram = lax.dot_general(
-        data, both_ref[:, :ent], (((1,), (1,)), ((), ())), preferred_element_type=jnp.float32
+        data, noise, (((1,), (1,)), ((), ())), preferred_element_type=jnp.float32
     )
     wide = data.astype(jnp.float32)
     data_sq = jnp.sum(wide * wide, axis=1, keepdims=True)
@@ -85,7 +87,7 @@
     out_ref[...] = jnp.broadcast_to(total[None], out_ref.shape)
 
 
-def sweep_kernel(cost_ref, both_ref, out_ref, pots_ref, bias, kern, row_base, col_base, row_fac, col_fac):
+def sweep_kernel(cost_ref, data_ref, out_ref, pots_ref, bias, kern, row_base, col_base, row_fac, col_fac):
     bias[...] = whole_of(cost_ref) * (-1.0 / (LATENT * BIT))
 
     def log_sweep():
@@ -141,9 +143,10 @@
 
     scaled = kern[...]
     weights = (scaled / jnp.sum(scaled, axis=0, keepdims=True)).astype(jnp.bfloat16)
-    out_ref[...] = lax.dot_general(
-        weights, both_ref[:, both_ref.shape[1] // 2 :], (((0,), (0,)), ((), ())), preferred_element_type=jnp.float32
-    ).astype(jnp.bfloat16)
+    moved = lax.dot_general(
+        weights, data_ref[...], (((0,), (0,)), ((), ())), preferred_element_type=jnp.float32
+    )
+    out_ref[...] = moved.astype(jnp.bfloat16).reshape(out_ref.shape)
     pots_ref[0:1, :] = (row_base[...] + jnp.log2(row_fac[...])) * BIT
     pots_ref[1:2, :] = jnp.transpose((col_base[...] + jnp.log2(col_fac[...])) * BIT)
 
@@ -171,10 +174,14 @@
         compiler_params=params,
     )(units_of(noise), units_of(data))
     both = both.transpose(0, 2, 1, 3).reshape(devices, own, 2 * ent)
-    both = lax.all_to_all(both, AXES, split_axis=0, concat_axis=0).reshape(BATCH, 2 * ent)
+    both = lax.all_to_all(both, AXES, split_axis=0, concat_axis=0)
 
     pieces = jax.ShapeDtypeStruct((devices, 4, LANES), jnp.float32)
-    parts = pl.pallas_call(gram_kernel, out_shape=pieces, compiler_params=params)(both)
+    parts, data_ent = pl.pallas_call(
+        gram_kernel,
+        out_shape=(pieces, jax.ShapeDtypeStruct((BATCH, ent), data.dtype)),
+        compiler_params=params,
+    )(both)
     parts = lax.all_to_all(parts, AXES, split_axis=0, concat_axis=0)
     total = pl.pallas_call(sum_kernel, out_shape=pieces, compiler_params=params)(parts)
     total = lax.all_to_all(total, AXES, split_axis=0, concat_axis=0)
@@ -182,7 +189,7 @@
     moved, pots = pl.pallas_call(
         sweep_kernel,
         out_shape=(
-            jax.ShapeDtypeStruct((BATCH, ent), jnp.bfloat16),
+            jax.ShapeDtypeStruct((devices, own, ent), jnp.bfloat16),
             jax.ShapeDtypeStruct((2, BATCH), jnp.float32),
         ),
         scratch_shapes=[
@@ -194,8 +201,8 @@
             pltpu.VMEM((BATCH, 1), jnp.float32),
         ],
         compiler_params=params,
-    )(total, both)
-    moved = lax.all_to_all(moved.reshape(devices, own, ent), AXES, split_axis=0, concat_axis=0)
+    )(total, data_ent)
+    moved = lax.all_to_all(moved, AXES, split_axis=0, concat_axis=0)
     moved = moved.reshape(devices, own, UNITS, UNIT).transpose(0, 2, 1, 3)
     targets = pl.pallas_call(
         unpack_kernel,

time: 128 us -> 119 us (0.930)
  local copies, waits for them, and re-layouts: 13.6 us -> 4.27 us
    reshape x2 -> x0, local copies, waits for them, and re-layouts: 9.29 us -> none  [the longest x1 5.34 us: on_device(): lax.all_to_all(both, AXES, split_axis=0, concat_axis=0)]
where the time goes in v4:
time: 119 us; the launch traced here: 118 us
  blocking collectives  77.4 us (65%)
  waiting for transfers between devices  18.1 us (15%)
  Pallas kernels  9.93 us (8%)
  starting transfers between devices  4.63 us (4%)
  local copies, waits for them, and re-layouts  4.27 us (4%)
  other arithmetic  3.33 us (3%)
    all_to_all x1, blocking collectives, on_device(): both = lax.all_to_all(both, AXES, split_axis=0, concat_axis=0)  47 us
    all_to_all x1, waiting for transfers between devices, on_device(): moved = lax.all_to_all(moved, AXES, split_axis=0, concat_axis=0)  18.1 us
    all_to_all x1, blocking collectives, on_device(): total = lax.all_to_all(total, AXES, split_axis=0, concat_axis=0)  15.2 us
    all_to_all x1, blocking collectives, on_device(): parts = lax.all_to_all(parts, AXES, split_axis=0, concat_axis=0)  15.2 us
    pallas_call x1, Pallas kernels, on_device(): pl.pallas_call(sweep_kernel, out_shape=(jax.ShapeDtypeStruct((devices, ow...  6.95 us
    all_to_all x1, starting transfers between devices, on_device(): moved = lax.all_to_all(moved, AXES, split_axis=0, concat_axis=0)  4.63 us
    unnamed x8, local copies, waits for them, and re-layouts  3.68 us
    reduce_sum x1, other arithmetic, on_device(): noise_sq = jnp.sum(wide * wide, axis=1)  2.82 us
  transfers between devices with their start and end apart: 1, of which 1 were waited for; matrix products, arithmetic and copies ran while one was open for 3% of the time, Pallas kernels for 0%

profile of v4, /device:TPU:1, one launch (start us, length us, event | category | flops | bytes accessed | tf_op | source)
XLA Modules:
  0.0 118.4 jit_solution(12161720975328780987)
XLA Ops:
  0.6 0.0 copy-start
  0.6 1.3 %copy-done = bf16[2,324480]{1,0:T(2,128)(2,1)S(1)} copy-done((bf16[2,324480]{1,0:T(2,128)(2,1)S(1)}, bf16[2,324480]{1,0:T(2,128)(2,1)}, u32[]{:S(2)}) %copy-start) | copy-done | bytes 1297944
  1.9 0.0 copy-start.3
  1.9 1.3 %copy-done.3 = bf16[2,324480]{1,0:T(2,128)(2,1)S(1)} copy-done((bf16[2,324480]{1,0:T(2,128)(2,1)S(1)}, bf16[2,324480]{1,0:T(2,128)(2,1)}, u32[]{:S(2)}) %copy-start.3) | copy-done | bytes 1297944
  3.3 0.5 shard_map.49
  3.8 47.0 %all_to_all.20.both_ref = bf16[128,2,5120]{2,1,0:T(2,128)(2,1)S(1)} all-to-all(bf16[128,2,5120]{2,1,0:T(2,128)(2,1)S(1)} %bitcast.19), channel_id=1, replica_groups=mesh['dp'=16,'dim'=8] {'dp','dim'}, dimensions={0} | all-to-all | bytes 5242880 | tf_op jit(solution)/shard_map/all_to_all | solution.py:177
  50.8 1.2 %shard_map.50 = (f32[128,4,128]{2,1,0:T(4,128)S(1)}, bf16[256,2560]{1,0:T(8,128)(2,1)S(1)}) custom-call(bf16[128,2,5120]{2,1,0:T(2,128)(2,1)S(1)} %all_to_all.20.both_ref), custom_call_target="tpu_custom_call" | custom-call | tf_op jit(solution)/shard_map/pallas_call | solution.py:180
  52.0 15.2 %all_to_all.21.parts_ref = f32[128,4,128]{2,1,0:T(4,128)S(1)} all-to-all(f32[128,4,128]{2,1,0:T(4,128)S(1)} %get-tuple-element.7), channel_id=1, replica_groups=mesh['dp'=16,'dim'=8] {'dp','dim'}, dimensions={0} | all-to-all | bytes 524288 | tf_op jit(solution)/shard_map/all_to_all | solution.py:185
  67.2 0.2 shard_map.51
  67.4 15.2 %all_to_all.22.cost_ref = f32[128,4,128]{2,1,0:T(4,128)S(1)} all-to-all(f32[128,4,128]{2,1,0:T(4,128)S(1)} %shard_map.51), channel_id=1, replica_groups=mesh['dp'=16,'dim'=8] {'dp','dim'}, dimensions={0} | all-to-all | bytes 524288 | tf_op jit(solution)/shard_map/all_to_all | solution.py:187
  82.6 6.9 %shard_map.52 = (bf16[128,2,2560]{2,1,0:T(2,128)(2,1)S(1)}, f32[2,256]{1,0:T(2,128)S(1)}) custom-call(f32[128,4,128]{2,1,0:T(4,128)S(1)} %all_to_all.22.cost_ref, bf16[256,2560]{1,0:T(8,128)(2,1)S(1)} %get-tuple-element.8.data_ref), custom_call_target="tpu_custom_call" | custom-call | tf_op jit(solution)/shard_map/pallas_call | solution.py:189
  89.5 0.0 copy-start.2
  89.6 1.1 copy-done.2
  90.6 0.0 copy-start.1
  90.6 4.6 %all-to-all-start.3 = ((bf16[128,2,2560]{2,1,0:T(2,128)(2,1)}), bf16[128,2,2560]{2,1,0:T(2,128)(2,1)S(1)}, u32[]{:S(2)}, u32[]{:S(2)}) async-start(bf16[128,2,2560]{2,1,0:T(2,128)(2,1)} %copy-done.2), calls=%async_computation.3 | async-start | bytes 2621440 | tf_op jit(solution)/shard_map/all_to_all | solution.py:205
  95.3 0.0 copy-done.1
  95.3 2.8 %multiply_reduce_fusion = f32[2]{0:T(128)S(1)} fusion(bf16[2,324480]{1,0:T(2,128)(2,1)S(1)} %copy-done.1), kind=kLoop, calls=%fused_computation | loop fusion | flops 1946878 | bytes 1297928 | tf_op jit(solution)/shard_map/reduce_sum | solution.py:220
  98.1 0.1 constant_dynamic-slice_fusion
  98.2 0.5 slice_bitcast_fusion
  98.7 0.5 bitcast_add_fusion
  99.2 18.1 %all-to-all-done.3 = bf16[128,2,2560]{2,1,0:T(2,128)(2,1)S(1)} async-done(((bf16[128,2,2560]{2,1,0:T(2,128)(2,1)}), bf16[128,2,2560]{2,1,0:T(2,128)(2,1)S(1)}, u32[]{:S(2)}, u32[]{:S(2)}) %all-to-all-start.3) | async-done | bytes 1310752 | tf_op jit(solution)/shard_map/all_to_all | solution.py:205
  117.3 1.1 shard_map.53
Async XLA Ops:
  0.6 1.3 %copy-start = (bf16[2,324480]{1,0:T(2,128)(2,1)S(1)}, bf16[2,324480]{1,0:T(2,128)(2,1)}, u32[]{:S(2)}) copy-start(bf16[2,324480]{1,0:T(2,128)(2,1)} %param.2) | copy-start | bytes 3893764
  1.9 1.3 %copy-start.3 = (bf16[2,324480]{1,0:T(2,128)(2,1)S(1)}, bf16[2,324480]{1,0:T(2,128)(2,1)}, u32[]{:S(2)}) copy-start(bf16[2,324480]{1,0:T(2,128)(2,1)} %param.3) | copy-start | bytes 3893764
  89.5 1.1 copy-start.2
  90.6 4.6 %copy-start.1 = (bf16[2,324480]{1,0:T(2,128)(2,1)S(1)}, bf16[2,324480]{1,0:T(2,128)(2,1)}, u32[]{:S(2)}) copy-start(bf16[2,324480]{1,0:T(2,128)(2,1)} %param.2) | copy-start | bytes 3893764
  90.6 26.7 %all-to-all-start.3 = ((bf16[128,2,2560]{2,1,0:T(2,128)(2,1)}), bf16[128,2,2560]{2,1,0:T(2,128)(2,1)S(1)}, u32[]{:S(2)}, u32[]{:S(2)}) async-start(bf16[128,2,2560]{2,1,0:T(2,128)(2,1)} %copy-done.2), calls=%async_computation.3 | async-start | bytes 2621440 | tf_op jit(solution)/shard_map/all_to_all | solution.py:205

commit v5 on v4

--- a/solution.py
+++ b/solution.py
@@ -87,58 +87,73 @@
     out_ref[...] = jnp.broadcast_to(total[None], out_ref.shape)
 
 
-def sweep_kernel(cost_ref, data_ref, out_ref, pots_ref, bias, kern, row_base, col_base, row_fac, col_fac):
+def sweep_kernel(cost_ref, data_ref, out_ref, pots_ref, bias, kern, row_pot, col_pot, col_fac):
     bias[...] = whole_of(cost_ref) * (-1.0 / (LATENT * BIT))
+    col_pot[...] = jnp.zeros_like(col_pot)
 
     def log_sweep():
-        col = col_base[...] + jnp.log2(col_fac[...])
-        scaled = bias[...] + col
+        scaled = bias[...] + col_pot[...]
         top = jnp.max(scaled, axis=0, keepdims=True)
         row = -(top + jnp.log2(jnp.sum(jnp.exp2(scaled - top), axis=0, keepdims=True)))
         scaled = bias[...] + row
         top = jnp.max(scaled, axis=1, keepdims=True)
         col = -(top + jnp.log2(jnp.sum(jnp.exp2(scaled - top), axis=1, keepdims=True)))
-        row_base[...] = row
-        col_base[...] = col
-        row_fac[...] = jnp.ones_like(row)
-        col_fac[...] = jnp.ones_like(col)
+        row_pot[...] = row
+        col_pot[...] = col
         kern[...] = jnp.exp2(scaled + col)
 
-    col_base[...] = jnp.zeros_like(col_base)
+    log_sweep()
     col_fac[...] = jnp.ones_like(col_fac)
-    log_sweep()
+
+    tile = (8, LANES)
+    blocks = [pl.ds(start, 8) for start in range(0, BATCH, 8)]
+    halves = [pl.ds(start, LANES) for start in range(0, BATCH, LANES)]
 
     def sweep(step, carry):
-        row = 1.0 / jnp.sum(kern[...] * col_fac[...], axis=0, keepdims=True)
-        col = 1.0 / jnp.sum(kern[...] * row, axis=1, keepdims=True)
-        near = (
-            (jnp.max(row) <= DRIFT)
-            & (jnp.min(row) >= 1.0 / DRIFT)
-            & (jnp.max(col) <= DRIFT)
-            & (jnp.min(col) >= 1.0 / DRIFT)
-        )
-
-        @pl.when(near)
-        def _():
-            row_fac[...] = row
-            col_fac[...] = col
-
-        @pl.when(jnp.logical_not(near))
-        def _():
-            log_sweep()
-
-        return carry
-
-    lax.fori_loop(1, SWEEPS, sweep, 0)
-    near = jnp.min(jnp.sum(kern[...] * col_fac[...], axis=0)) >= 1.0 / DRIFT
+        low, high, _ = carry
+        sums = [[jnp.zeros(tile, jnp.float32) for _ in halves] for _ in range(2)]
+        for n, block in enumerate(blocks):
+            factor = col_fac[block, :]
+            for h, half in enumerate(halves):
+                sums[n % 2][h] += kern[block, half] * factor
+        rows = []
+        for first, second in zip(*sums):
+            total = jnp.broadcast_to(jnp.sum(first + second, axis=0, keepdims=True), tile)
+            low, high = jnp.minimum(low, total), jnp.maximum(high, total)
+            rows.append(1.0 / total)
+        for block in blocks:
+            total = sum(kern[block, half] * row for half, row in zip(halves, rows))
+            total = jnp.broadcast_to(jnp.sum(total, axis=1, keepdims=True), tile)
+            low, high = jnp.minimum(low, total), jnp.maximum(high, total)
+            col_fac[block, :] = 1.0 / total
+        return (low, high, tuple(rows))
+
+    ones = jnp.ones(tile, jnp.float32)
+    low, high, rows = lax.fori_loop(1, SWEEPS, sweep, (ones, ones, (ones, ones)))
+    near = (jnp.min(low) >= 1.0 / DRIFT) & (jnp.max(high) <= DRIFT)
 
     @pl.when(near)
     def _():
-        kern[...] = kern[...] * col_fac[...]
+        factor = col_fac[...]
+        row_pot[...] += jnp.log2(jnp.concatenate([row[:1] for row in rows], axis=1))
+        col_pot[...] += jnp.log2(factor[:, :1])
+        kern[...] *= jnp.concatenate([factor, factor], axis=1)
 
     @pl.when(jnp.logical_not(near))
     def _():
-        scaled = bias[...] + (col_base[...] + jnp.log2(col_fac[...]))
+        col_pot[...] = jnp.zeros_like(col_pot)
+
+        def again(step, carry):
+            log_sweep()
+            return carry
+
+        lax.fori_loop(0, SWEEPS, again, 0)
+
+    near = jnp.min(jnp.sum(kern[...], axis=0, keepdims=True)) >= 1.0 / DRIFT
+
+    @pl.when(jnp.logical_not(near))
+    def _():
+        scaled = bias[...] + col_pot[...]
         kern[...] = jnp.exp2(scaled - jnp.max(scaled, axis=0, keepdims=True))
 
     scaled = kern[...]
@@ -147,8 +162,8 @@
         weights, data_ref[...], (((0,), (0,)), ((), ())), preferred_element_type=jnp.float32
     )
     out_ref[...] = moved.astype(jnp.bfloat16).reshape(out_ref.shape)
-    pots_ref[0:1, :] = (row_base[...] + jnp.log2(row_fac[...])) * BIT
-    pots_ref[1:2, :] = jnp.transpose((col_base[...] + jnp.log2(col_fac[...])) * BIT)
+    pots_ref[0:1, :] = row_pot[...] * BIT
+    pots_ref[1:2, :] = jnp.transpose(col_pot[...] * BIT)
 
 
 def on_device(noise, data):
@@ -197,8 +212,7 @@
             pltpu.VMEM((BATCH, BATCH), jnp.float32),
             pltpu.VMEM((1, BATCH), jnp.float32),
             pltpu.VMEM((BATCH, 1), jnp.float32),
-            pltpu.VMEM((1, BATCH), jnp.float32),
-            pltpu.VMEM((BATCH, 1), jnp.float32),
+            pltpu.VMEM((BATCH, LANES), jnp.float32),
         ],
         compiler_params=params,
     )(total, data_ent)

time: 119 us -> 116 us (0.975)
  Pallas kernels: 9.93 us -> 7.08 us
    pallas_call x1, Pallas kernels: 6.95 us -> 4.11 us  [on_device(): pl.pallas_call(sweep_kernel, out_shape=(jax.ShapeDtypeStruct((devices, ow...]
where the time goes in v5:
time: 116 us
  blocking collectives  77.4 us (67%)
  waiting for transfers between devices  18.1 us (16%)
  Pallas kernels  7.08 us (6%)
  starting transfers between devices  4.63 us (4%)
  local copies, waits for them, and re-layouts  4.27 us (4%)
  other arithmetic  3.33 us (3%)
    all_to_all x1, blocking collectives, on_device(): both = lax.all_to_all(both, AXES, split_axis=0, concat_axis=0)  47 us
    all_to_all x1, waiting for transfers between devices, on_device(): moved = lax.all_to_all(moved, AXES, split_axis=0, concat_axis=0)  18.1 us
    all_to_all x1, blocking collectives, on_device(): total = lax.all_to_all(total, AXES, split_axis=0, concat_axis=0)  15.2 us
    all_to_all x1, blocking collectives, on_device(): parts = lax.all_to_all(parts, AXES, split_axis=0, concat_axis=0)  15.2 us
    all_to_all x1, starting transfers between devices, on_device(): moved = lax.all_to_all(moved, AXES, split_axis=0, concat_axis=0)  4.63 us
    pallas_call x1, Pallas kernels, on_device(): pl.pallas_call(sweep_kernel, out_shape=(jax.ShapeDtypeStruct((devices, ow...  4.11 us
    unnamed x8, local copies, waits for them, and re-layouts  3.68 us
    reduce_sum x1, other arithmetic, on_device(): noise_sq = jnp.sum(wide * wide, axis=1)  2.82 us
  transfers between devices with their start and end apart: 1, of which 1 were waited for; matrix products, arithmetic and copies ran while one was open for 3% of the time, Pallas kernels for 0%

profile of v5, /device:TPU:1, one launch (start us, length us, event | category | flops | bytes accessed | tf_op | source)
XLA Modules:
  0.0 115.5 jit_solution(11032001232649077055)
XLA Ops:
  0.6 0.0 copy-start
  0.6 1.3 %copy-done = bf16[2,324480]{1,0:T(2,128)(2,1)S(1)} copy-done((bf16[2,324480]{1,0:T(2,128)(2,1)S(1)}, bf16[2,324480]{1,0:T(2,128)(2,1)}, u32[]{:S(2)}) %copy-start) | copy-done | bytes 1297944
  1.9 0.0 copy-start.3
  1.9 1.3 %copy-done.3 = bf16[2,324480]{1,0:T(2,128)(2,1)S(1)} copy-done((bf16[2,324480]{1,0:T(2,128)(2,1)S(1)}, bf16[2,324480]{1,0:T(2,128)(2,1)}, u32[]{:S(2)}) %copy-start.3) | copy-done | bytes 1297944
  3.3 0.5 shard_map.49
  3.8 47.0 %all_to_all.20.both_ref = bf16[128,2,5120]{2,1,0:T(2,128)(2,1)S(1)} all-to-all(bf16[128,2,5120]{2,1,0:T(2,128)(2,1)S(1)} %bitcast.19), channel_id=1, replica_groups=mesh['dp'=16,'dim'=8] {'dp','dim'}, dimensions={0} | all-to-all | bytes 5242880 | tf_op jit(solution)/shard_map/all_to_all | solution.py:192
  50.8 1.2 %shard_map.50 = (f32[128,4,128]{2,1,0:T(4,128)S(1)}, bf16[256,2560]{1,0:T(8,128)(2,1)S(1)}) custom-call(bf16[128,2,5120]{2,1,0:T(2,128)(2,1)S(1)} %all_to_all.20.both_ref), custom_call_target="tpu_custom_call" | custom-call | tf_op jit(solution)/shard_map/pallas_call | solution.py:195
  52.0 15.2 %all_to_all.21.parts_ref = f32[128,4,128]{2,1,0:T(4,128)S(1)} all-to-all(f32[128,4,128]{2,1,0:T(4,128)S(1)} %get-tuple-element.7), channel_id=1, replica_groups=mesh['dp'=16,'dim'=8] {'dp','dim'}, dimensions={0} | all-to-all | bytes 524288 | tf_op jit(solution)/shard_map/all_to_all | solution.py:200
  67.2 0.2 shard_map.51
  67.4 15.2 %all_to_all.22.cost_ref = f32[128,4,128]{2,1,0:T(4,128)S(1)} all-to-all(f32[128,4,128]{2,1,0:T(4,128)S(1)} %shard_map.51), channel_id=1, replica_groups=mesh['dp'=16,'dim'=8] {'dp','dim'}, dimensions={0} | all-to-all | bytes 524288 | tf_op jit(solution)/shard_map/all_to_all | solution.py:202
  82.6 4.1 %shard_map.52 = (bf16[128,2,2560]{2,1,0:T(2,128)(2,1)S(1)}, f32[2,256]{1,0:T(2,128)S(1)}) custom-call(f32[128,4,128]{2,1,0:T(4,128)S(1)} %all_to_all.22.cost_ref, bf16[256,2560]{1,0:T(8,128)(2,1)S(1)} %get-tuple-element.8.data_ref), custom_call_target="tpu_custom_call" | custom-call | tf_op jit(solution)/shard_map/pallas_call | solution.py:204
  86.7 0.0 copy-start.2
  86.7 1.1 copy-done.2
  87.8 0.0 copy-start.1
  87.8 4.6 %all-to-all-start.3 = ((bf16[128,2,2560]{2,1,0:T(2,128)(2,1)}), bf16[128,2,2560]{2,1,0:T(2,128)(2,1)S(1)}, u32[]{:S(2)}, u32[]{:S(2)}) async-start(bf16[128,2,2560]{2,1,0:T(2,128)(2,1)} %copy-done.2), calls=%async_computation.3 | async-start | bytes 2621440 | tf_op jit(solution)/shard_map/all_to_all | solution.py:219
  92.4 0.0 copy-done.1
  92.4 2.8 %multiply_reduce_fusion = f32[2]{0:T(128)S(1)} fusion(bf16[2,324480]{1,0:T(2,128)(2,1)S(1)} %copy-done.1), kind=kLoop, calls=%fused_computation | loop fusion | flops 1946878 | bytes 1297928 | tf_op jit(solution)/shard_map/reduce_sum | solution.py:234
  95.2 0.1 constant_dynamic-slice_fusion
  95.3 0.5 slice_bitcast_fusion
  95.8 0.5 bitcast_add_fusion
  96.4 18.1 %all-to-all-done.3 = bf16[128,2,2560]{2,1,0:T(2,128)(2,1)S(1)} async-done(((bf16[128,2,2560]{2,1,0:T(2,128)(2,1)}), bf16[128,2,2560]{2,1,0:T(2,128)(2,1)S(1)}, u32[]{:S(2)}, u32[]{:S(2)}) %all-to-all-start.3) | async-done | bytes 1310752 | tf_op jit(solution)/shard_map/all_to_all | solution.py:219
  114.5 1.1 shard_map.53
Async XLA Ops:
  0.6 1.3 %copy-start = (bf16[2,324480]{1,0:T(2,128)(2,1)S(1)}, bf16[2,324480]{1,0:T(2,128)(2,1)}, u32[]{:S(2)}) copy-start(bf16[2,324480]{1,0:T(2,128)(2,1)} %param.2) | copy-start | bytes 3893764
  1.9 1.3 %copy-start.3 = (bf16[2,324480]{1,0:T(2,128)(2,1)S(1)}, bf16[2,324480]{1,0:T(2,128)(2,1)}, u32[]{:S(2)}) copy-start(bf16[2,324480]{1,0:T(2,128)(2,1)} %param.3) | copy-start | bytes 3893764
  86.7 1.1 copy-start.2
  87.8 4.6 %copy-start.1 = (bf16[2,324480]{1,0:T(2,128)(2,1)S(1)}, bf16[2,324480]{1,0:T(2,128)(2,1)}, u32[]{:S(2)}) copy-start(bf16[2,324480]{1,0:T(2,128)(2,1)} %param.2) | copy-start | bytes 3893764
  87.8 26.7 %all-to-all-start.3 = ((bf16[128,2,2560]{2,1,0:T(2,128)(2,1)}), bf16[128,2,2560]{2,1,0:T(2,128)(2,1)S(1)}, u32[]{:S(2)}, u32[]{:S(2)}) async-start(bf16[128,2,2560]{2,1,0:T(2,128)(2,1)} %copy-done.2), calls=%async_computation.3 | async-start | bytes 2621440 | tf_op jit(solution)/shard_map/all_to_all | solution.py:219

commit v6 on v5

--- a/solution.py
+++ b/solution.py
@@ -39,7 +39,20 @@
         copy.wait()
 
 
-def unpack_kernel(moved_ref, out_ref, sems):
+def square_kernel(noise_ref, after_ref, out_ref):
+    units = noise_ref.shape[1] // UNIT
+
+    def add(n, total):
+        unit = noise_ref[:, pl.ds(pl.multiple_of(n * UNIT, UNIT), UNIT)].astype(jnp.float32)
+        return total + unit * unit
+
+    total = jnp.zeros((noise_ref.shape[0], UNIT), jnp.float32)
+    total = lax.fori_loop(0, units, add, total, unroll=13)
+    total = jnp.sum(total, axis=1, keepdims=True)
+    out_ref[...] = jnp.broadcast_to(total, out_ref.shape)
+
+
+def unpack_kernel(moved_ref, pots_ref, noise_sq_ref, out_ref, row_ref, col_ref, sems):
     devices, units = moved_ref.shape[0], out_ref.shape[0]
     copies = []
     for q in range(UNITS):
@@ -52,6 +65,14 @@
         )
     for copy in copies:
         copy.start()
+    own = out_ref.shape[1]
+    first = (lax.axis_index("dp") * lax.axis_size("dim") + lax.axis_index("dim")) * own
+    lane = lax.broadcasted_iota(jnp.int32, (1, BATCH), 1)
+    for n in range(own):
+        mine = lane == first + n
+        row = jnp.sum(jnp.where(mine, pots_ref[0:1, :], 0.0))
+        row_ref[n] = row + jnp.max(noise_sq_ref[n : n + 1, :]) / LATENT
+        col_ref[n] = jnp.sum(jnp.where(mine, pots_ref[1:2, :], 0.0))
     for copy in copies:
         copy.wait()
 
@@ -82,7 +103,7 @@
     pieces_of(data_sq - 2.0 * gram, out_ref)
 
 
-def sum_kernel(parts_ref, out_ref):
+def sum_kernel(parts_ref, before_ref, out_ref):
     total = jnp.sum(parts_ref[...], axis=0)
     out_ref[...] = jnp.broadcast_to(total[None], out_ref.shape)
 
@@ -180,14 +201,14 @@
     both = pl.pallas_call(
         pack_kernel,
         out_shape=jax.ShapeDtypeStruct((devices, 2 * UNITS, own, UNIT), noise.dtype),
-        in_specs=[anywhere, anywhere],
+        in_specs=[pl.BlockSpec(memory_space=pltpu.HBM)] * 2,
         out_specs=anywhere,
         scratch_shapes=[
             pltpu.VMEM((UNITS * devices - units, own, UNIT), noise.dtype),
             pltpu.SemaphoreType.DMA((4 * UNITS,)),
         ],
         compiler_params=params,
-    )(units_of(noise), units_of(data))
+    )(*[pltpu.with_memory_space_constraint(units_of(rows), pltpu.HBM) for rows in (noise, data)])
     both = both.transpose(0, 2, 1, 3).reshape(devices, own, 2 * ent)
     both = lax.all_to_all(both, AXES, split_axis=0, concat_axis=0)
 
@@ -197,8 +218,22 @@
         out_shape=(pieces, jax.ShapeDtypeStruct((BATCH, ent), data.dtype)),
         compiler_params=params,
     )(both)
+    whole = pl.BlockSpec(memory_space=pltpu.VMEM)
+    noise_sq = pl.pallas_call(
+        square_kernel,
+        out_shape=jax.ShapeDtypeStruct((own, LANES), jnp.float32),
+        in_specs=[whole, anywhere],
+        out_specs=whole,
+        compiler_params=params,
+    )(noise, parts)
     parts = lax.all_to_all(parts, AXES, split_axis=0, concat_axis=0)
-    total = pl.pallas_call(sum_kernel, out_shape=pieces, compiler_params=params)(parts)
+    total = pl.pallas_call(
+        sum_kernel,
+        out_shape=pieces,
+        in_specs=[whole, anywhere],
+        out_specs=whole,
+        compiler_params=params,
+    )(parts, noise_sq)
     total = lax.all_to_all(total, AXES, split_axis=0, concat_axis=0)
 
     moved, pots = pl.pallas_call(
@@ -218,21 +253,20 @@
     )(total, data_ent)
     moved = lax.all_to_all(moved, AXES, split_axis=0, concat_axis=0)
     moved = moved.reshape(devices, own, UNITS, UNIT).transpose(0, 2, 1, 3)
-    targets = pl.pallas_call(
+    scalars = pl.BlockSpec(memory_space=pltpu.SMEM)
+    targets, row, col = pl.pallas_call(
         unpack_kernel,
-        out_shape=jax.ShapeDtypeStruct((units, own, UNIT), moved.dtype),
-        in_specs=[anywhere],
-        out_specs=anywhere,
+        out_shape=(
+            jax.ShapeDtypeStruct((units, own, UNIT), moved.dtype),
+            jax.ShapeDtypeStruct((own,), jnp.float32),
+            jax.ShapeDtypeStruct((own,), jnp.float32),
+        ),
+        in_specs=[anywhere, whole, whole],
+        out_specs=(anywhere, scalars, scalars),
         scratch_shapes=[pltpu.SemaphoreType.DMA((UNITS,))],
         compiler_params=params,
-    )(moved)
-    targets = targets.transpose(1, 0, 2).reshape(own, LATENT)
-
-    offset = lax.axis_index(AXES) * own
-    mine = lax.dynamic_slice_in_dim(pots, offset, own, 1)
-    wide = noise.astype(jnp.float32)
-    noise_sq = jnp.sum(wide * wide, axis=1)
-    return (targets, mine[0] + noise_sq / LATENT, mine[1])
+    )(moved, pots, noise_sq)
+    return (targets.transpose(1, 0, 2).reshape(own, LATENT), row, col)
 
 
 def solution(mesh):

time: 116 us -> 115 us (level)
  blocking collectives: 77.4 us -> 88.5 us
  waiting for transfers between devices: 18.1 us -> 10.2 us
  local copies, waits for them, and re-layouts: 4.27 us -> 0.01 us
  other arithmetic: 3.33 us -> 0 us
  Pallas kernels: 7.08 us -> 10.4 us
    all_to_all x1, blocking collectives: 15.2 us -> 26.2 us  [on_device(): moved = lax.all_to_all(moved, AXES, split_axis=0, concat_axis=0)]
    all_to_all x1, waiting for transfers between devices: 18.1 us -> 10.2 us  [on_device(): parts = lax.all_to_all(parts, AXES, split_axis=0, concat_axis=0)]
    unnamed x8 -> x2, local copies, waits for them, and re-layouts: 3.68 us -> 0.01 us
    reduce_sum x1 -> x0, other arithmetic: 2.82 us -> none  [on_device(): noise_sq = jnp.sum(wide * wide, axis=1)]
    pallas_call x2 -> x3, Pallas kernels: 1.25 us -> 2.6 us  [the longest x1 1.61 us: on_device(): pl.pallas_call(unpack_kernel, out_shape=(jax.ShapeDtypeStruct((units, own...]
    pallas_call x1, Pallas kernels: 0.52 us -> 1.8 us  [on_device(): pl.pallas_call(pack_kernel, out_shape=jax.ShapeDtypeStruct((devices, 2 *...]
  transfers between devices with their start and end apart: 1 -> 1, of which waited for: 1 -> 1; matrix products, arithmetic and copies ran while one was open for 3% -> 0% of each run, Pallas kernels for 0% -> 1%
where the time goes in v6:
time: 115 us
  blocking collectives  88.5 us (77%)
  Pallas kernels  10.4 us (9%)
  waiting for transfers between devices  10.2 us (9%)
  starting transfers between devices  4.75 us (4%)
    all_to_all x1, blocking collectives, on_device(): both = lax.all_to_all(both, AXES, split_axis=0, concat_axis=0)  47 us
    all_to_all x1, blocking collectives, on_device(): moved = lax.all_to_all(moved, AXES, split_axis=0, concat_axis=0)  26.2 us
    all_to_all x1, blocking collectives, on_device(): total = lax.all_to_all(total, AXES, split_axis=0, concat_axis=0)  15.3 us
    all_to_all x1, waiting for transfers between devices, on_device(): parts = lax.all_to_all(parts, AXES, split_axis=0, concat_axis=0)  10.2 us
    all_to_all x1, starting transfers between devices, on_device(): parts = lax.all_to_all(parts, AXES, split_axis=0, concat_axis=0)  4.75 us
    pallas_call x1, Pallas kernels, on_device(): pl.pallas_call(sweep_kernel, out_shape=(jax.ShapeDtypeStruct((devices, ow...  4.12 us
  transfers between devices with their start and end apart: 1, of which 1 were waited for; matrix products, arithmetic and copies ran while one was open for 0% of the time, Pallas kernels for 1%

profile of v6, /device:TPU:1, one launch (start us, length us, event | category | flops | bytes accessed | tf_op | source)
XLA Modules:
  0.0 114.6 jit_solution(13143446763526039213)
XLA Ops:
  0.6 1.8 %shard_map.49 = bf16[128,8,2,640]{3,2,1,0:T(2,128)(2,1)S(1)} custom-call(bf16[507,2,640]{2,1,0:T(2,128)(2,1)} %bitcast.17, bf16[507,2,640]{2,1,0:T(2,128)(2,1)} %bitcast.18), custom_call_target="tpu_custom_call" | custom-call | tf_op jit(solution)/shard_map/pallas_call | solution.py:201
  2.4 47.0 %all_to_all.20.both_ref = bf16[128,2,5120]{2,1,0:T(2,128)(2,1)S(1)} all-to-all(bf16[128,2,5120]{2,1,0:T(2,128)(2,1)S(1)} %bitcast.15), channel_id=1, replica_groups=mesh['dp'=16,'dim'=8] {'dp','dim'}, dimensions={0} | all-to-all | bytes 5242880 | tf_op jit(solution)/shard_map/all_to_all | solution.py:213
  49.5 0.0 copy-start
  49.5 1.9 %shard_map.50 = (f32[128,4,128]{2,1,0:T(4,128)}, bf16[256,2560]{1,0:T(8,128)(2,1)S(1)}) custom-call(bf16[128,2,5120]{2,1,0:T(2,128)(2,1)S(1)} %all_to_all.20.both_ref), custom_call_target="tpu_custom_call" | custom-call | tf_op jit(solution)/shard_map/pallas_call | solution.py:216
  51.4 4.8 %all-to-all-start.1 = ((f32[128,4,128]{2,1,0:T(4,128)}), f32[128,4,128]{2,1,0:T(4,128)S(1)}, u32[]{:S(2)}, u32[]{:S(2)}) async-start(f32[128,4,128]{2,1,0:T(4,128)} %get-tuple-element.10.after_ref), calls=%async_computation.1 | async-start | bytes 524288 | tf_op jit(solution)/shard_map/all_to_all | solution.py:229
  56.2 0.0 copy-done
  56.2 0.8 shard_map.51.before_ref.noise_sq_ref
  57.0 10.2 %all-to-all-done.1.parts_ref = f32[128,4,128]{2,1,0:T(4,128)S(1)} async-done(((f32[128,4,128]{2,1,0:T(4,128)}), f32[128,4,128]{2,1,0:T(4,128)S(1)}, u32[]{:S(2)}, u32[]{:S(2)}) %all-to-all-start.1) | async-done | bytes 262176 | tf_op jit(solution)/shard_map/all_to_all | solution.py:229
  67.2 0.2 shard_map.52
  67.3 15.3 %all_to_all.21.cost_ref = f32[128,4,128]{2,1,0:T(4,128)S(1)} all-to-all(f32[128,4,128]{2,1,0:T(4,128)S(1)} %shard_map.52), channel_id=1, replica_groups=mesh['dp'=16,'dim'=8] {'dp','dim'}, dimensions={0} | all-to-all | bytes 524288 | tf_op jit(solution)/shard_map/all_to_all | solution.py:237
  82.6 4.1 %shard_map.53 = (bf16[128,2,2560]{2,1,0:T(2,128)(2,1)S(1)}, f32[2,256]{1,0:T(2,128)S(1)}) custom-call(f32[128,4,128]{2,1,0:T(4,128)S(1)} %all_to_all.21.cost_ref, bf16[256,2560]{1,0:T(8,128)(2,1)S(1)} %get-tuple-element.11.data_ref), custom_call_target="tpu_custom_call" | custom-call | tf_op jit(solution)/shard_map/pallas_call | solution.py:239
  86.7 26.2 %all_to_all.22 = bf16[128,2,2560]{2,1,0:T(2,128)(2,1)S(1)} all-to-all(bf16[128,2,2560]{2,1,0:T(2,128)(2,1)S(1)} %get-tuple-element.12), channel_id=1, replica_groups=mesh['dp'=16,'dim'=8] {'dp','dim'}, dimensions={0} | all-to-all | bytes 2621440 | tf_op jit(solution)/shard_map/all_to_all | solution.py:254
  113.0 1.6 %shard_map.54 = (bf16[507,2,640]{2,1,0:T(2,128)(2,1)}, f32[2]{0:T(128)}, f32[2]{0:T(128)}) custom-call(bf16[128,4,2,640]{3,2,1,0:T(2,128)(2,1)S(1)} %bitcast.16, f32[2,256]{1,0:T(2,128)S(1)} %get-tuple-element.13.pots_ref, f32[2,128]{1,0:T(2,128)S(1)} %shard_map.51.before_ref.noise_sq_ref), custom_call_target="tpu_custom_call" | custom-call | tf_op jit(solution)/shard_map/pallas_call | solution.py:257
Async XLA Ops:
  49.5 6.7 %copy-start = (bf16[2,324480]{1,0:T(2,128)(2,1)S(1)}, bf16[2,324480]{1,0:T(2,128)(2,1)}, u32[]{:S(2)}) copy-start(bf16[2,324480]{1,0:T(2,128)(2,1)} %noise_ref.1) | copy-start | bytes 3893764
  51.4 15.8 %all-to-all-start.1 = ((f32[128,4,128]{2,1,0:T(4,128)}), f32[128,4,128]{2,1,0:T(4,128)S(1)}, u32[]{:S(2)}, u32[]{:S(2)}) async-start(f32[128,4,128]{2,1,0:T(4,128)} %get-tuple-element.10.after_ref), calls=%async_computation.1 | async-start | bytes 524288 | tf_op jit(solution)/shard_map/all_to_all | solution.py:229

commit v7 on v5

--- a/solution.py
+++ b/solution.py
@@ -39,18 +39,34 @@
         copy.wait()
 
 
-def unpack_kernel(moved_ref, out_ref, sems):
+def unpack_kernel(moved_ref, pots_ref, noise_ref, out_ref, row_ref, col_ref, row, col, sems):
     devices, units = moved_ref.shape[0], out_ref.shape[0]
+    own = out_ref.shape[1]
     copies = []
     for q in range(UNITS):
         start = q * devices
         count = min(devices, units - start)
-        copies.append(
-            pltpu.make_async_copy(
-                moved_ref.at[pl.ds(0, count), q], out_ref.at[pl.ds(start, count)], sems.at[q]
-            )
-        )
-    for copy in copies:
+        copies.append((moved_ref.at[pl.ds(0, count), q], out_ref.at[pl.ds(start, count)]))
+    copies.extend([(row, row_ref), (col, col_ref)])
+    copies = [pltpu.make_async_copy(src, dst, sems.at[n]) for n, (src, dst) in enumerate(copies)]
+    for copy in copies[:UNITS]:
+        copy.start()
+
+    def add(n, total):
+        unit = noise_ref[:, pl.ds(pl.multiple_of(n * UNIT, UNIT), UNIT)].astype(jnp.float32)
+        return total + unit * unit
+
+    noise_sq = jnp.zeros((own, UNIT), jnp.float32)
+    noise_sq = lax.fori_loop(0, units, add, noise_sq, unroll=13)
+    noise_sq = jnp.sum(noise_sq, axis=1, keepdims=True)
+    first = (lax.axis_index("dp") * lax.axis_size("dim") + lax.axis_index("dim")) * own
+    lane = lax.broadcasted_iota(jnp.int32, (1, BATCH), 1)
+    for n in range(own):
+        mine = lane == first + n
+        row_pot = jnp.sum(jnp.where(mine, pots_ref[0:1, :], 0.0))
+        row[n] = row_pot + jnp.sum(noise_sq[n : n + 1, :]) / LATENT
+        col[n] = jnp.sum(jnp.where(mine, pots_ref[1:2, :], 0.0))
+    for copy in copies[UNITS:]:
         copy.start()
     for copy in copies:
         copy.wait()
@@ -180,14 +196,14 @@
     both = pl.pallas_call(
         pack_kernel,
         out_shape=jax.ShapeDtypeStruct((devices, 2 * UNITS, own, UNIT), noise.dtype),
-        in_specs=[anywhere, anywhere],
+        in_specs=[pl.BlockSpec(memory_space=pltpu.HBM)] * 2,
         out_specs=anywhere,
         scratch_shapes=[
             pltpu.VMEM((UNITS * devices - units, own, UNIT), noise.dtype),
             pltpu.SemaphoreType.DMA((4 * UNITS,)),
         ],
         compiler_params=params,
-    )(units_of(noise), units_of(data))
+    )(*[pltpu.with_memory_space_constraint(units_of(rows), pltpu.HBM) for rows in (noise, data)])
     both = both.transpose(0, 2, 1, 3).reshape(devices, own, 2 * ent)
     both = lax.all_to_all(both, AXES, split_axis=0, concat_axis=0)
 
@@ -218,21 +234,24 @@
     )(total, data_ent)
     moved = lax.all_to_all(moved, AXES, split_axis=0, concat_axis=0)
     moved = moved.reshape(devices, own, UNITS, UNIT).transpose(0, 2, 1, 3)
-    targets = pl.pallas_call(
+    whole = pl.BlockSpec(memory_space=pltpu.VMEM)
+    targets, row, col = pl.pallas_call(
         unpack_kernel,
-        out_shape=jax.ShapeDtypeStruct((units, own, UNIT), moved.dtype),
-        in_specs=[anywhere],
-        out_specs=anywhere,
-        scratch_shapes=[pltpu.SemaphoreType.DMA((UNITS,))],
-        compiler_params=params,
-    )(moved)
-    targets = targets.transpose(1, 0, 2).reshape(own, LATENT)
-
-    offset = lax.axis_index(AXES) * own
-    mine = lax.dynamic_slice_in_dim(pots, offset, own, 1)
-    wide = noise.astype(jnp.float32)
-    noise_sq = jnp.sum(wide * wide, axis=1)
-    return (targets, mine[0] + noise_sq / LATENT, mine[1])
+        out_shape=(
+            jax.ShapeDtypeStruct((units, own, UNIT), moved.dtype),
+            jax.ShapeDtypeStruct((own,), jnp.float32),
+            jax.ShapeDtypeStruct((own,), jnp.float32),
+        ),
+        in_specs=[anywhere, whole, whole],
+        out_specs=(anywhere, anywhere, anywhere),
+        scratch_shapes=[
+            pltpu.SMEM((own,), jnp.float32),
+            pltpu.SMEM((own,), jnp.float32),
+            pltpu.SemaphoreType.DMA((UNITS + 2,)),
+        ],
+        compiler_params=params,
+    )(moved, pots, noise)
+    return (targets.transpose(1, 0, 2).reshape(own, LATENT), row, col)
 
 
 def solution(mesh):

time: 116 us -> 113 us (0.974)
  blocking collectives: 77.4 us -> 104 us
  waiting for transfers between devices: 18.1 us -> 0 us
  starting transfers between devices: 4.63 us -> 0 us
  local copies, waits for them, and re-layouts: 4.27 us -> 0.01 us
  other arithmetic: 3.33 us -> 0 us
  Pallas kernels: 7.08 us -> 8.78 us
    all_to_all x0 -> x1, blocking collectives: none -> 26.2 us  [on_device(): moved = lax.all_to_all(moved, AXES, split_axis=0, concat_axis=0)]
    all_to_all x1 -> x0, waiting for transfers between devices: 18.1 us -> none  [on_device(): moved = lax.all_to_all(moved, AXES, split_axis=0, concat_axis=0)]
    all_to_all x1 -> x0, starting transfers between devices: 4.63 us -> none  [on_device(): moved = lax.all_to_all(moved, AXES, split_axis=0, concat_axis=0)]
    unnamed x8 -> x2, local copies, waits for them, and re-layouts: 3.68 us -> 0.01 us
    reduce_sum x1 -> x0, other arithmetic: 2.82 us -> none  [on_device(): noise_sq = jnp.sum(wide * wide, axis=1)]
    pallas_call x1, Pallas kernels: 0.52 us -> 1.8 us  [on_device(): pl.pallas_call(pack_kernel, out_shape=jax.ShapeDtypeStruct((devices, 2 *...]
  transfers between devices with their start and end apart: 1 -> 0, of which waited for: 1 -> 0; matrix products, arithmetic and copies ran while one was open for 3% -> 0% of each run, Pallas kernels for 0% -> 0%
where the time goes in v7:
time: 113 us
  blocking collectives  104 us (92%)
  Pallas kernels  8.78 us (8%)
    all_to_all x1, blocking collectives, on_device(): both = lax.all_to_all(both, AXES, split_axis=0, concat_axis=0)  47 us
    all_to_all x1, blocking collectives, on_device(): moved = lax.all_to_all(moved, AXES, split_axis=0, concat_axis=0)  26.2 us
    all_to_all x1, blocking collectives, on_device(): total = lax.all_to_all(total, AXES, split_axis=0, concat_axis=0)  15.2 us
    all_to_all x1, blocking collectives, on_device(): parts = lax.all_to_all(parts, AXES, split_axis=0, concat_axis=0)  15.2 us
    pallas_call x1, Pallas kernels, on_device(): pl.pallas_call(sweep_kernel, out_shape=(jax.ShapeDtypeStruct((devices, ow...  4.12 us

profile of v7, /device:TPU:1, one launch (start us, length us, event | category | flops | bytes accessed | tf_op | source)
XLA Modules:
  0.0 113.1 jit_solution(2328990215015482375)
XLA Ops:
  0.6 1.8 %shard_map.49 = bf16[128,8,2,640]{3,2,1,0:T(2,128)(2,1)S(1)} custom-call(bf16[507,2,640]{2,1,0:T(2,128)(2,1)} %bitcast.17, bf16[507,2,640]{2,1,0:T(2,128)(2,1)} %bitcast.18), custom_call_target="tpu_custom_call" | custom-call | tf_op jit(solution)/shard_map/pallas_call | solution.py:196
  2.4 47.0 %all_to_all.20.both_ref = bf16[128,2,5120]{2,1,0:T(2,128)(2,1)S(1)} all-to-all(bf16[128,2,5120]{2,1,0:T(2,128)(2,1)S(1)} %bitcast.15), channel_id=1, replica_groups=mesh['dp'=16,'dim'=8] {'dp','dim'}, dimensions={0} | all-to-all | bytes 5242880 | tf_op jit(solution)/shard_map/all_to_all | solution.py:208
  49.5 1.2 %shard_map.50 = (f32[128,4,128]{2,1,0:T(4,128)S(1)}, bf16[256,2560]{1,0:T(8,128)(2,1)S(1)}) custom-call(bf16[128,2,5120]{2,1,0:T(2,128)(2,1)S(1)} %all_to_all.20.both_ref), custom_call_target="tpu_custom_call" | custom-call | tf_op jit(solution)/shard_map/pallas_call | solution.py:211
  50.7 15.2 %all_to_all.21.parts_ref = f32[128,4,128]{2,1,0:T(4,128)S(1)} all-to-all(f32[128,4,128]{2,1,0:T(4,128)S(1)} %get-tuple-element.10), channel_id=1, replica_groups=mesh['dp'=16,'dim'=8] {'dp','dim'}, dimensions={0} | all-to-all | bytes 524288 | tf_op jit(solution)/shard_map/all_to_all | solution.py:216
  65.8 0.2 shard_map.51
  66.0 15.2 %all_to_all.22.cost_ref = f32[128,4,128]{2,1,0:T(4,128)S(1)} all-to-all(f32[128,4,128]{2,1,0:T(4,128)S(1)} %shard_map.51), channel_id=1, replica_groups=mesh['dp'=16,'dim'=8] {'dp','dim'}, dimensions={0} | all-to-all | bytes 524288 | tf_op jit(solution)/shard_map/all_to_all | solution.py:218
  81.2 4.1 %shard_map.52 = (bf16[128,2,2560]{2,1,0:T(2,128)(2,1)S(1)}, f32[2,256]{1,0:T(2,128)S(1)}) custom-call(f32[128,4,128]{2,1,0:T(4,128)S(1)} %all_to_all.22.cost_ref, bf16[256,2560]{1,0:T(8,128)(2,1)S(1)} %get-tuple-element.11.data_ref), custom_call_target="tpu_custom_call" | custom-call | tf_op jit(solution)/shard_map/pallas_call | solution.py:220
  85.4 0.0 copy-start
  85.4 26.2 %all_to_all.23 = bf16[128,2,2560]{2,1,0:T(2,128)(2,1)S(1)} all-to-all(bf16[128,2,2560]{2,1,0:T(2,128)(2,1)S(1)} %get-tuple-element.12), channel_id=1, replica_groups=mesh['dp'=16,'dim'=8] {'dp','dim'}, dimensions={0} | all-to-all | bytes 2621440 | tf_op jit(solution)/shard_map/all_to_all | solution.py:235
  111.6 0.0 copy-done
  111.6 1.5 %shard_map.53 = (bf16[507,2,640]{2,1,0:T(2,128)(2,1)}, f32[2]{0:T(128)}, f32[2]{0:T(128)}) custom-call(bf16[128,4,2,640]{3,2,1,0:T(2,128)(2,1)S(1)} %bitcast.16, f32[2,256]{1,0:T(2,128)S(1)} %get-tuple-element.13.pots_ref, bf16[2,324480]{1,0:T(2,128)(2,1)S(1)} %copy-done), custom_call_target="tpu_custom_call" | custom-call | tf_op jit(solution)/shard_map/pallas_call | solution.py:238
Async XLA Ops:
  85.4 26.2 %copy-start = (bf16[2,324480]{1,0:T(2,128)(2,1)S(1)}, bf16[2,324480]{1,0:T(2,128)(2,1)}, u32[]{:S(2)}) copy-start(bf16[2,324480]{1,0:T(2,128)(2,1)} %noise_ref.1) | copy-start | bytes 3893764

commit v8 on v7

--- a/solution.py
+++ b/solution.py
@@ -103,7 +103,7 @@
     out_ref[...] = jnp.broadcast_to(total[None], out_ref.shape)
 
 
-def sweep_kernel(cost_ref, data_ref, out_ref, pots_ref, bias, kern, row_pot, col_pot, col_fac):
+def sweep_kernel(cost_ref, data_ref, out_ref, pots_ref, bias, kern, row_pot, col_pot, row_sum):
     bias[...] = whole_of(cost_ref) * (-1.0 / (LATENT * BIT))
     col_pot[...] = jnp.zeros_like(col_pot)
 
@@ -113,47 +113,58 @@
         row = -(top + jnp.log2(jnp.sum(jnp.exp2(scaled - top), axis=0, keepdims=True)))
         scaled = bias[...] + row
         top = jnp.max(scaled, axis=1, keepdims=True)
-        col = -(top + jnp.log2(jnp.sum(jnp.exp2(scaled - top), axis=1, keepdims=True)))
+        scaled = jnp.exp2(scaled - top)
+        total = jnp.sum(scaled, axis=1, keepdims=True)
         row_pot[...] = row
-        col_pot[...] = col
-        kern[...] = jnp.exp2(scaled + col)
+        col_pot[...] = -(top + jnp.log2(total))
+        kern[...] = scaled * (1.0 / total)
 
     log_sweep()
-    col_fac[...] = jnp.ones_like(col_fac)
 
     tile = (8, LANES)
     blocks = [pl.ds(start, 8) for start in range(0, BATCH, 8)]
     halves = [pl.ds(start, LANES) for start in range(0, BATCH, LANES)]
 
-    def sweep(step, carry):
-        low, high, _ = carry
+    def over_columns(low, high, rows, use):
         sums = [[jnp.zeros(tile, jnp.float32) for _ in halves] for _ in range(2)]
         for n, block in enumerate(blocks):
-            factor = col_fac[block, :]
-            for h, half in enumerate(halves):
-                sums[n % 2][h] += kern[block, half] * factor
-        rows = []
+            parts = [kern[block, half] for half in halves]
+            if rows is not None:
+                total = sum(part * row for part, row in zip(parts, rows))
+                total = jnp.broadcast_to(jnp.sum(total, axis=1, keepdims=True), tile)
+                low, high = jnp.minimum(low, total), jnp.maximum(high, total)
+                factor = 1.0 / total
+                parts = [part * factor for part in parts]
+                if use is not None:
+                    use(block, factor, parts)
+            for h, part in enumerate(parts):
+                sums[n % 2][h] += part
+        totals = []
         for first, second in zip(*sums):
             total = jnp.broadcast_to(jnp.sum(first + second, axis=0, keepdims=True), tile)
-            low, high = jnp.minimum(low, total), jnp.maximum(high, total)
-            rows.append(1.0 / total)
-        for block in blocks:
-            total = sum(kern[block, half] * row for half, row in zip(halves, rows))
-            total = jnp.broadcast_to(jnp.sum(total, axis=1, keepdims=True), tile)
-            low, high = jnp.minimum(low, total), jnp.maximum(high, total)
-            col_fac[block, :] = 1.0 / total
-        return (low, high, tuple(rows))
+            low = jnp.minimum(low, total)
+            totals.append(total)
+        return low, high, totals
+
+    def sweep(step, carry):
+        low, high, rows = carry
+        low, high, totals = over_columns(low, high, rows, None)
+        for total in totals:
+            high = jnp.maximum(high, total)
+        return (low, high, tuple(1.0 / total for total in totals))
+
+    def finish(block, factor, parts):
+        col_pot[block, :] += jnp.log2(factor[:, :1])
+        for half, part in zip(halves, parts):
+            kern[block, half] = part
 
     ones = jnp.ones(tile, jnp.float32)
-    low, high, rows = lax.fori_loop(1, SWEEPS, sweep, (ones, ones, (ones, ones)))
-    near = (jnp.min(low) >= 1.0 / DRIFT) & (jnp.max(high) <= DRIFT)
-
-    @pl.when(near)
-    def _():
-        factor = col_fac[...]
-        row_pot[...] += jnp.log2(jnp.concatenate([row[:1] for row in rows], axis=1))
-        col_pot[...] += jnp.log2(factor[:, :1])
-        kern[...] *= jnp.concatenate([factor, factor], axis=1)
+    carry = sweep(0, (ones, ones, None))
+    low, high, rows = lax.fori_loop(2, SWEEPS, sweep, carry)
+    low, high, totals = over_columns(low, high, rows, finish)
+    row_pot[...] += jnp.log2(jnp.concatenate([row[:1] for row in rows], axis=1))
+    row_sum[...] = jnp.concatenate([total[:1] for total in totals], axis=1)
+    near = jnp.min(jnp.where((low >= 1.0 / DRIFT) & (high <= DRIFT), 1.0, 0.0)) > 0.5
 
     @pl.when(jnp.logical_not(near))
     def _():
@@ -164,16 +175,12 @@
             return carry
 
         lax.fori_loop(0, SWEEPS, again, 0)
-
-    near = jnp.min(jnp.sum(kern[...], axis=0, keepdims=True)) >= 1.0 / DRIFT
-
-    @pl.when(jnp.logical_not(near))
-    def _():
         scaled = bias[...] + col_pot[...]
-        kern[...] = jnp.exp2(scaled - jnp.max(scaled, axis=0, keepdims=True))
-
-    scaled = kern[...]
-    weights = (scaled / jnp.sum(scaled, axis=0, keepdims=True)).astype(jnp.bfloat16)
+        scaled = jnp.exp2(scaled - jnp.max(scaled, axis=0, keepdims=True))
+        kern[...] = scaled
+        row_sum[...] = jnp.sum(scaled, axis=0, keepdims=True)
+
+    weights = (kern[...] * (1.0 / row_sum[...])).astype(jnp.bfloat16)
     moved = lax.dot_general(
         weights, data_ref[...], (((0,), (0,)), ((), ())), preferred_element_type=jnp.float32
     )
@@ -228,7 +235,7 @@
             pltpu.VMEM((BATCH, BATCH), jnp.float32),
             pltpu.VMEM((1, BATCH), jnp.float32),
             pltpu.VMEM((BATCH, 1), jnp.float32),
-            pltpu.VMEM((BATCH, LANES), jnp.float32),
+            pltpu.VMEM((1, BATCH), jnp.float32),
         ],
         compiler_params=params,
     )(total, data_ent)

time: 113 us -> 113 us (level)
  no operation moved by 1% of the time
where the time goes in v8:
time: 113 us
  blocking collectives  104 us (92%)
  Pallas kernels  8.25 us (7%)
    all_to_all x1, blocking collectives, on_device(): both = lax.all_to_all(both, AXES, split_axis=0, concat_axis=0)  47 us
    all_to_all x1, blocking collectives, on_device(): moved = lax.all_to_all(moved, AXES, split_axis=0, concat_axis=0)  26.2 us
    all_to_all x1, blocking collectives, on_device(): total = lax.all_to_all(total, AXES, split_axis=0, concat_axis=0)  15.2 us
    all_to_all x1, blocking collectives, on_device(): parts = lax.all_to_all(parts, AXES, split_axis=0, concat_axis=0)  15.2 us
    pallas_call x1, Pallas kernels, on_device(): pl.pallas_call(sweep_kernel, out_shape=(jax.ShapeDtypeStruct((devices, ow...  3.58 us

profile of v8, /device:TPU:1, one launch (start us, length us, event | category | flops | bytes accessed | tf_op | source)
XLA Modules:
  0.0 112.5 jit_solution(11651604161428631616)
XLA Ops:
  0.6 1.8 %shard_map.49 = bf16[128,8,2,640]{3,2,1,0:T(2,128)(2,1)S(1)} custom-call(bf16[507,2,640]{2,1,0:T(2,128)(2,1)} %bitcast.17, bf16[507,2,640]{2,1,0:T(2,128)(2,1)} %bitcast.18), custom_call_target="tpu_custom_call" | custom-call | tf_op jit(solution)/shard_map/pallas_call | solution.py:203
  2.4 47.0 %all_to_all.20.both_ref = bf16[128,2,5120]{2,1,0:T(2,128)(2,1)S(1)} all-to-all(bf16[128,2,5120]{2,1,0:T(2,128)(2,1)S(1)} %bitcast.15), channel_id=1, replica_groups=mesh['dp'=16,'dim'=8] {'dp','dim'}, dimensions={0} | all-to-all | bytes 5242880 | tf_op jit(solution)/shard_map/all_to_all | solution.py:215
  49.5 1.2 %shard_map.50 = (f32[128,4,128]{2,1,0:T(4,128)S(1)}, bf16[256,2560]{1,0:T(8,128)(2,1)S(1)}) custom-call(bf16[128,2,5120]{2,1,0:T(2,128)(2,1)S(1)} %all_to_all.20.both_ref), custom_call_target="tpu_custom_call" | custom-call | tf_op jit(solution)/shard_map/pallas_call | solution.py:218
  50.7 15.2 %all_to_all.21.parts_ref = f32[128,4,128]{2,1,0:T(4,128)S(1)} all-to-all(f32[128,4,128]{2,1,0:T(4,128)S(1)} %get-tuple-element.10), channel_id=1, replica_groups=mesh['dp'=16,'dim'=8] {'dp','dim'}, dimensions={0} | all-to-all | bytes 524288 | tf_op jit(solution)/shard_map/all_to_all | solution.py:223
  65.8 0.2 shard_map.51
  66.0 15.2 %all_to_all.22.cost_ref = f32[128,4,128]{2,1,0:T(4,128)S(1)} all-to-all(f32[128,4,128]{2,1,0:T(4,128)S(1)} %shard_map.51), channel_id=1, replica_groups=mesh['dp'=16,'dim'=8] {'dp','dim'}, dimensions={0} | all-to-all | bytes 524288 | tf_op jit(solution)/shard_map/all_to_all | solution.py:225
  81.2 3.6 %shard_map.52 = (bf16[128,2,2560]{2,1,0:T(2,128)(2,1)S(1)}, f32[2,256]{1,0:T(2,128)S(1)}) custom-call(f32[128,4,128]{2,1,0:T(4,128)S(1)} %all_to_all.22.cost_ref, bf16[256,2560]{1,0:T(8,128)(2,1)S(1)} %get-tuple-element.11.data_ref), custom_call_target="tpu_custom_call" | custom-call | tf_op jit(solution)/shard_map/pallas_call | solution.py:227
  84.8 0.0 copy-start
  84.8 26.2 %all_to_all.23 = bf16[128,2,2560]{2,1,0:T(2,128)(2,1)S(1)} all-to-all(bf16[128,2,2560]{2,1,0:T(2,128)(2,1)S(1)} %get-tuple-element.12), channel_id=1, replica_groups=mesh['dp'=16,'dim'=8] {'dp','dim'}, dimensions={0} | all-to-all | bytes 2621440 | tf_op jit(solution)/shard_map/all_to_all | solution.py:242
  111.1 0.0 copy-done
  111.1 1.5 %shard_map.53 = (bf16[507,2,640]{2,1,0:T(2,128)(2,1)}, f32[2]{0:T(128)}, f32[2]{0:T(128)}) custom-call(bf16[128,4,2,640]{3,2,1,0:T(2,128)(2,1)S(1)} %bitcast.16, f32[2,256]{1,0:T(2,128)S(1)} %get-tuple-element.13.pots_ref, bf16[2,324480]{1,0:T(2,128)(2,1)S(1)} %copy-done), custom_call_target="tpu_custom_call" | custom-call | tf_op jit(solution)/shard_map/pallas_call | solution.py:245
Async XLA Ops:
  84.8 26.2 %copy-start = (bf16[2,324480]{1,0:T(2,128)(2,1)S(1)}, bf16[2,324480]{1,0:T(2,128)(2,1)}, u32[]{:S(2)}) copy-start(bf16[2,324480]{1,0:T(2,128)(2,1)} %noise_ref.1) | copy-start | bytes 3893764

commit v9 on v8

--- a/solution.py
+++ b/solution.py
@@ -20,53 +20,54 @@
 UNIT = 640
 
 
-def pack_kernel(noise_ref, data_ref, out_ref, zeros, sems):
+def pack_kernel(noise_ref, data_ref, out_ref, noise_sq_ref, sems):
     devices, units = out_ref.shape[0], noise_ref.shape[0]
-    zeros[...] = jnp.zeros_like(zeros)
     copies = []
     for kind, ref in enumerate((noise_ref, data_ref)):
         for q in range(UNITS):
             slot = kind * UNITS + q
             start = q * devices
             count = min(devices, units - start)
-            copies.append((ref.at[pl.ds(start, count)], out_ref.at[pl.ds(0, count), slot]))
-            if count < devices:
-                copies.append((zeros, out_ref.at[pl.ds(count, devices - count), slot]))
-    copies = [pltpu.make_async_copy(src, dst, sems.at[n]) for n, (src, dst) in enumerate(copies)]
+            copies.append(
+                pltpu.make_async_copy(
+                    ref.at[pl.ds(start, count)], out_ref.at[pl.ds(0, count), slot], sems.at[slot]
+                )
+            )
     for copy in copies:
         copy.start()
-    for copy in copies:
-        copy.wait()
-
-
-def unpack_kernel(moved_ref, pots_ref, noise_ref, out_ref, row_ref, col_ref, row, col, sems):
+    rest = UNITS * devices - units
+    for kind in range(2):
+        slot = kind * UNITS + UNITS - 1
+        out_ref[devices - rest :, slot] = jnp.zeros((rest,) + out_ref.shape[2:], out_ref.dtype)
+    for copy in copies[:UNITS]:
+        copy.wait()
+
+    def add(n, total):
+        for q in range(UNITS):
+            unit = out_ref[n, q].astype(jnp.float32)
+            total = total + unit * unit
+        return total
+
+    total = jnp.zeros(out_ref.shape[2:], jnp.float32)
+    total = lax.fori_loop(0, devices, add, total, unroll=8)
+    total = jnp.sum(total, axis=1, keepdims=True)
+    noise_sq_ref[...] = jnp.broadcast_to(total, noise_sq_ref.shape)
+    for copy in copies[UNITS:]:
+        copy.wait()
+
+
+def unpack_kernel(moved_ref, out_ref, sems):
     devices, units = moved_ref.shape[0], out_ref.shape[0]
-    own = out_ref.shape[1]
     copies = []
     for q in range(UNITS):
         start = q * devices
         count = min(devices, units - start)
-        copies.append((moved_ref.at[pl.ds(0, count), q], out_ref.at[pl.ds(start, count)]))
-    copies.extend([(row, row_ref), (col, col_ref)])
-    copies = [pltpu.make_async_copy(src, dst, sems.at[n]) for n, (src, dst) in enumerate(copies)]
-    for copy in copies[:UNITS]:
-        copy.start()
-
-    def add(n, total):
-        unit = noise_ref[:, pl.ds(pl.multiple_of(n * UNIT, UNIT), UNIT)].astype(jnp.float32)
-        return total + unit * unit
-
-    noise_sq = jnp.zeros((own, UNIT), jnp.float32)
-    noise_sq = lax.fori_loop(0, units, add, noise_sq, unroll=13)
-    noise_sq = jnp.sum(noise_sq, axis=1, keepdims=True)
-    first = (lax.axis_index("dp") * lax.axis_size("dim") + lax.axis_index("dim")) * own
-    lane = lax.broadcasted_iota(jnp.int32, (1, BATCH), 1)
-    for n in range(own):
-        mine = lane == first + n
-        row_pot = jnp.sum(jnp.where(mine, pots_ref[0:1, :], 0.0))
-        row[n] = row_pot + jnp.sum(noise_sq[n : n + 1, :]) / LATENT
-        col[n] = jnp.sum(jnp.where(mine, pots_ref[1:2, :], 0.0))
-    for copy in copies[UNITS:]:
+        copies.append(
+            pltpu.make_async_copy(
+                moved_ref.at[pl.ds(0, count), q], out_ref.at[pl.ds(start, count)], sems.at[q]
+            )
+        )
+    for copy in copies:
         copy.start()
     for copy in copies:
         copy.wait()
@@ -103,7 +104,10 @@
     out_ref[...] = jnp.broadcast_to(total[None], out_ref.shape)
 
 
-def sweep_kernel(cost_ref, data_ref, out_ref, pots_ref, bias, kern, row_pot, col_pot, row_sum):
+def sweep_kernel(
+    cost_ref, data_ref, noise_sq_ref, out_ref, row_ref, col_ref,
+    bias, kern, row_pot, col_pot, row_sum, row_own, col_own, sems,
+):
     bias[...] = whole_of(cost_ref) * (-1.0 / (LATENT * BIT))
     col_pot[...] = jnp.zeros_like(col_pot)
 
@@ -180,13 +184,28 @@
         kern[...] = scaled
         row_sum[...] = jnp.sum(scaled, axis=0, keepdims=True)
 
+    own = out_ref.shape[1]
+    first = (lax.axis_index("dp") * lax.axis_size("dim") + lax.axis_index("dim")) * own
+    place = lax.broadcasted_iota(jnp.int32, (1, BATCH), 1)
+    rows = row_pot[...]
+    cols = jnp.transpose(col_pot[...])
+    for n in range(own):
+        mine = place == first + n
+        row = jnp.sum(jnp.where(mine, rows, 0.0)) * BIT
+        row_own[n] = row + jnp.max(noise_sq_ref[n : n + 1, :]) / LATENT
+        col_own[n] = jnp.sum(jnp.where(mine, cols, 0.0)) * BIT
+    copies = [(row_own, row_ref), (col_own, col_ref)]
+    copies = [pltpu.make_async_copy(src, dst, sems.at[n]) for n, (src, dst) in enumerate(copies)]
+    for copy in copies:
+        copy.start()
+
     weights = (kern[...] * (1.0 / row_sum[...])).astype(jnp.bfloat16)
     moved = lax.dot_general(
         weights, data_ref[...], (((0,), (0,)), ((), ())), preferred_element_type=jnp.float32
     )
     out_ref[...] = moved.astype(jnp.bfloat16).reshape(out_ref.shape)
-    pots_ref[0:1, :] = row_pot[...] * BIT
-    pots_ref[1:2, :] = jnp.transpose(col_pot[...] * BIT)
+    for copy in copies:
+        copy.wait()
 
 
 def on_device(noise, data):
@@ -196,19 +215,20 @@
     units = LATENT // UNIT
     params = pltpu.CompilerParams(vmem_limit_bytes=VMEM)
     anywhere = pl.BlockSpec(memory_space=pl.ANY)
+    whole = pl.BlockSpec(memory_space=pltpu.VMEM)
 
     def units_of(rows):
         return rows.reshape(own, units, UNIT).transpose(1, 0, 2)
 
-    both = pl.pallas_call(
+    both, noise_sq = pl.pallas_call(
         pack_kernel,
-        out_shape=jax.ShapeDtypeStruct((devices, 2 * UNITS, own, UNIT), noise.dtype),
-        in_specs=[pl.BlockSpec(memory_space=pltpu.HBM)] * 2,
-        out_specs=anywhere,
-        scratch_shapes=[
-            pltpu.VMEM((UNITS * devices - units, own, UNIT), noise.dtype),
-            pltpu.SemaphoreType.DMA((4 * UNITS,)),
-        ],
+        out_shape=(
+            jax.ShapeDtypeStruct((devices, 2 * UNITS, own, UNIT), noise.dtype),
+            jax.ShapeDtypeStruct((own, LANES), jnp.float32),
+        ),
+        in_specs=[anywhere, anywhere],
+        out_specs=(whole, whole),
+        scratch_shapes=[pltpu.SemaphoreType.DMA((2 * UNITS,))],
         compiler_params=params,
     )(*[pltpu.with_memory_space_constraint(units_of(rows), pltpu.HBM) for rows in (noise, data)])
     both = both.transpose(0, 2, 1, 3).reshape(devices, own, 2 * ent)
@@ -224,40 +244,34 @@
     total = pl.pallas_call(sum_kernel, out_shape=pieces, compiler_params=params)(parts)
     total = lax.all_to_all(total, AXES, split_axis=0, concat_axis=0)
 
-    moved, pots = pl.pallas_call(
+    scalars = jax.ShapeDtypeStruct((own,), jnp.float32)
+    moved, row, col = pl.pallas_call(
         sweep_kernel,
-        out_shape=(
-            jax.ShapeDtypeStruct((devices, own, ent), jnp.bfloat16),
-            jax.ShapeDtypeStruct((2, BATCH), jnp.float32),
-        ),
+        out_shape=(jax.ShapeDtypeStruct((devices, own, ent), jnp.bfloat16), scalars, scalars),
+        in_specs=[whole, whole, whole],
+        out_specs=(whole, anywhere, anywhere),
         scratch_shapes=[
             pltpu.VMEM((BATCH, BATCH), jnp.float32),
             pltpu.VMEM((BATCH, BATCH), jnp.float32),
             pltpu.VMEM((1, BATCH), jnp.float32),
             pltpu.VMEM((BATCH, 1), jnp.float32),
             pltpu.VMEM((1, BATCH), jnp.float32),
+            pltpu.SMEM((own,), jnp.float32),
+            pltpu.SMEM((own,), jnp.float32),
+            pltpu.SemaphoreType.DMA((2,)),
         ],
         compiler_params=params,
-    )(total, data_ent)
+    )(total, data_ent, noise_sq)
     moved = lax.all_to_all(moved, AXES, split_axis=0, concat_axis=0)
     moved = moved.reshape(devices, own, UNITS, UNIT).transpose(0, 2, 1, 3)
-    whole = pl.BlockSpec(memory_space=pltpu.VMEM)
-    targets, row, col = pl.pallas_call(
+    targets = pl.pallas_call(
         unpack_kernel,
-        out_shape=(
-            jax.ShapeDtypeStruct((units, own, UNIT), moved.dtype),
-            jax.ShapeDtypeStruct((own,), jnp.float32),
-            jax.ShapeDtypeStruct((own,), jnp.float32),
-        ),
-        in_specs=[anywhere, whole, whole],
-        out_specs=(anywhere, anywhere, anywhere),
-        scratch_shapes=[
-            pltpu.SMEM((own,), jnp.float32),
-            pltpu.SMEM((own,), jnp.float32),
-            pltpu.SemaphoreType.DMA((UNITS + 2,)),
-        ],
-        compiler_params=params,
-    )(moved, pots, noise)
+        out_shape=jax.ShapeDtypeStruct((units, own, UNIT), moved.dtype),
+        in_specs=[anywhere],
+        out_specs=anywhere,
+        scratch_shapes=[pltpu.SemaphoreType.DMA((UNITS,))],
+        compiler_params=params,
+    )(moved)
     return (targets.transpose(1, 0, 2).reshape(own, LATENT), row, col)
 
 

time: 113 us -> 113 us (level)
  no operation moved by 1% of the time
where the time goes in v9:
time: 113 us
  blocking collectives  104 us (92%)
  Pallas kernels  8.58 us (8%)
    all_to_all x1, blocking collectives, on_device(): both = lax.all_to_all(both, AXES, split_axis=0, concat_axis=0)  47 us
    all_to_all x1, blocking collectives, on_device(): moved = lax.all_to_all(moved, AXES, split_axis=0, concat_axis=0)  26.2 us
    all_to_all x1, blocking collectives, on_device(): total = lax.all_to_all(total, AXES, split_axis=0, concat_axis=0)  15.2 us
    all_to_all x1, blocking collectives, on_device(): parts = lax.all_to_all(parts, AXES, split_axis=0, concat_axis=0)  15.2 us
    pallas_call x1, Pallas kernels, on_device(): pl.pallas_call(sweep_kernel, out_shape=(jax.ShapeDtypeStruct((devices, ow...  4.11 us

profile of v9, /device:TPU:1, one launch (start us, length us, event | category | flops | bytes accessed | tf_op | source)
XLA Modules:
  0.0 112.9 jit_solution(4151352724365919716)
XLA Ops:
  0.6 2.0 %shard_map.49 = (bf16[128,8,2,640]{3,2,1,0:T(2,128)(2,1)S(1)}, f32[2,128]{1,0:T(2,128)S(1)}) custom-call(bf16[507,2,640]{2,1,0:T(2,128)(2,1)} %bitcast.17, bf16[507,2,640]{2,1,0:T(2,128)(2,1)} %bitcast.18), custom_call_target="tpu_custom_call" | custom-call | tf_op jit(solution)/shard_map/pallas_call | solution.py:223
  2.7 47.0 %all_to_all.20.both_ref = bf16[128,2,5120]{2,1,0:T(2,128)(2,1)S(1)} all-to-all(bf16[128,2,5120]{2,1,0:T(2,128)(2,1)S(1)} %bitcast.16), channel_id=1, replica_groups=mesh['dp'=16,'dim'=8] {'dp','dim'}, dimensions={0} | all-to-all | bytes 5242880 | tf_op jit(solution)/shard_map/all_to_all | solution.py:235
  49.7 1.2 %shard_map.50 = (f32[128,4,128]{2,1,0:T(4,128)S(1)}, bf16[256,2560]{1,0:T(8,128)(2,1)S(1)}) custom-call(bf16[128,2,5120]{2,1,0:T(2,128)(2,1)S(1)} %all_to_all.20.both_ref), custom_call_target="tpu_custom_call" | custom-call | tf_op jit(solution)/shard_map/pallas_call | solution.py:238
  50.9 15.2 %all_to_all.21.parts_ref = f32[128,4,128]{2,1,0:T(4,128)S(1)} all-to-all(f32[128,4,128]{2,1,0:T(4,128)S(1)} %get-tuple-element.11), channel_id=1, replica_groups=mesh['dp'=16,'dim'=8] {'dp','dim'}, dimensions={0} | all-to-all | bytes 524288 | tf_op jit(solution)/shard_map/all_to_all | solution.py:243
  66.1 0.2 shard_map.51
  66.2 15.2 %all_to_all.22.cost_ref = f32[128,4,128]{2,1,0:T(4,128)S(1)} all-to-all(f32[128,4,128]{2,1,0:T(4,128)S(1)} %shard_map.51), channel_id=1, replica_groups=mesh['dp'=16,'dim'=8] {'dp','dim'}, dimensions={0} | all-to-all | bytes 524288 | tf_op jit(solution)/shard_map/all_to_all | solution.py:245
  81.5 4.1 %shard_map.52 = (bf16[128,2,2560]{2,1,0:T(2,128)(2,1)S(1)}, f32[2]{0:T(128)}, f32[2]{0:T(128)}) custom-call(f32[128,4,128]{2,1,0:T(4,128)S(1)} %all_to_all.22.cost_ref, bf16[256,2560]{1,0:T(8,128)(2,1)S(1)} %get-tuple-element.12.data_ref, f32[2,128]{1,0:T(2,128)S(1)} %get-tuple-element.13.noise_sq_ref), custom_call_target="tpu_custom_call" | custom-call | tf_op jit(solution)/shard_map/pallas_call | solution.py:248
  85.6 26.2 %all_to_all.23 = bf16[128,2,2560]{2,1,0:T(2,128)(2,1)S(1)} all-to-all(bf16[128,2,2560]{2,1,0:T(2,128)(2,1)S(1)} %get-tuple-element.14), channel_id=1, replica_groups=mesh['dp'=16,'dim'=8] {'dp','dim'}, dimensions={0} | all-to-all | bytes 2621440 | tf_op jit(solution)/shard_map/all_to_all | solution.py:265
  111.8 1.1 shard_map.53

commit v10 on v8

--- a/solution.py
+++ b/solution.py
@@ -39,7 +39,7 @@
         copy.wait()
 
 
-def unpack_kernel(moved_ref, pots_ref, noise_ref, out_ref, row_ref, col_ref, row, col, sems):
+def unpack_kernel(moved_ref, pots_ref, noise_sq_ref, out_ref, row_ref, col_ref, row, col, sems):
     devices, units = moved_ref.shape[0], out_ref.shape[0]
     own = out_ref.shape[1]
     copies = []
@@ -52,19 +52,12 @@
     for copy in copies[:UNITS]:
         copy.start()
 
-    def add(n, total):
-        unit = noise_ref[:, pl.ds(pl.multiple_of(n * UNIT, UNIT), UNIT)].astype(jnp.float32)
-        return total + unit * unit
-
-    noise_sq = jnp.zeros((own, UNIT), jnp.float32)
-    noise_sq = lax.fori_loop(0, units, add, noise_sq, unroll=13)
-    noise_sq = jnp.sum(noise_sq, axis=1, keepdims=True)
     first = (lax.axis_index("dp") * lax.axis_size("dim") + lax.axis_index("dim")) * own
     lane = lax.broadcasted_iota(jnp.int32, (1, BATCH), 1)
     for n in range(own):
         mine = lane == first + n
         row_pot = jnp.sum(jnp.where(mine, pots_ref[0:1, :], 0.0))
-        row[n] = row_pot + jnp.sum(noise_sq[n : n + 1, :]) / LATENT
+        row[n] = row_pot + jnp.max(noise_sq_ref[n : n + 1, :]) / LATENT
         col[n] = jnp.sum(jnp.where(mine, pots_ref[1:2, :], 0.0))
     for copy in copies[UNITS:]:
         copy.start()
@@ -103,7 +96,10 @@
     out_ref[...] = jnp.broadcast_to(total[None], out_ref.shape)
 
 
-def sweep_kernel(cost_ref, data_ref, out_ref, pots_ref, bias, kern, row_pot, col_pot, row_sum):
+def sweep_kernel(
+    cost_ref, data_ref, noise_ref, out_ref, pots_ref, noise_sq_ref,
+    bias, kern, row_pot, col_pot, row_sum,
+):
     bias[...] = whole_of(cost_ref) * (-1.0 / (LATENT * BIT))
     col_pot[...] = jnp.zeros_like(col_pot)
 
@@ -146,12 +142,24 @@
             totals.append(total)
         return low, high, totals
 
+    units = noise_ref.shape[1] // UNIT
+    share = units // (SWEEPS - 2)
+
+    def squares(first, count, total):
+        for n in range(count):
+            start = pl.multiple_of((first + n) * UNIT, LANES)
+            unit = noise_ref[:, pl.ds(start, UNIT)].astype(jnp.float32)
+            total = total + unit * unit
+        return total
+
     def sweep(step, carry):
-        low, high, rows = carry
+        low, high, rows, noise_sq = carry
         low, high, totals = over_columns(low, high, rows, None)
         for total in totals:
             high = jnp.maximum(high, total)
-        return (low, high, tuple(1.0 / total for total in totals))
+        if rows is not None:
+            noise_sq = squares((step - 2) * share, share, noise_sq)
+        return (low, high, tuple(1.0 / total for total in totals), noise_sq)
 
     def finish(block, factor, parts):
         col_pot[block, :] += jnp.log2(factor[:, :1])
@@ -159,8 +167,11 @@
             kern[block, half] = part
 
     ones = jnp.ones(tile, jnp.float32)
-    carry = sweep(0, (ones, ones, None))
-    low, high, rows = lax.fori_loop(2, SWEEPS, sweep, carry)
+    carry = sweep(0, (ones, ones, None, jnp.zeros((noise_ref.shape[0], UNIT), jnp.float32)))
+    low, high, rows, noise_sq = lax.fori_loop(2, SWEEPS, sweep, carry)
+    done = (SWEEPS - 2) * share
+    noise_sq = jnp.sum(squares(done, units - done, noise_sq), axis=1, keepdims=True)
+    noise_sq_ref[...] = jnp.broadcast_to(noise_sq, noise_sq_ref.shape)
     low, high, totals = over_columns(low, high, rows, finish)
     row_pot[...] += jnp.log2(jnp.concatenate([row[:1] for row in rows], axis=1))
     row_sum[...] = jnp.concatenate([total[:1] for total in totals], axis=1)
@@ -224,11 +235,12 @@
     total = pl.pallas_call(sum_kernel, out_shape=pieces, compiler_params=params)(parts)
     total = lax.all_to_all(total, AXES, split_axis=0, concat_axis=0)
 
-    moved, pots = pl.pallas_call(
+    moved, pots, noise_sq = pl.pallas_call(
         sweep_kernel,
         out_shape=(
             jax.ShapeDtypeStruct((devices, own, ent), jnp.bfloat16),
             jax.ShapeDtypeStruct((2, BATCH), jnp.float32),
+            jax.ShapeDtypeStruct((own, LANES), jnp.float32),
         ),
         scratch_shapes=[
             pltpu.VMEM((BATCH, BATCH), jnp.float32),
@@ -238,7 +250,7 @@
             pltpu.VMEM((1, BATCH), jnp.float32),
         ],
         compiler_params=params,
-    )(total, data_ent)
+    )(total, data_ent, noise)
     moved = lax.all_to_all(moved, AXES, split_axis=0, concat_axis=0)
     moved = moved.reshape(devices, own, UNITS, UNIT).transpose(0, 2, 1, 3)
     whole = pl.BlockSpec(memory_space=pltpu.VMEM)
@@ -257,7 +269,7 @@
             pltpu.SemaphoreType.DMA((UNITS + 2,)),
         ],
         compiler_params=params,
-    )(moved, pots, noise)
+    )(moved, pots, noise_sq)
     return (targets.transpose(1, 0, 2).reshape(own, LATENT), row, col)
 
 

time: 113 us -> 113 us (level)
  no operation moved by 1% of the time
where the time goes in v10:
time: 113 us; the launch traced here: 112 us
  blocking collectives  104 us (92%)
  Pallas kernels  7.86 us (7%)
    all_to_all x1, blocking collectives, on_device(): both = lax.all_to_all(both, AXES, split_axis=0, concat_axis=0)  47 us
    all_to_all x1, blocking collectives, on_device(): moved = lax.all_to_all(moved, AXES, split_axis=0, concat_axis=0)  26.2 us
    all_to_all x1, blocking collectives, on_device(): parts = lax.all_to_all(parts, AXES, split_axis=0, concat_axis=0)  15.3 us
    all_to_all x1, blocking collectives, on_device(): total = lax.all_to_all(total, AXES, split_axis=0, concat_axis=0)  15.2 us
    pallas_call x1, Pallas kernels, on_device(): pl.pallas_call(sweep_kernel, out_shape=(jax.ShapeDtypeStruct((devices, ow...  3.57 us

profile of v10, /device:TPU:1, one launch (start us, length us, event | category | flops | bytes accessed | tf_op | source)
XLA Modules:
  0.0 112.3 jit_solution(8144788339315022491)
XLA Ops:
  0.6 1.8 %shard_map.49 = bf16[128,8,2,640]{3,2,1,0:T(2,128)(2,1)S(1)} custom-call(bf16[507,2,640]{2,1,0:T(2,128)(2,1)} %bitcast.17, bf16[507,2,640]{2,1,0:T(2,128)(2,1)} %bitcast.18), custom_call_target="tpu_custom_call" | custom-call | tf_op jit(solution)/shard_map/pallas_call | solution.py:214
  2.4 47.0 %all_to_all.20.both_ref = bf16[128,2,5120]{2,1,0:T(2,128)(2,1)S(1)} all-to-all(bf16[128,2,5120]{2,1,0:T(2,128)(2,1)S(1)} %bitcast.15), channel_id=1, replica_groups=mesh['dp'=16,'dim'=8] {'dp','dim'}, dimensions={0} | all-to-all | bytes 5242880 | tf_op jit(solution)/shard_map/all_to_all | solution.py:226
  49.5 1.2 %shard_map.50 = (f32[128,4,128]{2,1,0:T(4,128)S(1)}, bf16[256,2560]{1,0:T(8,128)(2,1)S(1)}) custom-call(bf16[128,2,5120]{2,1,0:T(2,128)(2,1)S(1)} %all_to_all.20.both_ref), custom_call_target="tpu_custom_call" | custom-call | tf_op jit(solution)/shard_map/pallas_call | solution.py:229
  50.7 0.0 copy-start
  50.7 15.3 %all_to_all.21.parts_ref = f32[128,4,128]{2,1,0:T(4,128)S(1)} all-to-all(f32[128,4,128]{2,1,0:T(4,128)S(1)} %get-tuple-element.11), channel_id=1, replica_groups=mesh['dp'=16,'dim'=8] {'dp','dim'}, dimensions={0} | all-to-all | bytes 524288 | tf_op jit(solution)/shard_map/all_to_all | solution.py:234
  66.0 0.2 shard_map.51
  66.2 15.2 %all_to_all.22.cost_ref = f32[128,4,128]{2,1,0:T(4,128)S(1)} all-to-all(f32[128,4,128]{2,1,0:T(4,128)S(1)} %shard_map.51), channel_id=1, replica_groups=mesh['dp'=16,'dim'=8] {'dp','dim'}, dimensions={0} | all-to-all | bytes 524288 | tf_op jit(solution)/shard_map/all_to_all | solution.py:236
  81.4 0.0 copy-done
  81.4 3.6 %shard_map.52 = (bf16[128,2,2560]{2,1,0:T(2,128)(2,1)S(1)}, f32[2,256]{1,0:T(2,128)S(1)}, f32[2,128]{1,0:T(2,128)S(1)}) custom-call(f32[128,4,128]{2,1,0:T(4,128)S(1)} %all_to_all.22.cost_ref, bf16[256,2560]{1,0:T(8,128)(2,1)S(1)} %get-tuple-element.12.data_ref, bf16[2,324480]{1,0:T(2,128)(2,1)S(1)} %copy-done), custom_call_target="tpu_custom_call" | custom-call | tf_op jit(solution)/shard_map/pallas_call | solution.py:238
  85.0 26.2 %all_to_all.23 = bf16[128,2,2560]{2,1,0:T(2,128)(2,1)S(1)} all-to-all(bf16[128,2,2560]{2,1,0:T(2,128)(2,1)S(1)} %get-tuple-element.13), channel_id=1, replica_groups=mesh['dp'=16,'dim'=8] {'dp','dim'}, dimensions={0} | all-to-all | bytes 2621440 | tf_op jit(solution)/shard_map/all_to_all | solution.py:254
  111.2 1.1 shard_map.53
Async XLA Ops:
  50.7 30.7 %copy-start = (bf16[2,324480]{1,0:T(2,128)(2,1)S(1)}, bf16[2,324480]{1,0:T(2,128)(2,1)}, u32[]{:S(2)}) copy-start(bf16[2,324480]{1,0:T(2,128)(2,1)} %noise_ref.1) | copy-start | bytes 3893764

commit v11 on v10

--- a/solution.py
+++ b/solution.py
@@ -86,8 +86,11 @@
     gram = lax.dot_general(
         data, noise, (((1,), (1,)), ((), ())), preferred_element_type=jnp.float32
     )
-    wide = data.astype(jnp.float32)
-    data_sq = jnp.sum(wide * wide, axis=1, keepdims=True)
+    data_sq = jnp.zeros((BATCH, LANES), jnp.float32)
+    for start in range(0, ent, LANES):
+        wide = data_ref[:, start : start + LANES].astype(jnp.float32)
+        data_sq = data_sq + wide * wide
+    data_sq = jnp.sum(data_sq, axis=1, keepdims=True)
     pieces_of(data_sq - 2.0 * gram, out_ref)
 
 

time: 113 us -> 112 us (level)
  no operation moved by 1% of the time
where the time goes in v11:
time: 112 us
  blocking collectives  104 us (93%)
  Pallas kernels  7.58 us (7%)
    all_to_all x1, blocking collectives, on_device(): both = lax.all_to_all(both, AXES, split_axis=0, concat_axis=0)  47 us
    all_to_all x1, blocking collectives, on_device(): moved = lax.all_to_all(moved, AXES, split_axis=0, concat_axis=0)  26.2 us
    all_to_all x1, blocking collectives, on_device(): parts = lax.all_to_all(parts, AXES, split_axis=0, concat_axis=0)  15.3 us
    all_to_all x1, blocking collectives, on_device(): total = lax.all_to_all(total, AXES, split_axis=0, concat_axis=0)  15.2 us
    pallas_call x1, Pallas kernels, on_device(): pl.pallas_call(sweep_kernel, out_shape=(jax.ShapeDtypeStruct((devices, ow...  3.57 us

profile of v11, /device:TPU:1, one launch (start us, length us, event | category | flops | bytes accessed | tf_op | source)
XLA Modules:
  0.0 112.0 jit_solution(10718842691452477806)
XLA Ops:
  0.6 1.8 %shard_map.49 = bf16[128,8,2,640]{3,2,1,0:T(2,128)(2,1)S(1)} custom-call(bf16[507,2,640]{2,1,0:T(2,128)(2,1)} %bitcast.17, bf16[507,2,640]{2,1,0:T(2,128)(2,1)} %bitcast.18), custom_call_target="tpu_custom_call" | custom-call | tf_op jit(solution)/shard_map/pallas_call | solution.py:217
  2.4 47.0 %all_to_all.20.both_ref = bf16[128,2,5120]{2,1,0:T(2,128)(2,1)S(1)} all-to-all(bf16[128,2,5120]{2,1,0:T(2,128)(2,1)S(1)} %bitcast.15), channel_id=1, replica_groups=mesh['dp'=16,'dim'=8] {'dp','dim'}, dimensions={0} | all-to-all | bytes 5242880 | tf_op jit(solution)/shard_map/all_to_all | solution.py:229
  49.5 0.9 shard_map.50
  50.4 0.0 copy-start
  50.4 15.3 %all_to_all.21.parts_ref = f32[128,4,128]{2,1,0:T(4,128)S(1)} all-to-all(f32[128,4,128]{2,1,0:T(4,128)S(1)} %get-tuple-element.11), channel_id=1, replica_groups=mesh['dp'=16,'dim'=8] {'dp','dim'}, dimensions={0} | all-to-all | bytes 524288 | tf_op jit(solution)/shard_map/all_to_all | solution.py:237
  65.7 0.2 shard_map.51
  65.9 15.2 %all_to_all.22.cost_ref = f32[128,4,128]{2,1,0:T(4,128)S(1)} all-to-all(f32[128,4,128]{2,1,0:T(4,128)S(1)} %shard_map.51), channel_id=1, replica_groups=mesh['dp'=16,'dim'=8] {'dp','dim'}, dimensions={0} | all-to-all | bytes 524288 | tf_op jit(solution)/shard_map/all_to_all | solution.py:239
  81.1 0.0 copy-done
  81.1 3.6 %shard_map.52 = (bf16[128,2,2560]{2,1,0:T(2,128)(2,1)S(1)}, f32[2,256]{1,0:T(2,128)S(1)}, f32[2,128]{1,0:T(2,128)S(1)}) custom-call(f32[128,4,128]{2,1,0:T(4,128)S(1)} %all_to_all.22.cost_ref, bf16[256,2560]{1,0:T(8,128)(2,1)S(1)} %get-tuple-element.12.data_ref, bf16[2,324480]{1,0:T(2,128)(2,1)S(1)} %copy-done), custom_call_target="tpu_custom_call" | custom-call | tf_op jit(solution)/shard_map/pallas_call | solution.py:241
  84.7 26.2 %all_to_all.23 = bf16[128,2,2560]{2,1,0:T(2,128)(2,1)S(1)} all-to-all(bf16[128,2,2560]{2,1,0:T(2,128)(2,1)S(1)} %get-tuple-element.13), channel_id=1, replica_groups=mesh['dp'=16,'dim'=8] {'dp','dim'}, dimensions={0} | all-to-all | bytes 2621440 | tf_op jit(solution)/shard_map/all_to_all | solution.py:257
  110.9 1.1 shard_map.53
Async XLA Ops:
  50.4 30.7 %copy-start = (bf16[2,324480]{1,0:T(2,128)(2,1)S(1)}, bf16[2,324480]{1,0:T(2,128)(2,1)}, u32[]{:S(2)}) copy-start(bf16[2,324480]{1,0:T(2,128)(2,1)} %noise_ref.1) | copy-start | bytes 3893764

commit v12 on v11

--- a/solution.py
+++ b/solution.py
@@ -65,17 +65,10 @@
         copy.wait()
 
 
-def pieces_of(value, pieces_ref):
-    for piece in range(BATCH * 2 // 4):
-        row, half = 4 * (piece // 2), LANES * (piece % 2)
-        pieces_ref[piece] = value[row : row + 4, half : half + LANES]
-
-
-def whole_of(pieces_ref):
-    rows = []
-    for row in range(BATCH // 4):
-        rows.append(jnp.concatenate([pieces_ref[2 * row], pieces_ref[2 * row + 1]], axis=1))
-    return jnp.concatenate(rows, axis=0)
+def tiles():
+    for tile in range(BATCH * BATCH // (8 * LANES)):
+        row, half = 8 * (tile // 2), LANES * (tile % 2)
+        yield tile, slice(row, row + 8), slice(half, half + LANES)
 
 
 def gram_kernel(both_ref, out_ref, data_ref):
@@ -91,11 +84,15 @@
         wide = data_ref[:, start : start + LANES].astype(jnp.float32)
         data_sq = data_sq + wide * wide
     data_sq = jnp.sum(data_sq, axis=1, keepdims=True)
-    pieces_of(data_sq - 2.0 * gram, out_ref)
+    parts = data_sq - 2.0 * gram
+    for tile, rows, half in tiles():
+        out_ref[tile] = parts[rows, half]
 
 
 def sum_kernel(parts_ref, out_ref):
     total = jnp.sum(parts_ref[...], axis=0)
+    total = total[:4] + total[4:]
+    total = jnp.concatenate([total, total], axis=0)
     out_ref[...] = jnp.broadcast_to(total[None], out_ref.shape)
 
 
@@ -103,7 +100,8 @@
     cost_ref, data_ref, noise_ref, out_ref, pots_ref, noise_sq_ref,
     bias, kern, row_pot, col_pot, row_sum,
 ):
-    bias[...] = whole_of(cost_ref) * (-1.0 / (LATENT * BIT))
+    for tile, rows, half in tiles():
+        bias[rows, half] = cost_ref[tile] * (-1.0 / (LATENT * BIT))
     col_pot[...] = jnp.zeros_like(col_pot)
 
     def log_sweep():
@@ -228,15 +226,19 @@
     both = both.transpose(0, 2, 1, 3).reshape(devices, own, 2 * ent)
     both = lax.all_to_all(both, AXES, split_axis=0, concat_axis=0)
 
-    pieces = jax.ShapeDtypeStruct((devices, 4, LANES), jnp.float32)
+    whole = jax.ShapeDtypeStruct((devices // 2, 8, LANES), jnp.float32)
+
+    def exchange(parts):
+        parts = parts.reshape(devices, 4, LANES)
+        return lax.all_to_all(parts, AXES, split_axis=0, concat_axis=0).reshape(whole.shape)
+
     parts, data_ent = pl.pallas_call(
         gram_kernel,
-        out_shape=(pieces, jax.ShapeDtypeStruct((BATCH, ent), data.dtype)),
+        out_shape=(whole, jax.ShapeDtypeStruct((BATCH, ent), data.dtype)),
         compiler_params=params,
     )(both)
-    parts = lax.all_to_all(parts, AXES, split_axis=0, concat_axis=0)
-    total = pl.pallas_call(sum_kernel, out_shape=pieces, compiler_params=params)(parts)
-    total = lax.all_to_all(total, AXES, split_axis=0, concat_axis=0)
+    total = pl.pallas_call(sum_kernel, out_shape=whole, compiler_params=params)(exchange(parts))
+    total = exchange(total)
 
     moved, pots, noise_sq = pl.pallas_call(
         sweep_kernel,
@@ -256,7 +258,7 @@
     )(total, data_ent, noise)
     moved = lax.all_to_all(moved, AXES, split_axis=0, concat_axis=0)
     moved = moved.reshape(devices, own, UNITS, UNIT).transpose(0, 2, 1, 3)
-    whole = pl.BlockSpec(memory_space=pltpu.VMEM)
+    in_vmem = pl.BlockSpec(memory_space=pltpu.VMEM)
     targets, row, col = pl.pallas_call(
         unpack_kernel,
         out_shape=(
@@ -264,7 +266,7 @@
             jax.ShapeDtypeStruct((own,), jnp.float32),
             jax.ShapeDtypeStruct((own,), jnp.float32),
         ),
-        in_specs=[anywhere, whole, whole],
+        in_specs=[anywhere, in_vmem, in_vmem],
         out_specs=(anywhere, anywhere, anywhere),
         scratch_shapes=[
             pltpu.SMEM((own,), jnp.float32),

time: 112 us -> 112 us (level)
  no operation moved by 1% of the time
where the time goes in v12:
time: 112 us
  blocking collectives  104 us (93%)
  Pallas kernels  7.5 us (7%)
    all_to_all x1, blocking collectives, on_device(): both = lax.all_to_all(both, AXES, split_axis=0, concat_axis=0)  47 us
    all_to_all x2, blocking collectives, exchange(): lax.all_to_all(parts, AXES, split_axis=0, concat_axis=0)  30.5 us
    all_to_all x1, blocking collectives, on_device(): moved = lax.all_to_all(moved, AXES, split_axis=0, concat_axis=0)  26.2 us
    pallas_call x1, Pallas kernels, on_device(): pl.pallas_call(sweep_kernel, out_shape=(jax.ShapeDtypeStruct((devices, ow...  3.57 us

profile of v12, /device:TPU:1, one launch (start us, length us, event | category | flops | bytes accessed | tf_op | source)
XLA Modules:
  0.0 111.9 jit_solution(11545255736914005977)
XLA Ops:
  0.6 1.8 %shard_map.49 = bf16[128,8,2,640]{3,2,1,0:T(2,128)(2,1)S(1)} custom-call(bf16[507,2,640]{2,1,0:T(2,128)(2,1)} %bitcast.21, bf16[507,2,640]{2,1,0:T(2,128)(2,1)} %bitcast.26), custom_call_target="tpu_custom_call" | custom-call | tf_op jit(solution)/shard_map/pallas_call | solution.py:215
  2.4 47.0 %all_to_all.20.both_ref = bf16[128,2,5120]{2,1,0:T(2,128)(2,1)S(1)} all-to-all(bf16[128,2,5120]{2,1,0:T(2,128)(2,1)S(1)} %bitcast.19), channel_id=1, replica_groups=mesh['dp'=16,'dim'=8] {'dp','dim'}, dimensions={0} | all-to-all | bytes 5242880 | tf_op jit(solution)/shard_map/all_to_all | solution.py:227
  49.5 0.9 shard_map.50
  50.4 0.0 copy-start
  50.4 15.3 %all_to_all.21 = f32[128,4,128]{2,1,0:T(4,128)S(1)} all-to-all(f32[128,4,128]{2,1,0:T(4,128)S(1)} %bitcast.25), channel_id=1, replica_groups=mesh['dp'=16,'dim'=8] {'dp','dim'}, dimensions={0} | all-to-all | bytes 524288 | tf_op jit(solution)/shard_map/all_to_all | solution.py:233
  65.7 0.1 shard_map.51
  65.8 15.2 %all_to_all.22 = f32[128,4,128]{2,1,0:T(4,128)S(1)} all-to-all(f32[128,4,128]{2,1,0:T(4,128)S(1)} %bitcast.24), channel_id=1, replica_groups=mesh['dp'=16,'dim'=8] {'dp','dim'}, dimensions={0} | all-to-all | bytes 524288 | tf_op jit(solution)/shard_map/all_to_all | solution.py:233
  81.0 0.0 copy-done
  81.0 3.6 %shard_map.52 = (bf16[128,2,2560]{2,1,0:T(2,128)(2,1)S(1)}, f32[2,256]{1,0:T(2,128)S(1)}, f32[2,128]{1,0:T(2,128)S(1)}) custom-call(f32[64,8,128]{2,1,0:T(8,128)S(1)} %bitcast.22, bf16[256,2560]{1,0:T(8,128)(2,1)S(1)} %get-tuple-element.12.data_ref, bf16[2,324480]{1,0:T(2,128)(2,1)S(1)} %copy-done), custom_call_target="tpu_custom_call" | custom-call | tf_op jit(solution)/shard_map/pallas_call | solution.py:243
  84.6 26.2 %all_to_all.23 = bf16[128,2,2560]{2,1,0:T(2,128)(2,1)S(1)} all-to-all(bf16[128,2,2560]{2,1,0:T(2,128)(2,1)S(1)} %get-tuple-element.13), channel_id=1, replica_groups=mesh['dp'=16,'dim'=8] {'dp','dim'}, dimensions={0} | all-to-all | bytes 2621440 | tf_op jit(solution)/shard_map/all_to_all | solution.py:259
  110.8 1.1 shard_map.53
Async XLA Ops:
  50.4 30.6 %copy-start = (bf16[2,324480]{1,0:T(2,128)(2,1)S(1)}, bf16[2,324480]{1,0:T(2,128)(2,1)}, u32[]{:S(2)}) copy-start(bf16[2,324480]{1,0:T(2,128)(2,1)} %noise_ref.1) | copy-start | bytes 3893764

commit v13 on v12

--- a/solution.py
+++ b/solution.py
@@ -65,28 +65,48 @@
         copy.wait()
 
 
-def tiles():
-    for tile in range(BATCH * BATCH // (8 * LANES)):
+def tiles(rows):
+    for tile in range(rows * BATCH // (8 * LANES)):
         row, half = 8 * (tile // 2), LANES * (tile % 2)
         yield tile, slice(row, row + 8), slice(half, half + LANES)
 
 
-def gram_kernel(both_ref, out_ref, data_ref):
-    ent = data_ref.shape[1]
-    noise = both_ref[:, :, :ent].reshape(data_ref.shape)
-    data = both_ref[:, :, ent:].reshape(data_ref.shape)
+def core():
+    return lax.rem(lax.axis_index("dim"), 2)
+
+
+def half_of(both_ref, noise, part, data_ref, out_ref):
+    rows, ent = data_ref.shape
+    pairs = rows // both_ref.shape[1]
+    data = both_ref[pl.ds(pl.multiple_of(part * pairs, pairs), pairs), :, ent:].reshape(rows, ent)
     data_ref[...] = data
     gram = lax.dot_general(
         data, noise, (((1,), (1,)), ((), ())), preferred_element_type=jnp.float32
     )
-    data_sq = jnp.zeros((BATCH, LANES), jnp.float32)
+    data_sq = jnp.zeros((rows, LANES), jnp.float32)
     for start in range(0, ent, LANES):
         wide = data_ref[:, start : start + LANES].astype(jnp.float32)
         data_sq = data_sq + wide * wide
     data_sq = jnp.sum(data_sq, axis=1, keepdims=True)
     parts = data_sq - 2.0 * gram
-    for tile, rows, half in tiles():
-        out_ref[tile] = parts[rows, half]
+    for tile, span, half in tiles(rows):
+        out_ref[tile] = parts[span, half]
+
+
+def sent_kernel(both_ref, out_ref, noise_ref, data_ref):
+    noise_ref[...] = both_ref[:, :, : noise_ref.shape[1]].reshape(noise_ref.shape)
+    half_of(both_ref, noise_ref[...], 1 - core(), data_ref, out_ref)
+
+
+def kept_kernel(both_ref, noise_ref, other_ref, out_ref, data_ref, own):
+    rows = own.shape[0]
+    half_of(both_ref, noise_ref[...], core(), own, out_ref)
+    data_ref[pl.ds(pl.multiple_of(core() * rows, rows), rows), :] = own[...]
+    data_ref[pl.ds(pl.multiple_of((1 - core()) * rows, rows), rows), :] = other_ref[...]
+
+
+def add_kernel(first_ref, second_ref, out_ref):
+    out_ref[...] = first_ref[...] + second_ref[...]
 
 
 def sum_kernel(parts_ref, out_ref):
@@ -97,11 +117,14 @@
 
 
 def sweep_kernel(
-    cost_ref, data_ref, noise_ref, out_ref, pots_ref, noise_sq_ref,
+    cost_ref, other_ref, data_ref, noise_ref, out_ref, pots_ref, noise_sq_ref,
     bias, kern, row_pot, col_pot, row_sum,
 ):
-    for tile, rows, half in tiles():
-        bias[rows, half] = cost_ref[tile] * (-1.0 / (LATENT * BIT))
+    for part, ref in ((core(), cost_ref), (1 - core(), other_ref)):
+        first = part * (BATCH // 2)
+        for tile, span, half in tiles(BATCH // 2):
+            rows = pl.ds(pl.multiple_of(first + span.start, 8), 8)
+            bias[rows, half] = ref[tile] * (-1.0 / (LATENT * BIT))
     col_pot[...] = jnp.zeros_like(col_pot)
 
     def log_sweep():
@@ -226,18 +249,32 @@
     both = both.transpose(0, 2, 1, 3).reshape(devices, own, 2 * ent)
     both = lax.all_to_all(both, AXES, split_axis=0, concat_axis=0)
 
-    whole = jax.ShapeDtypeStruct((devices // 2, 8, LANES), jnp.float32)
+    part = jax.ShapeDtypeStruct((devices // 4, 8, LANES), jnp.float32)
+    data_half = jax.ShapeDtypeStruct((BATCH // 2, ent), data.dtype)
+    data_whole = jax.ShapeDtypeStruct((BATCH, ent), data.dtype)
 
     def exchange(parts):
-        parts = parts.reshape(devices, 4, LANES)
-        return lax.all_to_all(parts, AXES, split_axis=0, concat_axis=0).reshape(whole.shape)
-
-    parts, data_ent = pl.pallas_call(
-        gram_kernel,
-        out_shape=(whole, jax.ShapeDtypeStruct((BATCH, ent), data.dtype)),
+        parts = parts.reshape(devices, 2, LANES)
+        return lax.all_to_all(parts, AXES, split_axis=0, concat_axis=0).reshape(part.shape)
+
+    def other_core(parts):
+        return lax.ppermute(parts, "dim", [(k, k ^ 1) for k in range(lax.axis_size("dim"))])
+
+    sent, noise_ent, data_other = pl.pallas_call(
+        sent_kernel, out_shape=(part, data_whole, data_half), compiler_params=params
+    )(both)
+    got = other_core(sent)
+    kept, data_ent = pl.pallas_call(
+        kept_kernel,
+        out_shape=(part, data_whole),
+        scratch_shapes=[pltpu.VMEM(data_half.shape, data_half.dtype)],
         compiler_params=params,
-    )(both)
-    total = pl.pallas_call(sum_kernel, out_shape=whole, compiler_params=params)(exchange(parts))
+        cost_estimate=pl.CostEstimate(
+            flops=BATCH * BATCH * ent, bytes_accessed=6 * BATCH * ent, transcendentals=0
+        ),
+    )(both, noise_ent, data_other)
+    parts = pl.pallas_call(add_kernel, out_shape=part, compiler_params=params)(kept, got)
+    total = pl.pallas_call(sum_kernel, out_shape=part, compiler_params=params)(exchange(parts))
     total = exchange(total)
 
     moved, pots, noise_sq = pl.pallas_call(
@@ -255,7 +292,7 @@
             pltpu.VMEM((1, BATCH), jnp.float32),
         ],
         compiler_params=params,
-    )(total, data_ent, noise)
+    )(total, other_core(total), data_ent, noise)
     moved = lax.all_to_all(moved, AXES, split_axis=0, concat_axis=0)
     moved = moved.reshape(devices, own, UNITS, UNIT).transpose(0, 2, 1, 3)
     in_vmem = pl.BlockSpec(memory_space=pltpu.VMEM)

time: 112 us -> 112 us (level)
  blocking collectives: 104 us -> 99.9 us
  starting transfers between devices: 0 us -> 2.4 us
  waiting for transfers between devices: 0 us -> 1.32 us
    all_to_all x2, blocking collectives: 30.5 us -> 27.4 us  [exchange(): lax.all_to_all(parts, AXES, split_axis=0, concat_axis=0).reshape(part.shape)]
    ppermute x0 -> x2, starting transfers between devices: none -> 2.4 us  [other_core(): lax.ppermute(parts, 'dim', [(k, k ^ 1) for k in range(lax.axis_size('dim'...]
    ppermute x0 -> x2, waiting for transfers between devices: none -> 1.32 us  [other_core(): lax.ppermute(parts, 'dim', [(k, k ^ 1) for k in range(lax.axis_size('dim'...]
  transfers between devices with their start and end apart: 0 -> 2, of which waited for: 0 -> 2; matrix products, arithmetic and copies ran while one was open for 0% -> 0% of each run, Pallas kernels for 0% -> 1%
where the time goes in v13:
time: 112 us
  blocking collectives  99.9 us (89%)
  Pallas kernels  7.89 us (7%)
  starting transfers between devices  2.4 us (2%)
  waiting for transfers between devices  1.32 us (1%)
    all_to_all x1, blocking collectives, on_device(): both = lax.all_to_all(both, AXES, split_axis=0, concat_axis=0)  47 us
    all_to_all x2, blocking collectives, exchange(): lax.all_to_all(parts, AXES, split_axis=0, concat_axis=0).reshape(part.shape)  27.4 us
    all_to_all x1, blocking collectives, on_device(): moved = lax.all_to_all(moved, AXES, split_axis=0, concat_axis=0)  25.5 us
    pallas_call x1, Pallas kernels, on_device(): pl.pallas_call(sweep_kernel, out_shape=(jax.ShapeDtypeStruct((devices, ow...  3.57 us
    ppermute x2, starting transfers between devices, other_core(): lax.ppermute(parts, 'dim', [(k, k ^ 1) for k in range(lax.axis_size('dim'...  2.4 us
  transfers between devices with their start and end apart: 2, of which 2 were waited for; matrix products, arithmetic and copies ran while one was open for 0% of the time, Pallas kernels for 1%

profile of v13, /device:TPU:1, one launch (start us, length us, event | category | flops | bytes accessed | tf_op | source)
XLA Modules:
  0.0 112.2 jit_solution(3457865479329121544)
XLA Ops:
  0.6 1.8 %shard_map.49 = bf16[128,8,2,640]{3,2,1,0:T(2,128)(2,1)S(1)} custom-call(bf16[507,2,640]{2,1,0:T(2,128)(2,1)} %bitcast.21, bf16[507,2,640]{2,1,0:T(2,128)(2,1)} %bitcast.27), custom_call_target="tpu_custom_call" | custom-call | tf_op jit(solution)/shard_map/pallas_call | solution.py:238
  2.4 47.0 %all_to_all.20.both_ref = bf16[128,2,5120]{2,1,0:T(2,128)(2,1)S(1)} all-to-all(bf16[128,2,5120]{2,1,0:T(2,128)(2,1)S(1)} %bitcast.19), channel_id=1, replica_groups=mesh['dp'=16,'dim'=8] {'dp','dim'}, dimensions={0} | all-to-all | bytes 5242880 | tf_op jit(solution)/shard_map/all_to_all | solution.py:250
  49.5 0.7 shard_map.50
  50.2 1.4 %collective-permute-start = (f32[32,8,128]{2,1,0:T(8,128)S(1)}, f32[32,8,128]{2,1,0:T(8,128)S(1)}, u32[]{:S(2)}, u32[]{:S(2)}) collective-permute-start(f32[32,8,128]{2,1,0:T(8,128)S(1)} %get-tuple-element.17), channel_id=1, source_target_pairs={{0,1},{1,0},{2,3},{3,2},{4,5},{5,4},{6,7},{7,6},{8,9},{9,8},{10,11... | collective-permute-start | bytes 393224 | tf_op jit(solution)/shard_map/ppermute | solution.py:261
  51.6 0.0 copy-start
  51.6 0.6 shard_map.51
  52.2 0.3 collective-permute-done.second_ref
  52.6 13.2 %all_to_all.21 = f32[128,2,128]{2,1,0:T(2,128)S(1)} all-to-all(f32[128,2,128]{2,1,0:T(2,128)S(1)} %bitcast.24), channel_id=1, replica_groups=mesh['dp'=16,'dim'=8] {'dp','dim'}, dimensions={0} | all-to-all | bytes 262144 | tf_op jit(solution)/shard_map/all_to_all | solution.py:258
  65.9 14.2 %all_to_all.22 = f32[128,2,128]{2,1,0:T(2,128)S(1)} all-to-all(f32[128,2,128]{2,1,0:T(2,128)S(1)} %bitcast.26), channel_id=1, replica_groups=mesh['dp'=16,'dim'=8] {'dp','dim'}, dimensions={0} | all-to-all | bytes 262144 | tf_op jit(solution)/shard_map/all_to_all | solution.py:258
  80.1 1.0 collective-permute-start.1
  81.0 1.0 collective-permute-done.1.other_ref
  82.0 0.0 copy-done
  82.0 3.6 %shard_map.54 = (bf16[128,2,2560]{2,1,0:T(2,128)(2,1)S(1)}, f32[2,256]{1,0:T(2,128)S(1)}, f32[2,128]{1,0:T(2,128)S(1)}) custom-call(f32[32,8,128]{2,1,0:T(8,128)S(1)} %bitcast.23, f32[32,8,128]{2,1,0:T(8,128)S(1)} %collective-permute-done.1.other_ref, bf16[256,2560]{1,0:T(8,128)(2,1)S(1)} %get-tuple-element.18.data_ref, bf16[2,324480]{1,0:T(2,128)(2,1)S(1)} %copy-done), custom_call_target="tpu_custom_call" | custom-call | tf_op jit(solution)/shard_map/pallas_call | solution.py:280
  85.6 25.5 %all_to_all.23 = bf16[128,2,2560]{2,1,0:T(2,128)(2,1)S(1)} all-to-all(bf16[128,2,2560]{2,1,0:T(2,128)(2,1)S(1)} %get-tuple-element.19), channel_id=1, replica_groups=mesh['dp'=16,'dim'=8] {'dp','dim'}, dimensions={0} | all-to-all | bytes 2621440 | tf_op jit(solution)/shard_map/all_to_all | solution.py:296
  111.1 1.1 shard_map.55
  (2 shorter events, 0.1 us)
Async XLA Ops:
  50.2 2.4 %collective-permute-start = (f32[32,8,128]{2,1,0:T(8,128)S(1)}, f32[32,8,128]{2,1,0:T(8,128)S(1)}, u32[]{:S(2)}, u32[]{:S(2)}) collective-permute-start(f32[32,8,128]{2,1,0:T(8,128)S(1)} %get-tuple-element.17), channel_id=1, source_target_pairs={{0,1},{1,0},{2,3},{3,2},{4,5},{5,4},{6,7},{7,6},{8,9},{9,8},{10,11... | collective-permute-start | bytes 393224 | tf_op jit(solution)/shard_map/ppermute | solution.py:261
  51.6 30.4 %copy-start = (bf16[2,324480]{1,0:T(2,128)(2,1)S(1)}, bf16[2,324480]{1,0:T(2,128)(2,1)}, u32[]{:S(2)}) copy-start(bf16[2,324480]{1,0:T(2,128)(2,1)} %noise_ref.1) | copy-start | bytes 3893764
  80.1 2.0 %collective-permute-start.1 = (f32[32,8,128]{2,1,0:T(8,128)S(1)}, f32[32,8,128]{2,1,0:T(8,128)S(1)}, u32[]{:S(2)}, u32[]{:S(2)}) collective-permute-start(f32[32,8,128]{2,1,0:T(8,128)S(1)} %bitcast.22), channel_id=1, source_target_pairs={{0,1},{1,0},{2,3},{3,2},{4,5},{5,4},{6,7},{7,6},{8,9},{9,8},{10,11... | collective-permute-start | bytes 393224 | tf_op jit(solution)/shard_map/ppermute | solution.py:261

commit v14 on v13

--- a/solution.py
+++ b/solution.py
@@ -75,17 +75,15 @@
     return lax.rem(lax.axis_index("dim"), 2)
 
 
-def half_of(both_ref, noise, part, data_ref, out_ref):
-    rows, ent = data_ref.shape
-    pairs = rows // both_ref.shape[1]
-    data = both_ref[pl.ds(pl.multiple_of(part * pairs, pairs), pairs), :, ent:].reshape(rows, ent)
-    data_ref[...] = data
+def half_of(both_ref, noise, part, data, out_ref):
+    rows, ent = data.shape
+    data[...] = both_ref[:, part, :, ent:].reshape(rows, ent)
     gram = lax.dot_general(
-        data, noise, (((1,), (1,)), ((), ())), preferred_element_type=jnp.float32
+        data[...], noise, (((1,), (1,)), ((), ())), preferred_element_type=jnp.float32
     )
     data_sq = jnp.zeros((rows, LANES), jnp.float32)
     for start in range(0, ent, LANES):
-        wide = data_ref[:, start : start + LANES].astype(jnp.float32)
+        wide = data[:, start : start + LANES].astype(jnp.float32)
         data_sq = data_sq + wide * wide
     data_sq = jnp.sum(data_sq, axis=1, keepdims=True)
     parts = data_sq - 2.0 * gram
@@ -93,16 +91,14 @@
         out_ref[tile] = parts[span, half]
 
 
-def sent_kernel(both_ref, out_ref, noise_ref, data_ref):
-    noise_ref[...] = both_ref[:, :, : noise_ref.shape[1]].reshape(noise_ref.shape)
-    half_of(both_ref, noise_ref[...], 1 - core(), data_ref, out_ref)
-
-
-def kept_kernel(both_ref, noise_ref, other_ref, out_ref, data_ref, own):
-    rows = own.shape[0]
-    half_of(both_ref, noise_ref[...], core(), own, out_ref)
-    data_ref[pl.ds(pl.multiple_of(core() * rows, rows), rows), :] = own[...]
-    data_ref[pl.ds(pl.multiple_of((1 - core()) * rows, rows), rows), :] = other_ref[...]
+def sent_kernel(both_ref, out_ref, noise_ref, data):
+    noise_ref[...] = both_ref[:, :, :, : noise_ref.shape[1]].reshape(noise_ref.shape)
+    half_of(both_ref, noise_ref[...], 1 - core(), data, out_ref)
+
+
+def kept_kernel(both_ref, noise_ref, out_ref, data_ref, data):
+    half_of(both_ref, noise_ref[...], core(), data, out_ref)
+    data_ref[...] = both_ref[:, :, :, noise_ref.shape[1] :].reshape(data_ref.shape)
 
 
 def add_kernel(first_ref, second_ref, out_ref):
@@ -117,14 +113,13 @@
 
 
 def sweep_kernel(
-    cost_ref, other_ref, data_ref, noise_ref, out_ref, pots_ref, noise_sq_ref,
+    cost_ref, data_ref, noise_ref, out_ref, pots_ref, noise_sq_ref,
     bias, kern, row_pot, col_pot, row_sum,
 ):
-    for part, ref in ((core(), cost_ref), (1 - core(), other_ref)):
-        first = part * (BATCH // 2)
-        for tile, span, half in tiles(BATCH // 2):
-            rows = pl.ds(pl.multiple_of(first + span.start, 8), 8)
-            bias[rows, half] = ref[tile] * (-1.0 / (LATENT * BIT))
+    for tile, rows, half in tiles(BATCH):
+        block, side = tile // 2, tile % 2
+        place = 4 * (block // 2) + 2 * side + block % 2
+        bias[rows, half] = cost_ref[place] * (-1.0 / (LATENT * BIT))
     col_pot[...] = jnp.zeros_like(col_pot)
 
     def log_sweep():
@@ -250,31 +245,31 @@
     both = lax.all_to_all(both, AXES, split_axis=0, concat_axis=0)
 
     part = jax.ShapeDtypeStruct((devices // 4, 8, LANES), jnp.float32)
-    data_half = jax.ShapeDtypeStruct((BATCH // 2, ent), data.dtype)
+    whole = jax.ShapeDtypeStruct((devices // 2, 8, LANES), jnp.float32)
     data_whole = jax.ShapeDtypeStruct((BATCH, ent), data.dtype)
+    data_half = pltpu.VMEM((BATCH // 2, ent), data.dtype)
 
     def exchange(parts):
-        parts = parts.reshape(devices, 2, LANES)
-        return lax.all_to_all(parts, AXES, split_axis=0, concat_axis=0).reshape(part.shape)
-
-    def other_core(parts):
-        return lax.ppermute(parts, "dim", [(k, k ^ 1) for k in range(lax.axis_size("dim"))])
-
-    sent, noise_ent, data_other = pl.pallas_call(
-        sent_kernel, out_shape=(part, data_whole, data_half), compiler_params=params
+        shape = parts.shape
+        parts = parts.reshape(devices, -1, LANES)
+        return lax.all_to_all(parts, AXES, split_axis=0, concat_axis=0).reshape(shape)
+
+    both = both.reshape(devices // 2, 2, own, 2 * ent)
+    sent, noise_ent = pl.pallas_call(
+        sent_kernel, out_shape=(part, data_whole), scratch_shapes=[data_half], compiler_params=params
     )(both)
-    got = other_core(sent)
+    got = lax.ppermute(sent, "dim", [(k, k ^ 1) for k in range(lax.axis_size("dim"))])
     kept, data_ent = pl.pallas_call(
         kept_kernel,
         out_shape=(part, data_whole),
-        scratch_shapes=[pltpu.VMEM(data_half.shape, data_half.dtype)],
+        scratch_shapes=[data_half],
         compiler_params=params,
         cost_estimate=pl.CostEstimate(
             flops=BATCH * BATCH * ent, bytes_accessed=6 * BATCH * ent, transcendentals=0
         ),
-    )(both, noise_ent, data_other)
+    )(both, noise_ent)
     parts = pl.pallas_call(add_kernel, out_shape=part, compiler_params=params)(kept, got)
-    total = pl.pallas_call(sum_kernel, out_shape=part, compiler_params=params)(exchange(parts))
+    total = pl.pallas_call(sum_kernel, out_shape=whole, compiler_params=params)(exchange(parts))
     total = exchange(total)
 
     moved, pots, noise_sq = pl.pallas_call(
@@ -292,7 +287,7 @@
             pltpu.VMEM((1, BATCH), jnp.float32),
         ],
         compiler_params=params,
-    )(total, other_core(total), data_ent, noise)
+    )(total, data_ent, noise)
     moved = lax.all_to_all(moved, AXES, split_axis=0, concat_axis=0)
     moved = moved.reshape(devices, own, UNITS, UNIT).transpose(0, 2, 1, 3)
     in_vmem = pl.BlockSpec(memory_space=pltpu.VMEM)

time: 112 us -> 112 us (level)
  blocking collectives: 99.9 us -> 102 us
    ppermute x2 -> x1, starting transfers between devices: 2.4 us -> 1.45 us  [on_device(): lax.ppermute(sent, 'dim', [(k, k ^ 1) for k in range(lax.axis_size('dim'))])]
  transfers between devices with their start and end apart: 2 -> 1, of which waited for: 2 -> 1; matrix products, arithmetic and copies ran while one was open for 0% -> 0% of each run, Pallas kernels for 1% -> 1%
where the time goes in v14:
time: 112 us
  blocking collectives  102 us (91%)
  Pallas kernels  7.96 us (7%)
  starting transfers between devices  1.45 us (1%)
    all_to_all x1, blocking collectives, on_device(): both = lax.all_to_all(both, AXES, split_axis=0, concat_axis=0)  47 us
    all_to_all x2, blocking collectives, exchange(): lax.all_to_all(parts, AXES, split_axis=0, concat_axis=0).reshape(shape)  28.4 us
    all_to_all x1, blocking collectives, on_device(): moved = lax.all_to_all(moved, AXES, split_axis=0, concat_axis=0)  26.2 us
    pallas_call x1, Pallas kernels, on_device(): pl.pallas_call(sweep_kernel, out_shape=(jax.ShapeDtypeStruct((devices, ow...  3.57 us
  transfers between devices with their start and end apart: 1, of which 1 were waited for; matrix products, arithmetic and copies ran while one was open for 0% of the time, Pallas kernels for 1%

profile of v14, /device:TPU:1, one launch (start us, length us, event | category | flops | bytes accessed | tf_op | source)
XLA Modules:
  0.0 111.9 jit_solution(16871413039989864572)
XLA Ops:
  0.6 1.8 %shard_map.49 = bf16[128,8,2,640]{3,2,1,0:T(2,128)(2,1)S(1)} custom-call(bf16[507,2,640]{2,1,0:T(2,128)(2,1)} %bitcast.24, bf16[507,2,640]{2,1,0:T(2,128)(2,1)} %bitcast.29), custom_call_target="tpu_custom_call" | custom-call | tf_op jit(solution)/shard_map/pallas_call | solution.py:233
  2.4 47.0 %all_to_all.20 = bf16[128,2,5120]{2,1,0:T(2,128)(2,1)S(1)} all-to-all(bf16[128,2,5120]{2,1,0:T(2,128)(2,1)S(1)} %bitcast.22), channel_id=1, replica_groups=mesh['dp'=16,'dim'=8] {'dp','dim'}, dimensions={0} | all-to-all | bytes 5242880 | tf_op jit(solution)/shard_map/all_to_all | solution.py:245
  49.5 0.7 shard_map.50
  50.2 1.5 %collective-permute-start = (f32[32,8,128]{2,1,0:T(8,128)S(1)}, f32[32,8,128]{2,1,0:T(8,128)S(1)}, u32[]{:S(2)}, u32[]{:S(2)}) collective-permute-start(f32[32,8,128]{2,1,0:T(8,128)S(1)} %get-tuple-element.15), channel_id=1, source_target_pairs={{0,1},{1,0},{2,3},{3,2},{4,5},{5,4},{6,7},{7,6},{8,9},{9,8},{10,11... | collective-permute-start | bytes 393224 | tf_op jit(solution)/shard_map/ppermute | solution.py:261
  51.6 0.7 shard_map.51
  52.3 0.0 copy-start
  52.3 0.3 collective-permute-done.second_ref
  52.6 13.2 %all_to_all.21 = f32[128,2,128]{2,1,0:T(2,128)S(1)} all-to-all(f32[128,2,128]{2,1,0:T(2,128)S(1)} %bitcast.27), channel_id=1, replica_groups=mesh['dp'=16,'dim'=8] {'dp','dim'}, dimensions={0} | all-to-all | bytes 262144 | tf_op jit(solution)/shard_map/all_to_all | solution.py:255
  65.9 0.1 shard_map.53
  65.9 15.1 %all_to_all.22 = f32[128,4,128]{2,1,0:T(4,128)S(1)} all-to-all(f32[128,4,128]{2,1,0:T(4,128)S(1)} %bitcast.26), channel_id=1, replica_groups=mesh['dp'=16,'dim'=8] {'dp','dim'}, dimensions={0} | all-to-all | bytes 524288 | tf_op jit(solution)/shard_map/all_to_all | solution.py:255
  81.0 0.0 copy-done
  81.0 3.6 %shard_map.54 = (bf16[128,2,2560]{2,1,0:T(2,128)(2,1)S(1)}, f32[2,256]{1,0:T(2,128)S(1)}, f32[2,128]{1,0:T(2,128)S(1)}) custom-call(f32[64,8,128]{2,1,0:T(8,128)S(1)} %bitcast.25, bf16[256,2560]{1,0:T(8,128)(2,1)S(1)} %get-tuple-element.16.data_ref, bf16[2,324480]{1,0:T(2,128)(2,1)S(1)} %copy-done), custom_call_target="tpu_custom_call" | custom-call | tf_op jit(solution)/shard_map/pallas_call | solution.py:275
  84.6 26.2 %all_to_all.23 = bf16[128,2,2560]{2,1,0:T(2,128)(2,1)S(1)} all-to-all(bf16[128,2,2560]{2,1,0:T(2,128)(2,1)S(1)} %get-tuple-element.17), channel_id=1, replica_groups=mesh['dp'=16,'dim'=8] {'dp','dim'}, dimensions={0} | all-to-all | bytes 2621440 | tf_op jit(solution)/shard_map/all_to_all | solution.py:291
  110.8 1.1 shard_map.55
  (1 shorter events, 0.0 us)
Async XLA Ops:
  50.2 2.4 %collective-permute-start = (f32[32,8,128]{2,1,0:T(8,128)S(1)}, f32[32,8,128]{2,1,0:T(8,128)S(1)}, u32[]{:S(2)}, u32[]{:S(2)}) collective-permute-start(f32[32,8,128]{2,1,0:T(8,128)S(1)} %get-tuple-element.15), channel_id=1, source_target_pairs={{0,1},{1,0},{2,3},{3,2},{4,5},{5,4},{6,7},{7,6},{8,9},{9,8},{10,11... | collective-permute-start | bytes 393224 | tf_op jit(solution)/shard_map/ppermute | solution.py:261
  52.3 28.7 %copy-start = (bf16[2,324480]{1,0:T(2,128)(2,1)S(1)}, bf16[2,324480]{1,0:T(2,128)(2,1)}, u32[]{:S(2)}) copy-start(bf16[2,324480]{1,0:T(2,128)(2,1)} %noise_ref.1) | copy-start | bytes 3893764

commit v15 on v12

--- a/solution.py
+++ b/solution.py
@@ -102,10 +102,8 @@
 ):
     for tile, rows, half in tiles():
         bias[rows, half] = cost_ref[tile] * (-1.0 / (LATENT * BIT))
-    col_pot[...] = jnp.zeros_like(col_pot)
-
-    def log_sweep():
-        scaled = bias[...] + col_pot[...]
+
+    def log_sweep(scaled):
         top = jnp.max(scaled, axis=0, keepdims=True)
         row = -(top + jnp.log2(jnp.sum(jnp.exp2(scaled - top), axis=0, keepdims=True)))
         scaled = bias[...] + row
@@ -114,9 +112,11 @@
         total = jnp.sum(scaled, axis=1, keepdims=True)
         row_pot[...] = row
         col_pot[...] = -(top + jnp.log2(total))
-        kern[...] = scaled * (1.0 / total)
-
-    log_sweep()
+        scaled = scaled * (1.0 / total)
+        kern[...] = scaled
+        return jnp.sum(scaled, axis=0, keepdims=True)
+
+    total = log_sweep(bias[...])
 
     tile = (8, LANES)
     blocks = [pl.ds(start, 8) for start in range(0, BATCH, 8)]
@@ -126,14 +126,13 @@
         sums = [[jnp.zeros(tile, jnp.float32) for _ in halves] for _ in range(2)]
         for n, block in enumerate(blocks):
             parts = [kern[block, half] for half in halves]
-            if rows is not None:
-                total = sum(part * row for part, row in zip(parts, rows))
-                total = jnp.broadcast_to(jnp.sum(total, axis=1, keepdims=True), tile)
-                low, high = jnp.minimum(low, total), jnp.maximum(high, total)
-                factor = 1.0 / total
-                parts = [part * factor for part in parts]
-                if use is not None:
-                    use(block, factor, parts)
+            total = sum(part * row for part, row in zip(parts, rows))
+            total = jnp.broadcast_to(jnp.sum(total, axis=1, keepdims=True), tile)
+            low, high = jnp.minimum(low, total), jnp.maximum(high, total)
+            factor = 1.0 / total
+            parts = [part * factor for part in parts]
+            if use is not None:
+                use(block, factor, parts)
             for h, part in enumerate(parts):
                 sums[n % 2][h] += part
         totals = []
@@ -158,8 +157,7 @@
         low, high, totals = over_columns(low, high, rows, None)
         for total in totals:
             high = jnp.maximum(high, total)
-        if rows is not None:
-            noise_sq = squares((step - 2) * share, share, noise_sq)
+        noise_sq = squares((step - 2) * share, share, noise_sq)
         return (low, high, tuple(1.0 / total for total in totals), noise_sq)
 
     def finish(block, factor, parts):
@@ -167,8 +165,10 @@
         for half, part in zip(halves, parts):
             kern[block, half] = part
 
-    ones = jnp.ones(tile, jnp.float32)
-    carry = sweep(0, (ones, ones, None, jnp.zeros((noise_ref.shape[0], UNIT), jnp.float32)))
+    totals = [jnp.broadcast_to(total[:, half.start : half.start + LANES], tile) for half in halves]
+    low, high = jnp.minimum(*totals), jnp.maximum(*totals)
+    noise_sq = jnp.zeros((noise_ref.shape[0], UNIT), jnp.float32)
+    carry = (low, high, tuple(1.0 / total for total in totals), noise_sq)
     low, high, rows, noise_sq = lax.fori_loop(2, SWEEPS, sweep, carry)
     done = (SWEEPS - 2) * share
     noise_sq = jnp.sum(squares(done, units - done, noise_sq), axis=1, keepdims=True)
@@ -183,7 +183,7 @@
         col_pot[...] = jnp.zeros_like(col_pot)
 
         def again(step, carry):
-            log_sweep()
+            log_sweep(bias[...] + col_pot[...])
             return carry
 
         lax.fori_loop(0, SWEEPS, again, 0)

time: 112 us -> 112 us (level)
  no operation moved by 1% of the time
where the time goes in v15:
time: 112 us
  blocking collectives  104 us (93%)
  Pallas kernels  7.43 us (7%)
    all_to_all x1, blocking collectives, on_device(): both = lax.all_to_all(both, AXES, split_axis=0, concat_axis=0)  47 us
    all_to_all x2, blocking collectives, exchange(): lax.all_to_all(parts, AXES, split_axis=0, concat_axis=0)  30.5 us
    all_to_all x1, blocking collectives, on_device(): moved = lax.all_to_all(moved, AXES, split_axis=0, concat_axis=0)  26.2 us
    pallas_call x1, Pallas kernels, on_device(): pl.pallas_call(sweep_kernel, out_shape=(jax.ShapeDtypeStruct((devices, ow...  3.5 us

profile of v15, /device:TPU:1, one launch (start us, length us, event | category | flops | bytes accessed | tf_op | source)
XLA Modules:
  0.0 111.8 jit_solution(18083261295530384067)
XLA Ops:
  0.6 1.8 %shard_map.49 = bf16[128,8,2,640]{3,2,1,0:T(2,128)(2,1)S(1)} custom-call(bf16[507,2,640]{2,1,0:T(2,128)(2,1)} %bitcast.21, bf16[507,2,640]{2,1,0:T(2,128)(2,1)} %bitcast.26), custom_call_target="tpu_custom_call" | custom-call | tf_op jit(solution)/shard_map/pallas_call | solution.py:215
  2.4 47.0 %all_to_all.20.both_ref = bf16[128,2,5120]{2,1,0:T(2,128)(2,1)S(1)} all-to-all(bf16[128,2,5120]{2,1,0:T(2,128)(2,1)S(1)} %bitcast.19), channel_id=1, replica_groups=mesh['dp'=16,'dim'=8] {'dp','dim'}, dimensions={0} | all-to-all | bytes 5242880 | tf_op jit(solution)/shard_map/all_to_all | solution.py:227
  49.5 0.9 shard_map.50
  50.4 0.0 copy-start
  50.4 15.3 %all_to_all.21 = f32[128,4,128]{2,1,0:T(4,128)S(1)} all-to-all(f32[128,4,128]{2,1,0:T(4,128)S(1)} %bitcast.25), channel_id=1, replica_groups=mesh['dp'=16,'dim'=8] {'dp','dim'}, dimensions={0} | all-to-all | bytes 524288 | tf_op jit(solution)/shard_map/all_to_all | solution.py:233
  65.7 0.1 shard_map.51
  65.8 15.2 %all_to_all.22 = f32[128,4,128]{2,1,0:T(4,128)S(1)} all-to-all(f32[128,4,128]{2,1,0:T(4,128)S(1)} %bitcast.24), channel_id=1, replica_groups=mesh['dp'=16,'dim'=8] {'dp','dim'}, dimensions={0} | all-to-all | bytes 524288 | tf_op jit(solution)/shard_map/all_to_all | solution.py:233
  81.0 0.0 copy-done
  81.0 3.5 %shard_map.52 = (bf16[128,2,2560]{2,1,0:T(2,128)(2,1)S(1)}, f32[2,256]{1,0:T(2,128)S(1)}, f32[2,128]{1,0:T(2,128)S(1)}) custom-call(f32[64,8,128]{2,1,0:T(8,128)S(1)} %bitcast.22, bf16[256,2560]{1,0:T(8,128)(2,1)S(1)} %get-tuple-element.12.data_ref, bf16[2,324480]{1,0:T(2,128)(2,1)S(1)} %copy-done), custom_call_target="tpu_custom_call" | custom-call | tf_op jit(solution)/shard_map/pallas_call | solution.py:243
  84.5 26.2 %all_to_all.23 = bf16[128,2,2560]{2,1,0:T(2,128)(2,1)S(1)} all-to-all(bf16[128,2,2560]{2,1,0:T(2,128)(2,1)S(1)} %get-tuple-element.13), channel_id=1, replica_groups=mesh['dp'=16,'dim'=8] {'dp','dim'}, dimensions={0} | all-to-all | bytes 2621440 | tf_op jit(solution)/shard_map/all_to_all | solution.py:259
  110.7 1.1 shard_map.53
Async XLA Ops:
  50.4 30.6 %copy-start = (bf16[2,324480]{1,0:T(2,128)(2,1)S(1)}, bf16[2,324480]{1,0:T(2,128)(2,1)}, u32[]{:S(2)}) copy-start(bf16[2,324480]{1,0:T(2,128)(2,1)} %noise_ref.1) | copy-start | bytes 3893764

commit v16 on v15

--- a/solution.py
+++ b/solution.py
@@ -73,12 +73,10 @@
 
 def gram_kernel(both_ref, out_ref, data_ref):
     ent = data_ref.shape[1]
-    noise = both_ref[:, :, :ent].reshape(data_ref.shape)
+    noise = jnp.transpose(both_ref[:, :, :ent].reshape(data_ref.shape))
     data = both_ref[:, :, ent:].reshape(data_ref.shape)
     data_ref[...] = data
-    gram = lax.dot_general(
-        data, noise, (((1,), (1,)), ((), ())), preferred_element_type=jnp.float32
-    )
+    gram = jnp.dot(data, noise, preferred_element_type=jnp.float32)
     data_sq = jnp.zeros((BATCH, LANES), jnp.float32)
     for start in range(0, ent, LANES):
         wide = data_ref[:, start : start + LANES].astype(jnp.float32)
@@ -178,6 +176,15 @@
     row_sum[...] = jnp.concatenate([total[:1] for total in totals], axis=1)
     near = jnp.min(jnp.where((low >= 1.0 / DRIFT) & (high <= DRIFT), 1.0, 0.0)) > 0.5
 
+    def targets():
+        weights = (kern[...] * (1.0 / row_sum[...])).astype(jnp.bfloat16)
+        moved = lax.dot_general(
+            weights, data_ref[...], (((0,), (0,)), ((), ())), preferred_element_type=jnp.float32
+        )
+        out_ref[...] = moved.astype(jnp.bfloat16).reshape(out_ref.shape)
+
+    targets()
+
     @pl.when(jnp.logical_not(near))
     def _():
         col_pot[...] = jnp.zeros_like(col_pot)
@@ -191,12 +198,8 @@
         scaled = jnp.exp2(scaled - jnp.max(scaled, axis=0, keepdims=True))
         kern[...] = scaled
         row_sum[...] = jnp.sum(scaled, axis=0, keepdims=True)
-
-    weights = (kern[...] * (1.0 / row_sum[...])).astype(jnp.bfloat16)
-    moved = lax.dot_general(
-        weights, data_ref[...], (((0,), (0,)), ((), ())), preferred_element_type=jnp.float32
-    )
-    out_ref[...] = moved.astype(jnp.bfloat16).reshape(out_ref.shape)
+        targets()
+
     pots_ref[0:1, :] = row_pot[...] * BIT
     pots_ref[1:2, :] = jnp.transpose(col_pot[...] * BIT)
 

time: 112 us -> 112 us (level)
  no operation moved by 1% of the time
where the time goes in v16:
time: 112 us
  blocking collectives  104 us (93%)
  Pallas kernels  7.4 us (7%)
    all_to_all x1, blocking collectives, on_device(): both = lax.all_to_all(both, AXES, split_axis=0, concat_axis=0)  47 us
    all_to_all x2, blocking collectives, exchange(): lax.all_to_all(parts, AXES, split_axis=0, concat_axis=0)  30.5 us
    all_to_all x1, blocking collectives, on_device(): moved = lax.all_to_all(moved, AXES, split_axis=0, concat_axis=0)  26.2 us
    pallas_call x1, Pallas kernels, on_device(): pl.pallas_call(sweep_kernel, out_shape=(jax.ShapeDtypeStruct((devices, ow...  3.46 us

profile of v16, /device:TPU:1, one launch (start us, length us, event | category | flops | bytes accessed | tf_op | source)
XLA Modules:
  0.0 111.8 jit_solution(10303783664807687622)
XLA Ops:
  0.6 1.8 %shard_map.49 = bf16[128,8,2,640]{3,2,1,0:T(2,128)(2,1)S(1)} custom-call(bf16[507,2,640]{2,1,0:T(2,128)(2,1)} %bitcast.21, bf16[507,2,640]{2,1,0:T(2,128)(2,1)} %bitcast.26), custom_call_target="tpu_custom_call" | custom-call | tf_op jit(solution)/shard_map/pallas_call | solution.py:218
  2.4 47.0 %all_to_all.20.both_ref = bf16[128,2,5120]{2,1,0:T(2,128)(2,1)S(1)} all-to-all(bf16[128,2,5120]{2,1,0:T(2,128)(2,1)S(1)} %bitcast.19), channel_id=1, replica_groups=mesh['dp'=16,'dim'=8] {'dp','dim'}, dimensions={0} | all-to-all | bytes 5242880 | tf_op jit(solution)/shard_map/all_to_all | solution.py:230
  49.5 0.9 shard_map.50
  50.4 0.0 copy-start
  50.4 15.3 %all_to_all.21 = f32[128,4,128]{2,1,0:T(4,128)S(1)} all-to-all(f32[128,4,128]{2,1,0:T(4,128)S(1)} %bitcast.25), channel_id=1, replica_groups=mesh['dp'=16,'dim'=8] {'dp','dim'}, dimensions={0} | all-to-all | bytes 524288 | tf_op jit(solution)/shard_map/all_to_all | solution.py:236
  65.7 0.1 shard_map.51
  65.8 15.2 %all_to_all.22 = f32[128,4,128]{2,1,0:T(4,128)S(1)} all-to-all(f32[128,4,128]{2,1,0:T(4,128)S(1)} %bitcast.24), channel_id=1, replica_groups=mesh['dp'=16,'dim'=8] {'dp','dim'}, dimensions={0} | all-to-all | bytes 524288 | tf_op jit(solution)/shard_map/all_to_all | solution.py:236
  81.0 0.0 copy-done
  81.0 3.5 %shard_map.52 = (bf16[128,2,2560]{2,1,0:T(2,128)(2,1)S(1)}, f32[2,256]{1,0:T(2,128)S(1)}, f32[2,128]{1,0:T(2,128)S(1)}) custom-call(f32[64,8,128]{2,1,0:T(8,128)S(1)} %bitcast.22, bf16[256,2560]{1,0:T(8,128)(2,1)S(1)} %get-tuple-element.12.data_ref, bf16[2,324480]{1,0:T(2,128)(2,1)S(1)} %copy-done), custom_call_target="tpu_custom_call" | custom-call | tf_op jit(solution)/shard_map/pallas_call | solution.py:246
  84.5 26.2 %all_to_all.23 = bf16[128,2,2560]{2,1,0:T(2,128)(2,1)S(1)} all-to-all(bf16[128,2,2560]{2,1,0:T(2,128)(2,1)S(1)} %get-tuple-element.13), channel_id=1, replica_groups=mesh['dp'=16,'dim'=8] {'dp','dim'}, dimensions={0} | all-to-all | bytes 2621440 | tf_op jit(solution)/shard_map/all_to_all | solution.py:262
  110.7 1.1 shard_map.53
Async XLA Ops:
  50.4 30.6 %copy-start = (bf16[2,324480]{1,0:T(2,128)(2,1)S(1)}, bf16[2,324480]{1,0:T(2,128)(2,1)}, u32[]{:S(2)}) copy-start(bf16[2,324480]{1,0:T(2,128)(2,1)} %noise_ref.1) | copy-start | bytes 3893764

commit v17 on v16

--- a/solution.py
+++ b/solution.py
@@ -74,9 +74,8 @@
 def gram_kernel(both_ref, out_ref, data_ref):
     ent = data_ref.shape[1]
     noise = jnp.transpose(both_ref[:, :, :ent].reshape(data_ref.shape))
-    data = both_ref[:, :, ent:].reshape(data_ref.shape)
-    data_ref[...] = data
-    gram = jnp.dot(data, noise, preferred_element_type=jnp.float32)
+    data_ref[...] = both_ref[:, :, ent:].reshape(data_ref.shape)
+    gram = jnp.dot(data_ref[...], noise, preferred_element_type=jnp.float32)
     data_sq = jnp.zeros((BATCH, LANES), jnp.float32)
     for start in range(0, ent, LANES):
         wide = data_ref[:, start : start + LANES].astype(jnp.float32)

time: 112 us -> 112 us (level)
  no operation moved by 1% of the time
where the time goes in v17:
time: 112 us
  blocking collectives  104 us (93%)
  Pallas kernels  7.27 us (6%)
    all_to_all x1, blocking collectives, on_device(): both = lax.all_to_all(both, AXES, split_axis=0, concat_axis=0)  47 us
    all_to_all x2, blocking collectives, exchange(): lax.all_to_all(parts, AXES, split_axis=0, concat_axis=0)  30.5 us
    all_to_all x1, blocking collectives, on_device(): moved = lax.all_to_all(moved, AXES, split_axis=0, concat_axis=0)  26.2 us
    pallas_call x1, Pallas kernels, on_device(): pl.pallas_call(sweep_kernel, out_shape=(jax.ShapeDtypeStruct((devices, ow...  3.46 us

profile of v17, /device:TPU:1, one launch (start us, length us, event | category | flops | bytes accessed | tf_op | source)
XLA Modules:
  0.0 111.7 jit_solution(14591071629766609389)
XLA Ops:
  0.6 1.8 %shard_map.49 = bf16[128,8,2,640]{3,2,1,0:T(2,128)(2,1)S(1)} custom-call(bf16[507,2,640]{2,1,0:T(2,128)(2,1)} %bitcast.21, bf16[507,2,640]{2,1,0:T(2,128)(2,1)} %bitcast.26), custom_call_target="tpu_custom_call" | custom-call | tf_op jit(solution)/shard_map/pallas_call | solution.py:217
  2.4 47.0 %all_to_all.20.both_ref = bf16[128,2,5120]{2,1,0:T(2,128)(2,1)S(1)} all-to-all(bf16[128,2,5120]{2,1,0:T(2,128)(2,1)S(1)} %bitcast.19), channel_id=1, replica_groups=mesh['dp'=16,'dim'=8] {'dp','dim'}, dimensions={0} | all-to-all | bytes 5242880 | tf_op jit(solution)/shard_map/all_to_all | solution.py:229
  49.5 0.8 shard_map.50
  50.3 0.0 copy-start
  50.3 15.3 %all_to_all.21 = f32[128,4,128]{2,1,0:T(4,128)S(1)} all-to-all(f32[128,4,128]{2,1,0:T(4,128)S(1)} %bitcast.25), channel_id=1, replica_groups=mesh['dp'=16,'dim'=8] {'dp','dim'}, dimensions={0} | all-to-all | bytes 524288 | tf_op jit(solution)/shard_map/all_to_all | solution.py:235
  65.6 0.1 shard_map.51
  65.7 15.2 %all_to_all.22 = f32[128,4,128]{2,1,0:T(4,128)S(1)} all-to-all(f32[128,4,128]{2,1,0:T(4,128)S(1)} %bitcast.24), channel_id=1, replica_groups=mesh['dp'=16,'dim'=8] {'dp','dim'}, dimensions={0} | all-to-all | bytes 524288 | tf_op jit(solution)/shard_map/all_to_all | solution.py:235
  80.9 0.0 copy-done
  80.9 3.5 %shard_map.52 = (bf16[128,2,2560]{2,1,0:T(2,128)(2,1)S(1)}, f32[2,256]{1,0:T(2,128)S(1)}, f32[2,128]{1,0:T(2,128)S(1)}) custom-call(f32[64,8,128]{2,1,0:T(8,128)S(1)} %bitcast.22, bf16[256,2560]{1,0:T(8,128)(2,1)S(1)} %get-tuple-element.12.data_ref, bf16[2,324480]{1,0:T(2,128)(2,1)S(1)} %copy-done), custom_call_target="tpu_custom_call" | custom-call | tf_op jit(solution)/shard_map/pallas_call | solution.py:245
  84.4 26.2 %all_to_all.23 = bf16[128,2,2560]{2,1,0:T(2,128)(2,1)S(1)} all-to-all(bf16[128,2,2560]{2,1,0:T(2,128)(2,1)S(1)} %get-tuple-element.13), channel_id=1, replica_groups=mesh['dp'=16,'dim'=8] {'dp','dim'}, dimensions={0} | all-to-all | bytes 2621440 | tf_op jit(solution)/shard_map/all_to_all | solution.py:261
  110.6 1.1 shard_map.53
Async XLA Ops:
  50.3 30.6 %copy-start = (bf16[2,324480]{1,0:T(2,128)(2,1)S(1)}, bf16[2,324480]{1,0:T(2,128)(2,1)}, u32[]{:S(2)}) copy-start(bf16[2,324480]{1,0:T(2,128)(2,1)} %noise_ref.1) | copy-start | bytes 3893764

commit v18 on v14

--- a/solution.py
+++ b/solution.py
@@ -78,9 +78,7 @@
 def half_of(both_ref, noise, part, data, out_ref):
     rows, ent = data.shape
     data[...] = both_ref[:, part, :, ent:].reshape(rows, ent)
-    gram = lax.dot_general(
-        data[...], noise, (((1,), (1,)), ((), ())), preferred_element_type=jnp.float32
-    )
+    gram = jnp.dot(data[...], noise, preferred_element_type=jnp.float32)
     data_sq = jnp.zeros((rows, LANES), jnp.float32)
     for start in range(0, ent, LANES):
         wide = data[:, start : start + LANES].astype(jnp.float32)
@@ -92,13 +90,14 @@
 
 
 def sent_kernel(both_ref, out_ref, noise_ref, data):
-    noise_ref[...] = both_ref[:, :, :, : noise_ref.shape[1]].reshape(noise_ref.shape)
+    ent = noise_ref.shape[0]
+    noise_ref[...] = jnp.transpose(both_ref[:, :, :, :ent].reshape(BATCH, ent))
     half_of(both_ref, noise_ref[...], 1 - core(), data, out_ref)
 
 
 def kept_kernel(both_ref, noise_ref, out_ref, data_ref, data):
     half_of(both_ref, noise_ref[...], core(), data, out_ref)
-    data_ref[...] = both_ref[:, :, :, noise_ref.shape[1] :].reshape(data_ref.shape)
+    data_ref[...] = both_ref[:, :, :, data_ref.shape[1] :].reshape(data_ref.shape)
 
 
 def add_kernel(first_ref, second_ref, out_ref):
@@ -120,10 +119,8 @@
         block, side = tile // 2, tile % 2
         place = 4 * (block // 2) + 2 * side + block % 2
         bias[rows, half] = cost_ref[place] * (-1.0 / (LATENT * BIT))
-    col_pot[...] = jnp.zeros_like(col_pot)
-
-    def log_sweep():
-        scaled = bias[...] + col_pot[...]
+
+    def log_sweep(scaled):
         top = jnp.max(scaled, axis=0, keepdims=True)
         row = -(top + jnp.log2(jnp.sum(jnp.exp2(scaled - top), axis=0, keepdims=True)))
         scaled = bias[...] + row
@@ -132,9 +129,11 @@
         total = jnp.sum(scaled, axis=1, keepdims=True)
         row_pot[...] = row
         col_pot[...] = -(top + jnp.log2(total))
-        kern[...] = scaled * (1.0 / total)
-
-    log_sweep()
+        scaled = scaled * (1.0 / total)
+        kern[...] = scaled
+        return jnp.sum(scaled, axis=0, keepdims=True)
+
+    total = log_sweep(bias[...])
 
     tile = (8, LANES)
     blocks = [pl.ds(start, 8) for start in range(0, BATCH, 8)]
@@ -144,14 +143,13 @@
         sums = [[jnp.zeros(tile, jnp.float32) for _ in halves] for _ in range(2)]
         for n, block in enumerate(blocks):
             parts = [kern[block, half] for half in halves]
-            if rows is not None:
-                total = sum(part * row for part, row in zip(parts, rows))
-                total = jnp.broadcast_to(jnp.sum(total, axis=1, keepdims=True), tile)
-                low, high = jnp.minimum(low, total), jnp.maximum(high, total)
-                factor = 1.0 / total
-                parts = [part * factor for part in parts]
-                if use is not None:
-                    use(block, factor, parts)
+            total = sum(part * row for part, row in zip(parts, rows))
+            total = jnp.broadcast_to(jnp.sum(total, axis=1, keepdims=True), tile)
+            low, high = jnp.minimum(low, total), jnp.maximum(high, total)
+            factor = 1.0 / total
+            parts = [part * factor for part in parts]
+            if use is not None:
+                use(block, factor, parts)
             for h, part in enumerate(parts):
                 sums[n % 2][h] += part
         totals = []
@@ -176,8 +174,7 @@
         low, high, totals = over_columns(low, high, rows, None)
         for total in totals:
             high = jnp.maximum(high, total)
-        if rows is not None:
-            noise_sq = squares((step - 2) * share, share, noise_sq)
+        noise_sq = squares((step - 2) * share, share, noise_sq)
         return (low, high, tuple(1.0 / total for total in totals), noise_sq)
 
     def finish(block, factor, parts):
@@ -185,8 +182,10 @@
         for half, part in zip(halves, parts):
             kern[block, half] = part
 
-    ones = jnp.ones(tile, jnp.float32)
-    carry = sweep(0, (ones, ones, None, jnp.zeros((noise_ref.shape[0], UNIT), jnp.float32)))
+    totals = [jnp.broadcast_to(total[:, half.start : half.start + LANES], tile) for half in halves]
+    low, high = jnp.minimum(*totals), jnp.maximum(*totals)
+    noise_sq = jnp.zeros((noise_ref.shape[0], UNIT), jnp.float32)
+    carry = (low, high, tuple(1.0 / total for total in totals), noise_sq)
     low, high, rows, noise_sq = lax.fori_loop(2, SWEEPS, sweep, carry)
     done = (SWEEPS - 2) * share
     noise_sq = jnp.sum(squares(done, units - done, noise_sq), axis=1, keepdims=True)
@@ -196,12 +195,21 @@
     row_sum[...] = jnp.concatenate([total[:1] for total in totals], axis=1)
     near = jnp.min(jnp.where((low >= 1.0 / DRIFT) & (high <= DRIFT), 1.0, 0.0)) > 0.5
 
+    def targets():
+        weights = (kern[...] * (1.0 / row_sum[...])).astype(jnp.bfloat16)
+        moved = lax.dot_general(
+            weights, data_ref[...], (((0,), (0,)), ((), ())), preferred_element_type=jnp.float32
+        )
+        out_ref[...] = moved.astype(jnp.bfloat16).reshape(out_ref.shape)
+
+    targets()
+
     @pl.when(jnp.logical_not(near))
     def _():
         col_pot[...] = jnp.zeros_like(col_pot)
 
         def again(step, carry):
-            log_sweep()
+            log_sweep(bias[...] + col_pot[...])
             return carry
 
         lax.fori_loop(0, SWEEPS, again, 0)
@@ -209,12 +217,8 @@
         scaled = jnp.exp2(scaled - jnp.max(scaled, axis=0, keepdims=True))
         kern[...] = scaled
         row_sum[...] = jnp.sum(scaled, axis=0, keepdims=True)
-
-    weights = (kern[...] * (1.0 / row_sum[...])).astype(jnp.bfloat16)
-    moved = lax.dot_general(
-        weights, data_ref[...], (((0,), (0,)), ((), ())), preferred_element_type=jnp.float32
-    )
-    out_ref[...] = moved.astype(jnp.bfloat16).reshape(out_ref.shape)
+        targets()
+
     pots_ref[0:1, :] = row_pot[...] * BIT
     pots_ref[1:2, :] = jnp.transpose(col_pot[...] * BIT)
 
@@ -247,6 +251,7 @@
     part = jax.ShapeDtypeStruct((devices // 4, 8, LANES), jnp.float32)
     whole = jax.ShapeDtypeStruct((devices // 2, 8, LANES), jnp.float32)
     data_whole = jax.ShapeDtypeStruct((BATCH, ent), data.dtype)
+    noise_whole = jax.ShapeDtypeStruct((ent, BATCH), noise.dtype)
     data_half = pltpu.VMEM((BATCH // 2, ent), data.dtype)
 
     def exchange(parts):
@@ -256,7 +261,7 @@
 
     both = both.reshape(devices // 2, 2, own, 2 * ent)
     sent, noise_ent = pl.pallas_call(
-        sent_kernel, out_shape=(part, data_whole), scratch_shapes=[data_half], compiler_params=params
+        sent_kernel, out_shape=(part, noise_whole), scratch_shapes=[data_half], compiler_params=params
     )(both)
     got = lax.ppermute(sent, "dim", [(k, k ^ 1) for k in range(lax.axis_size("dim"))])
     kept, data_ent = pl.pallas_call(

time: 112 us -> 112 us (level)
  no operation moved by 1% of the time
where the time goes in v18:
time: 112 us
  blocking collectives  102 us (91%)
  Pallas kernels  7.77 us (7%)
  starting transfers between devices  1.44 us (1%)
    all_to_all x1, blocking collectives, on_device(): both = lax.all_to_all(both, AXES, split_axis=0, concat_axis=0)  47 us
    all_to_all x2, blocking collectives, exchange(): lax.all_to_all(parts, AXES, split_axis=0, concat_axis=0).reshape(shape)  28.4 us
    all_to_all x1, blocking collectives, on_device(): moved = lax.all_to_all(moved, AXES, split_axis=0, concat_axis=0)  26.2 us
    pallas_call x1, Pallas kernels, on_device(): pl.pallas_call(sweep_kernel, out_shape=(jax.ShapeDtypeStruct((devices, ow...  3.46 us
  transfers between devices with their start and end apart: 1, of which 1 were waited for; matrix products, arithmetic and copies ran while one was open for 0% of the time, Pallas kernels for 1%

profile of v18, /device:TPU:1, one launch (start us, length us, event | category | flops | bytes accessed | tf_op | source)
XLA Modules:
  0.0 111.9 jit_solution(12995640196959393383)
XLA Ops:
  0.6 1.8 %shard_map.49 = bf16[128,8,2,640]{3,2,1,0:T(2,128)(2,1)S(1)} custom-call(bf16[507,2,640]{2,1,0:T(2,128)(2,1)} %bitcast.24, bf16[507,2,640]{2,1,0:T(2,128)(2,1)} %bitcast.29), custom_call_target="tpu_custom_call" | custom-call | tf_op jit(solution)/shard_map/pallas_call | solution.py:237
  2.4 47.0 %all_to_all.20 = bf16[128,2,5120]{2,1,0:T(2,128)(2,1)S(1)} all-to-all(bf16[128,2,5120]{2,1,0:T(2,128)(2,1)S(1)} %bitcast.22), channel_id=1, replica_groups=mesh['dp'=16,'dim'=8] {'dp','dim'}, dimensions={0} | all-to-all | bytes 5242880 | tf_op jit(solution)/shard_map/all_to_all | solution.py:249
  49.5 0.7 shard_map.50
  50.2 1.4 %collective-permute-start = (f32[32,8,128]{2,1,0:T(8,128)S(1)}, f32[32,8,128]{2,1,0:T(8,128)S(1)}, u32[]{:S(2)}, u32[]{:S(2)}) collective-permute-start(f32[32,8,128]{2,1,0:T(8,128)S(1)} %get-tuple-element.15), channel_id=1, source_target_pairs={{0,1},{1,0},{2,3},{3,2},{4,5},{5,4},{6,7},{7,6},{8,9},{9,8},{10,11... | collective-permute-start | bytes 393224 | tf_op jit(solution)/shard_map/ppermute | solution.py:266
  51.6 0.6 shard_map.51
  52.2 0.0 copy-start
  52.3 0.4 collective-permute-done.second_ref
  52.7 13.2 %all_to_all.21 = f32[128,2,128]{2,1,0:T(2,128)S(1)} all-to-all(f32[128,2,128]{2,1,0:T(2,128)S(1)} %bitcast.27), channel_id=1, replica_groups=mesh['dp'=16,'dim'=8] {'dp','dim'}, dimensions={0} | all-to-all | bytes 262144 | tf_op jit(solution)/shard_map/all_to_all | solution.py:260
  65.9 0.1 shard_map.53
  65.9 15.1 %all_to_all.22 = f32[128,4,128]{2,1,0:T(4,128)S(1)} all-to-all(f32[128,4,128]{2,1,0:T(4,128)S(1)} %bitcast.26), channel_id=1, replica_groups=mesh['dp'=16,'dim'=8] {'dp','dim'}, dimensions={0} | all-to-all | bytes 524288 | tf_op jit(solution)/shard_map/all_to_all | solution.py:260
  81.1 0.0 copy-done
  81.1 3.5 %shard_map.54 = (bf16[128,2,2560]{2,1,0:T(2,128)(2,1)S(1)}, f32[2,256]{1,0:T(2,128)S(1)}, f32[2,128]{1,0:T(2,128)S(1)}) custom-call(f32[64,8,128]{2,1,0:T(8,128)S(1)} %bitcast.25, bf16[256,2560]{1,0:T(8,128)(2,1)S(1)} %get-tuple-element.16.data_ref, bf16[2,324480]{1,0:T(2,128)(2,1)S(1)} %copy-done), custom_call_target="tpu_custom_call" | custom-call | tf_op jit(solution)/shard_map/pallas_call | solution.py:280
  84.5 26.2 %all_to_all.23 = bf16[128,2,2560]{2,1,0:T(2,128)(2,1)S(1)} all-to-all(bf16[128,2,2560]{2,1,0:T(2,128)(2,1)S(1)} %get-tuple-element.17), channel_id=1, replica_groups=mesh['dp'=16,'dim'=8] {'dp','dim'}, dimensions={0} | all-to-all | bytes 2621440 | tf_op jit(solution)/shard_map/all_to_all | solution.py:296
  110.8 1.1 shard_map.55
  (1 shorter events, 0.0 us)
Async XLA Ops:
  50.2 2.4 %collective-permute-start = (f32[32,8,128]{2,1,0:T(8,128)S(1)}, f32[32,8,128]{2,1,0:T(8,128)S(1)}, u32[]{:S(2)}, u32[]{:S(2)}) collective-permute-start(f32[32,8,128]{2,1,0:T(8,128)S(1)} %get-tuple-element.15), channel_id=1, source_target_pairs={{0,1},{1,0},{2,3},{3,2},{4,5},{5,4},{6,7},{7,6},{8,9},{9,8},{10,11... | collective-permute-start | bytes 393224 | tf_op jit(solution)/shard_map/ppermute | solution.py:266
  52.2 28.8 %copy-start = (bf16[2,324480]{1,0:T(2,128)(2,1)S(1)}, bf16[2,324480]{1,0:T(2,128)(2,1)}, u32[]{:S(2)}) copy-start(bf16[2,324480]{1,0:T(2,128)(2,1)} %noise_ref.1) | copy-start | bytes 3893764

commit v19 on v17

--- a/solution.py
+++ b/solution.py
@@ -39,7 +39,10 @@
         copy.wait()
 
 
-def unpack_kernel(moved_ref, pots_ref, noise_sq_ref, out_ref, row_ref, col_ref, row, col, sems):
+def unpack_kernel(
+    moved_ref, row_pot_ref, row_fac_ref, col_pot_ref, col_fac_ref, noise_sq_ref,
+    out_ref, row_ref, col_ref, row, col, sems,
+):
     devices, units = moved_ref.shape[0], out_ref.shape[0]
     own = out_ref.shape[1]
     copies = []
@@ -53,12 +56,14 @@
         copy.start()
 
     first = (lax.axis_index("dp") * lax.axis_size("dim") + lax.axis_index("dim")) * own
-    lane = lax.broadcasted_iota(jnp.int32, (1, BATCH), 1)
+    row_pot = (row_pot_ref[...] + jnp.log2(row_fac_ref[...])) * BIT
+    col_pot = (col_pot_ref[...] + jnp.log2(col_fac_ref[...])) * BIT
+    lane = lax.broadcasted_iota(jnp.int32, row_pot.shape, 1)
+    sublane = lax.broadcasted_iota(jnp.int32, col_pot.shape, 0)
     for n in range(own):
-        mine = lane == first + n
-        row_pot = jnp.sum(jnp.where(mine, pots_ref[0:1, :], 0.0))
-        row[n] = row_pot + jnp.max(noise_sq_ref[n : n + 1, :]) / LATENT
-        col[n] = jnp.sum(jnp.where(mine, pots_ref[1:2, :], 0.0))
+        mine = jnp.sum(jnp.where(lane == first + n, row_pot, 0.0))
+        row[n] = mine + jnp.max(noise_sq_ref[n : n + 1, :]) / LATENT
+        col[n] = jnp.sum(jnp.where(sublane == first + n, col_pot, 0.0))
     for copy in copies[UNITS:]:
         copy.start()
     for copy in copies:
@@ -94,8 +99,8 @@
 
 
 def sweep_kernel(
-    cost_ref, data_ref, noise_ref, out_ref, pots_ref, noise_sq_ref,
-    bias, kern, row_pot, col_pot, row_sum,
+    cost_ref, data_ref, noise_ref, out_ref, row_pot, row_fac, col_pot, col_fac, noise_sq_ref,
+    bias, kern, row_sum,
 ):
     for tile, rows, half in tiles():
         bias[rows, half] = cost_ref[tile] * (-1.0 / (LATENT * BIT))
@@ -158,7 +163,7 @@
         return (low, high, tuple(1.0 / total for total in totals), noise_sq)
 
     def finish(block, factor, parts):
-        col_pot[block, :] += jnp.log2(factor[:, :1])
+        col_fac[block, :] = factor[:, :1]
         for half, part in zip(halves, parts):
             kern[block, half] = part
 
@@ -171,7 +176,7 @@
     noise_sq = jnp.sum(squares(done, units - done, noise_sq), axis=1, keepdims=True)
     noise_sq_ref[...] = jnp.broadcast_to(noise_sq, noise_sq_ref.shape)
     low, high, totals = over_columns(low, high, rows, finish)
-    row_pot[...] += jnp.log2(jnp.concatenate([row[:1] for row in rows], axis=1))
+    row_fac[...] = jnp.concatenate([row[:1] for row in rows], axis=1)
     row_sum[...] = jnp.concatenate([total[:1] for total in totals], axis=1)
     near = jnp.min(jnp.where((low >= 1.0 / DRIFT) & (high <= DRIFT), 1.0, 0.0)) > 0.5
 
@@ -193,14 +198,13 @@
             return carry
 
         lax.fori_loop(0, SWEEPS, again, 0)
+        row_fac[...] = jnp.ones_like(row_fac)
+        col_fac[...] = jnp.ones_like(col_fac)
         scaled = bias[...] + col_pot[...]
         scaled = jnp.exp2(scaled - jnp.max(scaled, axis=0, keepdims=True))
         kern[...] = scaled
         row_sum[...] = jnp.sum(scaled, axis=0, keepdims=True)
         targets()
-
-    pots_ref[0:1, :] = row_pot[...] * BIT
-    pots_ref[1:2, :] = jnp.transpose(col_pot[...] * BIT)
 
 
 def on_device(noise, data):
@@ -242,18 +246,21 @@
     total = pl.pallas_call(sum_kernel, out_shape=whole, compiler_params=params)(exchange(parts))
     total = exchange(total)
 
-    moved, pots, noise_sq = pl.pallas_call(
+    along_lanes = jax.ShapeDtypeStruct((1, BATCH), jnp.float32)
+    along_sublanes = jax.ShapeDtypeStruct((BATCH, 1), jnp.float32)
+    moved, *pots, noise_sq = pl.pallas_call(
         sweep_kernel,
         out_shape=(
             jax.ShapeDtypeStruct((devices, own, ent), jnp.bfloat16),
-            jax.ShapeDtypeStruct((2, BATCH), jnp.float32),
+            along_lanes,
+            along_lanes,
+            along_sublanes,
+            along_sublanes,
             jax.ShapeDtypeStruct((own, LANES), jnp.float32),
         ),
         scratch_shapes=[
             pltpu.VMEM((BATCH, BATCH), jnp.float32),
             pltpu.VMEM((BATCH, BATCH), jnp.float32),
-            pltpu.VMEM((1, BATCH), jnp.float32),
-            pltpu.VMEM((BATCH, 1), jnp.float32),
             pltpu.VMEM((1, BATCH), jnp.float32),
         ],
         compiler_params=params,
@@ -268,7 +275,7 @@
             jax.ShapeDtypeStruct((own,), jnp.float32),
             jax.ShapeDtypeStruct((own,), jnp.float32),
         ),
-        in_specs=[anywhere, in_vmem, in_vmem],
+        in_specs=[anywhere] + [in_vmem] * 5,
         out_specs=(anywhere, anywhere, anywhere),
         scratch_shapes=[
             pltpu.SMEM((own,), jnp.float32),
@@ -276,7 +283,7 @@
             pltpu.SemaphoreType.DMA((UNITS + 2,)),
         ],
         compiler_params=params,
-    )(moved, pots, noise_sq)
+    )(moved, *pots, noise_sq)
     return (targets.transpose(1, 0, 2).reshape(own, LATENT), row, col)
 
 

time: 112 us -> 112 us (level)
  no operation moved by 1% of the time
where the time goes in v19:
time: 112 us
  blocking collectives  104 us (93%)
  Pallas kernels  7.31 us (7%)
    all_to_all x1, blocking collectives, on_device(): both = lax.all_to_all(both, AXES, split_axis=0, concat_axis=0)  47 us
    all_to_all x2, blocking collectives, exchange(): lax.all_to_all(parts, AXES, split_axis=0, concat_axis=0)  30.5 us
    all_to_all x1, blocking collectives, on_device(): moved = lax.all_to_all(moved, AXES, split_axis=0, concat_axis=0)  26.2 us
    pallas_call x1, Pallas kernels, on_device(): pl.pallas_call(sweep_kernel, out_shape=(jax.ShapeDtypeStruct((devices, ow...  3.4 us

profile of v19, /device:TPU:1, one launch (start us, length us, event | category | flops | bytes accessed | tf_op | source)
XLA Modules:
  0.0 111.7 jit_solution(1092961641731352667)
XLA Ops:
  0.6 1.8 %shard_map.49 = bf16[128,8,2,640]{3,2,1,0:T(2,128)(2,1)S(1)} custom-call(bf16[507,2,640]{2,1,0:T(2,128)(2,1)} %bitcast.21, bf16[507,2,640]{2,1,0:T(2,128)(2,1)} %bitcast.26), custom_call_target="tpu_custom_call" | custom-call | tf_op jit(solution)/shard_map/pallas_call | solution.py:221
  2.4 47.0 %all_to_all.20.both_ref = bf16[128,2,5120]{2,1,0:T(2,128)(2,1)S(1)} all-to-all(bf16[128,2,5120]{2,1,0:T(2,128)(2,1)S(1)} %bitcast.19), channel_id=1, replica_groups=mesh['dp'=16,'dim'=8] {'dp','dim'}, dimensions={0} | all-to-all | bytes 5242880 | tf_op jit(solution)/shard_map/all_to_all | solution.py:233
  49.5 0.9 shard_map.50
  50.4 0.0 copy-start
  50.4 15.3 %all_to_all.21 = f32[128,4,128]{2,1,0:T(4,128)S(1)} all-to-all(f32[128,4,128]{2,1,0:T(4,128)S(1)} %bitcast.25), channel_id=1, replica_groups=mesh['dp'=16,'dim'=8] {'dp','dim'}, dimensions={0} | all-to-all | bytes 524288 | tf_op jit(solution)/shard_map/all_to_all | solution.py:239
  65.7 0.1 shard_map.51
  65.8 15.2 %all_to_all.22 = f32[128,4,128]{2,1,0:T(4,128)S(1)} all-to-all(f32[128,4,128]{2,1,0:T(4,128)S(1)} %bitcast.24), channel_id=1, replica_groups=mesh['dp'=16,'dim'=8] {'dp','dim'}, dimensions={0} | all-to-all | bytes 524288 | tf_op jit(solution)/shard_map/all_to_all | solution.py:239
  81.0 0.0 copy-done
  81.0 3.4 %shard_map.52 = (bf16[128,2,2560]{2,1,0:T(2,128)(2,1)S(1)}, f32[1,256]{1,0:T(1,128)S(1)}, f32[1,256]{1,0:T(1,128)S(1)}, f32[256,1]{1,0:T(8,128)S(1)}, f32[256,1]{1,0:T(8,128)S(1)}, /*index=5*/f32[2,128]{1,0:T(2,128)S(1)}) custom-call(f32[64,8,128]{2,1,0:T(8,128)S(1)} %bitcast.22, bf16[256,2560]{1,0:T(8,128)(2,1)S(1)} %get-tuple-element.15.data_ref, ...), custom_call_target="tpu_custom_call" | custom-call | tf_op jit(solution)/shard_map/pallas_call | solution.py:251
  84.4 26.2 %all_to_all.23 = bf16[128,2,2560]{2,1,0:T(2,128)(2,1)S(1)} all-to-all(bf16[128,2,2560]{2,1,0:T(2,128)(2,1)S(1)} %get-tuple-element.16), channel_id=1, replica_groups=mesh['dp'=16,'dim'=8] {'dp','dim'}, dimensions={0} | all-to-all | bytes 2621440 | tf_op jit(solution)/shard_map/all_to_all | solution.py:268
  110.6 1.1 %shard_map.53 = (bf16[507,2,640]{2,1,0:T(2,128)(2,1)}, f32[2]{0:T(128)}, f32[2]{0:T(128)}) custom-call(bf16[128,4,2,640]{3,2,1,0:T(2,128)(2,1)S(1)} %bitcast.20, f32[1,256]{1,0:T(1,128)S(1)} %get-tuple-element.17.row_pot_ref, f32[1,256]{1,0:T(1,128)S(1)} %get-tuple-element.18.row_fac_ref, f32[256,1]{1,0:T(8,128)S(1)} %get-tuple-element.19.col_pot_ref, ...), custom_call_target="tpu_custom_call" | custom-call | tf_op jit(solution)/shard_map/pallas_call | solution.py:271
Async XLA Ops:
  50.4 30.6 %copy-start = (bf16[2,324480]{1,0:T(2,128)(2,1)S(1)}, bf16[2,324480]{1,0:T(2,128)(2,1)}, u32[]{:S(2)}) copy-start(bf16[2,324480]{1,0:T(2,128)(2,1)} %noise_ref.1) | copy-start | bytes 3893764

commit v20 on v19

--- a/solution.py
+++ b/solution.py
@@ -62,7 +62,7 @@
     sublane = lax.broadcasted_iota(jnp.int32, col_pot.shape, 0)
     for n in range(own):
         mine = jnp.sum(jnp.where(lane == first + n, row_pot, 0.0))
-        row[n] = mine + jnp.max(noise_sq_ref[n : n + 1, :]) / LATENT
+        row[n] = mine + jnp.sum(noise_sq_ref[n : n + 1, :]) / LATENT
         col[n] = jnp.sum(jnp.where(sublane == first + n, col_pot, 0.0))
     for copy in copies[UNITS:]:
         copy.start()
@@ -173,8 +173,7 @@
     carry = (low, high, tuple(1.0 / total for total in totals), noise_sq)
     low, high, rows, noise_sq = lax.fori_loop(2, SWEEPS, sweep, carry)
     done = (SWEEPS - 2) * share
-    noise_sq = jnp.sum(squares(done, units - done, noise_sq), axis=1, keepdims=True)
-    noise_sq_ref[...] = jnp.broadcast_to(noise_sq, noise_sq_ref.shape)
+    noise_sq_ref[...] = squares(done, units - done, noise_sq)
     low, high, totals = over_columns(low, high, rows, finish)
     row_fac[...] = jnp.concatenate([row[:1] for row in rows], axis=1)
     row_sum[...] = jnp.concatenate([total[:1] for total in totals], axis=1)
@@ -256,7 +255,7 @@
             along_lanes,
             along_sublanes,
             along_sublanes,
-            jax.ShapeDtypeStruct((own, LANES), jnp.float32),
+            jax.ShapeDtypeStruct((own, UNIT), jnp.float32),
         ),
         scratch_shapes=[
             pltpu.VMEM((BATCH, BATCH), jnp.float32),

time: 112 us -> 112 us (level)
  no operation moved by 1% of the time
where the time goes in v20:
time: 112 us
  blocking collectives  104 us (93%)
  Pallas kernels  7.24 us (6%)
    all_to_all x1, blocking collectives, on_device(): both = lax.all_to_all(both, AXES, split_axis=0, concat_axis=0)  47 us
    all_to_all x2, blocking collectives, exchange(): lax.all_to_all(parts, AXES, split_axis=0, concat_axis=0)  30.5 us
    all_to_all x1, blocking collectives, on_device(): moved = lax.all_to_all(moved, AXES, split_axis=0, concat_axis=0)  26.2 us
    pallas_call x1, Pallas kernels, on_device(): pl.pallas_call(sweep_kernel, out_shape=(jax.ShapeDtypeStruct((devices, ow...  3.39 us

profile of v20, /device:TPU:1, one launch (start us, length us, event | category | flops | bytes accessed | tf_op | source)
XLA Modules:
  0.0 111.7 jit_solution(8041454637523654871)
XLA Ops:
  0.6 1.8 %shard_map.49 = bf16[128,8,2,640]{3,2,1,0:T(2,128)(2,1)S(1)} custom-call(bf16[507,2,640]{2,1,0:T(2,128)(2,1)} %bitcast.21, bf16[507,2,640]{2,1,0:T(2,128)(2,1)} %bitcast.26), custom_call_target="tpu_custom_call" | custom-call | tf_op jit(solution)/shard_map/pallas_call | solution.py:220
  2.4 47.0 %all_to_all.20.both_ref = bf16[128,2,5120]{2,1,0:T(2,128)(2,1)S(1)} all-to-all(bf16[128,2,5120]{2,1,0:T(2,128)(2,1)S(1)} %bitcast.19), channel_id=1, replica_groups=mesh['dp'=16,'dim'=8] {'dp','dim'}, dimensions={0} | all-to-all | bytes 5242880 | tf_op jit(solution)/shard_map/all_to_all | solution.py:232
  49.5 0.8 shard_map.50
  50.3 0.0 copy-start
  50.3 15.3 %all_to_all.21 = f32[128,4,128]{2,1,0:T(4,128)S(1)} all-to-all(f32[128,4,128]{2,1,0:T(4,128)S(1)} %bitcast.25), channel_id=1, replica_groups=mesh['dp'=16,'dim'=8] {'dp','dim'}, dimensions={0} | all-to-all | bytes 524288 | tf_op jit(solution)/shard_map/all_to_all | solution.py:238
  65.6 0.1 shard_map.51
  65.7 15.2 %all_to_all.22 = f32[128,4,128]{2,1,0:T(4,128)S(1)} all-to-all(f32[128,4,128]{2,1,0:T(4,128)S(1)} %bitcast.24), channel_id=1, replica_groups=mesh['dp'=16,'dim'=8] {'dp','dim'}, dimensions={0} | all-to-all | bytes 524288 | tf_op jit(solution)/shard_map/all_to_all | solution.py:238
  80.9 0.0 copy-done
  80.9 3.4 %shard_map.52 = (bf16[128,2,2560]{2,1,0:T(2,128)(2,1)S(1)}, f32[1,256]{1,0:T(1,128)S(1)}, f32[1,256]{1,0:T(1,128)S(1)}, f32[256,1]{1,0:T(8,128)S(1)}, f32[256,1]{1,0:T(8,128)S(1)}, /*index=5*/f32[2,640]{1,0:T(2,128)S(1)}) custom-call(f32[64,8,128]{2,1,0:T(8,128)S(1)} %bitcast.22, bf16[256,2560]{1,0:T(8,128)(2,1)S(1)} %get-tuple-element.15.data_ref, ...), custom_call_target="tpu_custom_call" | custom-call | tf_op jit(solution)/shard_map/pallas_call | solution.py:250
  84.3 26.2 %all_to_all.23 = bf16[128,2,2560]{2,1,0:T(2,128)(2,1)S(1)} all-to-all(bf16[128,2,2560]{2,1,0:T(2,128)(2,1)S(1)} %get-tuple-element.16), channel_id=1, replica_groups=mesh['dp'=16,'dim'=8] {'dp','dim'}, dimensions={0} | all-to-all | bytes 2621440 | tf_op jit(solution)/shard_map/all_to_all | solution.py:267
  110.5 1.1 %shard_map.53 = (bf16[507,2,640]{2,1,0:T(2,128)(2,1)}, f32[2]{0:T(128)}, f32[2]{0:T(128)}) custom-call(bf16[128,4,2,640]{3,2,1,0:T(2,128)(2,1)S(1)} %bitcast.20, f32[1,256]{1,0:T(1,128)S(1)} %get-tuple-element.17.row_pot_ref, f32[1,256]{1,0:T(1,128)S(1)} %get-tuple-element.18.row_fac_ref, f32[256,1]{1,0:T(8,128)S(1)} %get-tuple-element.19.col_pot_ref, ...), custom_call_target="tpu_custom_call" | custom-call | tf_op jit(solution)/shard_map/pallas_call | solution.py:270
Async XLA Ops:
  50.3 30.6 %copy-start = (bf16[2,324480]{1,0:T(2,128)(2,1)S(1)}, bf16[2,324480]{1,0:T(2,128)(2,1)}, u32[]{:S(2)}) copy-start(bf16[2,324480]{1,0:T(2,128)(2,1)} %noise_ref.1) | copy-start | bytes 3893764

commit v21 on v19

--- a/solution.py
+++ b/solution.py
@@ -148,10 +148,11 @@
     share = units // (SWEEPS - 2)
 
     def squares(first, count, total):
-        for n in range(count):
-            start = pl.multiple_of((first + n) * UNIT, LANES)
-            unit = noise_ref[:, pl.ds(start, UNIT)].astype(jnp.float32)
-            total = total + unit * unit
+        width = total.shape[1]
+        for n in range(count * UNIT // width):
+            start = pl.multiple_of(first * UNIT + n * width, LANES)
+            wide = noise_ref[:, pl.ds(start, width)].astype(jnp.float32)
+            total = total + wide * wide
         return total
 
     def sweep(step, carry):
@@ -169,11 +170,12 @@
 
     totals = [jnp.broadcast_to(total[:, half.start : half.start + LANES], tile) for half in halves]
     low, high = jnp.minimum(*totals), jnp.maximum(*totals)
-    noise_sq = jnp.zeros((noise_ref.shape[0], UNIT), jnp.float32)
+    noise_sq = jnp.zeros((noise_ref.shape[0], 4 * UNIT), jnp.float32)
     carry = (low, high, tuple(1.0 / total for total in totals), noise_sq)
     low, high, rows, noise_sq = lax.fori_loop(2, SWEEPS, sweep, carry)
     done = (SWEEPS - 2) * share
-    noise_sq = jnp.sum(squares(done, units - done, noise_sq), axis=1, keepdims=True)
+    rest = squares(done, units - done, jnp.zeros((noise_ref.shape[0], UNIT), jnp.float32))
+    noise_sq = jnp.sum(noise_sq, axis=1, keepdims=True) + jnp.sum(rest, axis=1, keepdims=True)
     noise_sq_ref[...] = jnp.broadcast_to(noise_sq, noise_sq_ref.shape)
     low, high, totals = over_columns(low, high, rows, finish)
     row_fac[...] = jnp.concatenate([row[:1] for row in rows], axis=1)

time: 112 us -> 112 us (level)
  no operation moved by 1% of the time
where the time goes in v21:
time: 112 us
  blocking collectives  104 us (93%)
  Pallas kernels  7.31 us (7%)
    all_to_all x1, blocking collectives, on_device(): both = lax.all_to_all(both, AXES, split_axis=0, concat_axis=0)  47 us
    all_to_all x2, blocking collectives, exchange(): lax.all_to_all(parts, AXES, split_axis=0, concat_axis=0)  30.5 us
    all_to_all x1, blocking collectives, on_device(): moved = lax.all_to_all(moved, AXES, split_axis=0, concat_axis=0)  26.2 us
    pallas_call x1, Pallas kernels, on_device(): pl.pallas_call(sweep_kernel, out_shape=(jax.ShapeDtypeStruct((devices, ow...  3.41 us

profile of v21, /device:TPU:1, one launch (start us, length us, event | category | flops | bytes accessed | tf_op | source)
XLA Modules:
  0.0 111.7 jit_solution(17762212630976816027)
XLA Ops:
  0.6 1.8 %shard_map.49 = bf16[128,8,2,640]{3,2,1,0:T(2,128)(2,1)S(1)} custom-call(bf16[507,2,640]{2,1,0:T(2,128)(2,1)} %bitcast.21, bf16[507,2,640]{2,1,0:T(2,128)(2,1)} %bitcast.26), custom_call_target="tpu_custom_call" | custom-call | tf_op jit(solution)/shard_map/pallas_call | solution.py:223
  2.4 47.0 %all_to_all.20.both_ref = bf16[128,2,5120]{2,1,0:T(2,128)(2,1)S(1)} all-to-all(bf16[128,2,5120]{2,1,0:T(2,128)(2,1)S(1)} %bitcast.19), channel_id=1, replica_groups=mesh['dp'=16,'dim'=8] {'dp','dim'}, dimensions={0} | all-to-all | bytes 5242880 | tf_op jit(solution)/shard_map/all_to_all | solution.py:235
  49.5 0.9 shard_map.50
  50.4 0.0 copy-start
  50.4 15.3 %all_to_all.21 = f32[128,4,128]{2,1,0:T(4,128)S(1)} all-to-all(f32[128,4,128]{2,1,0:T(4,128)S(1)} %bitcast.25), channel_id=1, replica_groups=mesh['dp'=16,'dim'=8] {'dp','dim'}, dimensions={0} | all-to-all | bytes 524288 | tf_op jit(solution)/shard_map/all_to_all | solution.py:241
  65.7 0.1 shard_map.51
  65.8 15.2 %all_to_all.22 = f32[128,4,128]{2,1,0:T(4,128)S(1)} all-to-all(f32[128,4,128]{2,1,0:T(4,128)S(1)} %bitcast.24), channel_id=1, replica_groups=mesh['dp'=16,'dim'=8] {'dp','dim'}, dimensions={0} | all-to-all | bytes 524288 | tf_op jit(solution)/shard_map/all_to_all | solution.py:241
  81.0 0.0 copy-done
  81.0 3.4 %shard_map.52 = (bf16[128,2,2560]{2,1,0:T(2,128)(2,1)S(1)}, f32[1,256]{1,0:T(1,128)S(1)}, f32[1,256]{1,0:T(1,128)S(1)}, f32[256,1]{1,0:T(8,128)S(1)}, f32[256,1]{1,0:T(8,128)S(1)}, /*index=5*/f32[2,128]{1,0:T(2,128)S(1)}) custom-call(f32[64,8,128]{2,1,0:T(8,128)S(1)} %bitcast.22, bf16[256,2560]{1,0:T(8,128)(2,1)S(1)} %get-tuple-element.15.data_ref, ...), custom_call_target="tpu_custom_call" | custom-call | tf_op jit(solution)/shard_map/pallas_call | solution.py:253
  84.4 26.2 %all_to_all.23 = bf16[128,2,2560]{2,1,0:T(2,128)(2,1)S(1)} all-to-all(bf16[128,2,2560]{2,1,0:T(2,128)(2,1)S(1)} %get-tuple-element.16), channel_id=1, replica_groups=mesh['dp'=16,'dim'=8] {'dp','dim'}, dimensions={0} | all-to-all | bytes 2621440 | tf_op jit(solution)/shard_map/all_to_all | solution.py:270
  110.6 1.1 %shard_map.53 = (bf16[507,2,640]{2,1,0:T(2,128)(2,1)}, f32[2]{0:T(128)}, f32[2]{0:T(128)}) custom-call(bf16[128,4,2,640]{3,2,1,0:T(2,128)(2,1)S(1)} %bitcast.20, f32[1,256]{1,0:T(1,128)S(1)} %get-tuple-element.17.row_pot_ref, f32[1,256]{1,0:T(1,128)S(1)} %get-tuple-element.18.row_fac_ref, f32[256,1]{1,0:T(8,128)S(1)} %get-tuple-element.19.col_pot_ref, ...), custom_call_target="tpu_custom_call" | custom-call | tf_op jit(solution)/shard_map/pallas_call | solution.py:273
Async XLA Ops:
  50.4 30.6 %copy-start = (bf16[2,324480]{1,0:T(2,128)(2,1)S(1)}, bf16[2,324480]{1,0:T(2,128)(2,1)}, u32[]{:S(2)}) copy-start(bf16[2,324480]{1,0:T(2,128)(2,1)} %noise_ref.1) | copy-start | bytes 3893764

commit v22 on v19

--- a/solution.py
+++ b/solution.py
@@ -243,6 +243,7 @@
         out_shape=(whole, jax.ShapeDtypeStruct((BATCH, ent), data.dtype)),
         compiler_params=params,
     )(both)
+    noise, parts = lax.optimization_barrier((noise, parts))
     total = pl.pallas_call(sum_kernel, out_shape=whole, compiler_params=params)(exchange(parts))
     total = exchange(total)
 

time: 112 us -> 112 us (level)
  no operation moved by 1% of the time
where the time goes in v22:
time: 112 us
  blocking collectives  104 us (93%)
  Pallas kernels  7.31 us (7%)
    all_to_all x1, blocking collectives, on_device(): both = lax.all_to_all(both, AXES, split_axis=0, concat_axis=0)  47 us
    all_to_all x2, blocking collectives, exchange(): lax.all_to_all(parts, AXES, split_axis=0, concat_axis=0)  30.5 us
    all_to_all x1, blocking collectives, on_device(): moved = lax.all_to_all(moved, AXES, split_axis=0, concat_axis=0)  26.2 us
    pallas_call x1, Pallas kernels, on_device(): pl.pallas_call(sweep_kernel, out_shape=(jax.ShapeDtypeStruct((devices, ow...  3.4 us

profile of v22, /device:TPU:1, one launch (start us, length us, event | category | flops | bytes accessed | tf_op | source)
XLA Modules:
  0.0 111.7 jit_solution(1092961641731352667)
XLA Ops:
  0.6 1.8 %shard_map.49 = bf16[128,8,2,640]{3,2,1,0:T(2,128)(2,1)S(1)} custom-call(bf16[507,2,640]{2,1,0:T(2,128)(2,1)} %bitcast.21, bf16[507,2,640]{2,1,0:T(2,128)(2,1)} %bitcast.26), custom_call_target="tpu_custom_call" | custom-call | tf_op jit(solution)/shard_map/pallas_call | solution.py:221
  2.4 47.0 %all_to_all.20.both_ref = bf16[128,2,5120]{2,1,0:T(2,128)(2,1)S(1)} all-to-all(bf16[128,2,5120]{2,1,0:T(2,128)(2,1)S(1)} %bitcast.19), channel_id=1, replica_groups=mesh['dp'=16,'dim'=8] {'dp','dim'}, dimensions={0} | all-to-all | bytes 5242880 | tf_op jit(solution)/shard_map/all_to_all | solution.py:233
  49.5 0.9 shard_map.50
  50.4 0.0 copy-start
  50.4 15.3 %all_to_all.21 = f32[128,4,128]{2,1,0:T(4,128)S(1)} all-to-all(f32[128,4,128]{2,1,0:T(4,128)S(1)} %bitcast.25), channel_id=1, replica_groups=mesh['dp'=16,'dim'=8] {'dp','dim'}, dimensions={0} | all-to-all | bytes 524288 | tf_op jit(solution)/shard_map/all_to_all | solution.py:239
  65.7 0.1 shard_map.51
  65.8 15.2 %all_to_all.22 = f32[128,4,128]{2,1,0:T(4,128)S(1)} all-to-all(f32[128,4,128]{2,1,0:T(4,128)S(1)} %bitcast.24), channel_id=1, replica_groups=mesh['dp'=16,'dim'=8] {'dp','dim'}, dimensions={0} | all-to-all | bytes 524288 | tf_op jit(solution)/shard_map/all_to_all | solution.py:239
  81.0 0.0 copy-done
  81.0 3.4 %shard_map.52 = (bf16[128,2,2560]{2,1,0:T(2,128)(2,1)S(1)}, f32[1,256]{1,0:T(1,128)S(1)}, f32[1,256]{1,0:T(1,128)S(1)}, f32[256,1]{1,0:T(8,128)S(1)}, f32[256,1]{1,0:T(8,128)S(1)}, /*index=5*/f32[2,128]{1,0:T(2,128)S(1)}) custom-call(f32[64,8,128]{2,1,0:T(8,128)S(1)} %bitcast.22, bf16[256,2560]{1,0:T(8,128)(2,1)S(1)} %get-tuple-element.18.data_ref, ...), custom_call_target="tpu_custom_call" | custom-call | tf_op jit(solution)/shard_map/pallas_call | solution.py:252
  84.4 26.2 %all_to_all.23 = bf16[128,2,2560]{2,1,0:T(2,128)(2,1)S(1)} all-to-all(bf16[128,2,2560]{2,1,0:T(2,128)(2,1)S(1)} %get-tuple-element.20), channel_id=1, replica_groups=mesh['dp'=16,'dim'=8] {'dp','dim'}, dimensions={0} | all-to-all | bytes 2621440 | tf_op jit(solution)/shard_map/all_to_all | solution.py:269
  110.6 1.1 %shard_map.53 = (bf16[507,2,640]{2,1,0:T(2,128)(2,1)}, f32[2]{0:T(128)}, f32[2]{0:T(128)}) custom-call(bf16[128,4,2,640]{3,2,1,0:T(2,128)(2,1)S(1)} %bitcast.20, f32[1,256]{1,0:T(1,128)S(1)} %get-tuple-element.21.row_pot_ref, f32[1,256]{1,0:T(1,128)S(1)} %get-tuple-element.22.row_fac_ref, f32[256,1]{1,0:T(8,128)S(1)} %get-tuple-element.23.col_pot_ref, ...), custom_call_target="tpu_custom_call" | custom-call | tf_op jit(solution)/shard_map/pallas_call | solution.py:272
Async XLA Ops:
  50.4 30.6 %copy-start = (bf16[2,324480]{1,0:T(2,128)(2,1)S(1)}, bf16[2,324480]{1,0:T(2,128)(2,1)}, u32[]{:S(2)}) copy-start(bf16[2,324480]{1,0:T(2,128)(2,1)} %noise_ref) | copy-start | bytes 3893764

commit v23 on v19

--- a/solution.py
+++ b/solution.py
@@ -61,11 +61,12 @@
     lane = lax.broadcasted_iota(jnp.int32, row_pot.shape, 1)
     sublane = lax.broadcasted_iota(jnp.int32, col_pot.shape, 0)
     for n in range(own):
+        col[n] = jnp.sum(jnp.where(sublane == first + n, col_pot, 0.0))
+    copies[UNITS + 1].start()
+    for n in range(own):
         mine = jnp.sum(jnp.where(lane == first + n, row_pot, 0.0))
         row[n] = mine + jnp.max(noise_sq_ref[n : n + 1, :]) / LATENT
-        col[n] = jnp.sum(jnp.where(sublane == first + n, col_pot, 0.0))
-    for copy in copies[UNITS:]:
-        copy.start()
+    copies[UNITS].start()
     for copy in copies:
         copy.wait()
 

time: 112 us -> 112 us (level)
  no operation moved by 1% of the time
where the time goes in v23:
time: 112 us
  blocking collectives  104 us (93%)
  Pallas kernels  7.3 us (7%)
    all_to_all x1, blocking collectives, on_device(): both = lax.all_to_all(both, AXES, split_axis=0, concat_axis=0)  47 us
    all_to_all x2, blocking collectives, exchange(): lax.all_to_all(parts, AXES, split_axis=0, concat_axis=0)  30.5 us
    all_to_all x1, blocking collectives, on_device(): moved = lax.all_to_all(moved, AXES, split_axis=0, concat_axis=0)  26.2 us
    pallas_call x1, Pallas kernels, on_device(): pl.pallas_call(sweep_kernel, out_shape=(jax.ShapeDtypeStruct((devices, ow...  3.4 us

profile of v23, /device:TPU:1, one launch (start us, length us, event | category | flops | bytes accessed | tf_op | source)
XLA Modules:
  0.0 111.7 jit_solution(3549126633641435985)
XLA Ops:
  0.6 1.8 %shard_map.49 = bf16[128,8,2,640]{3,2,1,0:T(2,128)(2,1)S(1)} custom-call(bf16[507,2,640]{2,1,0:T(2,128)(2,1)} %bitcast.21, bf16[507,2,640]{2,1,0:T(2,128)(2,1)} %bitcast.26), custom_call_target="tpu_custom_call" | custom-call | tf_op jit(solution)/shard_map/pallas_call | solution.py:222
  2.4 47.0 %all_to_all.20.both_ref = bf16[128,2,5120]{2,1,0:T(2,128)(2,1)S(1)} all-to-all(bf16[128,2,5120]{2,1,0:T(2,128)(2,1)S(1)} %bitcast.19), channel_id=1, replica_groups=mesh['dp'=16,'dim'=8] {'dp','dim'}, dimensions={0} | all-to-all | bytes 5242880 | tf_op jit(solution)/shard_map/all_to_all | solution.py:234
  49.5 0.9 shard_map.50
  50.4 0.0 copy-start
  50.4 15.3 %all_to_all.21 = f32[128,4,128]{2,1,0:T(4,128)S(1)} all-to-all(f32[128,4,128]{2,1,0:T(4,128)S(1)} %bitcast.25), channel_id=1, replica_groups=mesh['dp'=16,'dim'=8] {'dp','dim'}, dimensions={0} | all-to-all | bytes 524288 | tf_op jit(solution)/shard_map/all_to_all | solution.py:240
  65.7 0.1 shard_map.51
  65.8 15.2 %all_to_all.22 = f32[128,4,128]{2,1,0:T(4,128)S(1)} all-to-all(f32[128,4,128]{2,1,0:T(4,128)S(1)} %bitcast.24), channel_id=1, replica_groups=mesh['dp'=16,'dim'=8] {'dp','dim'}, dimensions={0} | all-to-all | bytes 524288 | tf_op jit(solution)/shard_map/all_to_all | solution.py:240
  81.0 0.0 copy-done
  81.0 3.4 %shard_map.52 = (bf16[128,2,2560]{2,1,0:T(2,128)(2,1)S(1)}, f32[1,256]{1,0:T(1,128)S(1)}, f32[1,256]{1,0:T(1,128)S(1)}, f32[256,1]{1,0:T(8,128)S(1)}, f32[256,1]{1,0:T(8,128)S(1)}, /*index=5*/f32[2,128]{1,0:T(2,128)S(1)}) custom-call(f32[64,8,128]{2,1,0:T(8,128)S(1)} %bitcast.22, bf16[256,2560]{1,0:T(8,128)(2,1)S(1)} %get-tuple-element.15.data_ref, ...), custom_call_target="tpu_custom_call" | custom-call | tf_op jit(solution)/shard_map/pallas_call | solution.py:252
  84.4 26.2 %all_to_all.23 = bf16[128,2,2560]{2,1,0:T(2,128)(2,1)S(1)} all-to-all(bf16[128,2,2560]{2,1,0:T(2,128)(2,1)S(1)} %get-tuple-element.16), channel_id=1, replica_groups=mesh['dp'=16,'dim'=8] {'dp','dim'}, dimensions={0} | all-to-all | bytes 2621440 | tf_op jit(solution)/shard_map/all_to_all | solution.py:269
  110.6 1.1 %shard_map.53 = (bf16[507,2,640]{2,1,0:T(2,128)(2,1)}, f32[2]{0:T(128)}, f32[2]{0:T(128)}) custom-call(bf16[128,4,2,640]{3,2,1,0:T(2,128)(2,1)S(1)} %bitcast.20, f32[1,256]{1,0:T(1,128)S(1)} %get-tuple-element.17.row_pot_ref, f32[1,256]{1,0:T(1,128)S(1)} %get-tuple-element.18.row_fac_ref, f32[256,1]{1,0:T(8,128)S(1)} %get-tuple-element.19.col_pot_ref, ...), custom_call_target="tpu_custom_call" | custom-call | tf_op jit(solution)/shard_map/pallas_call | solution.py:272
Async XLA Ops:
  50.4 30.6 %copy-start = (bf16[2,324480]{1,0:T(2,128)(2,1)S(1)}, bf16[2,324480]{1,0:T(2,128)(2,1)}, u32[]{:S(2)}) copy-start(bf16[2,324480]{1,0:T(2,128)(2,1)} %noise_ref.1) | copy-start | bytes 3893764
